TPU v7x, 32 devices: a whole 2x2x4 slice. The times are simulated.
32 devices in a mesh: frame: 8 (over z, y), coord: 4 (over x, core).
Axes of the slice: x: 2, y: 2, z: 4, core: 2. Of those that a mesh axis runs over, the one named last changes fastest.
Arguments:
- frames: bfloat16 [8192, 4224], P('frame'), may hold values from -0.5 to 1.5
- b_values: bfloat16 [4096, 512], P('coord'), may hold values from -0.25 to 0.25
- b_cols: int32 [64, 8], P('coord'), may hold values from 0 to 65, as said below
- frame_window: int32 [8192], P('frame'), may hold values from 0 to 1, as said below
Outputs:
- count: float32 [], replicated
- mean: float32 [4096], P('coord')
- covariance: float32 [4096, 4096], P('frame', 'coord')
Inputs may be any that keep to these rules, and one draw needn't show every extreme that they name: `b_cols`: each row holds 8 different column-block indices. `frame_window`: the first and the last frame are always in the window.
All inputs are finite; a program needn't handle non-finite values.
Results may differ from a plain program's by a relative error of at most 0.0022.
Values may be sent and summed in bfloat16 or wider, within the bound.
No kernel may reach another device: no remote copies, remote signals or barrier semaphores. Data moves between devices by JAX's collectives and lax.ppermute only.
A program may use at most 128 MiB of HBM per device.

v0:
```python
import jax
import jax.numpy as jnp
from jax import lax
from jax.sharding import PartitionSpec as P

BLOCK = 64


def project(frames, values, col_blocks):
    frame_rows = frames.shape[0]
    blocks = frames.reshape(frame_rows, -1, BLOCK)
    picked = jnp.take(blocks, col_blocks, axis=1)
    panel = values.reshape(col_blocks.shape[0], BLOCK, col_blocks.shape[1], BLOCK)
    product = jnp.einsum("frkc,rjkc->frj", picked, panel, preferred_element_type=jnp.float32)
    return product.reshape(frame_rows, -1).astype(jnp.bfloat16)


def on_device(frames, b_values, b_cols, frame_window):
    weight = frame_window.astype(jnp.float32)
    weight_half = frame_window.astype(jnp.bfloat16)
    coords_mine = project(frames, b_values, b_cols)
    local_count = jnp.sum(weight)
    local_sums = jnp.dot(weight_half, coords_mine, preferred_element_type=jnp.float32)
    count, col_sums = lax.psum((local_count, local_sums), "frame")
    mean_mine = col_sums / count
    centered_mine = (weight[:, None] * (coords_mine.astype(jnp.float32) - mean_mine)).astype(
        jnp.bfloat16
    )
    centered_full = lax.all_gather(centered_mine, "coord", axis=1, tiled=True)
    gram_share = lax.psum_scatter(
        lax.dot_general(
            centered_full,
            centered_mine,
            (((0,), (0,)), ((), ())),
            preferred_element_type=jnp.float32,
        ),
        "frame",
        scatter_dimension=0,
        tiled=True,
    )
    covariance = gram_share / (count - 1.0)
    return (count, mean_mine, covariance)


def solution(mesh):
    return jax.shard_map(
        on_device,
        mesh=mesh,
        in_specs=(P("frame", None), P("coord", None), P("coord", None), P("frame")),
        out_specs=(P(), P("coord"), P("frame", "coord")),
        check_vma=False,
    )
```

profile of v0, /device:TPU:2, one launch (start us, length us, event | category | flops | bytes accessed | tf_op | source)
XLA Modules:
  0.0 438.0 jit_solution(5088696287089750922)
XLA Ops:
  7.2 0.0 all-gather.2.cloned.1.call-start
  7.2 0.7 compare_select_fusion
  7.9 0.7 compare_and_fusion
  8.6 0.8 fusion.9
  9.4 1.3 convert_reduce_fusion
  10.7 12.4 %copy.12 = bf16[1024,4224]{0,1:T(8,128)(2,1)} copy(bf16[1024,4224]{1,0:T(8,128)(2,1)} %param.4) | data formatting | bytes 17301504 | tf_op args[0]
  23.1 0.1 copy.13
  23.1 0.1 reshape.25
  23.3 2.1 reshape.22
  25.3 0.1 copy.11
  25.4 11.8 %gather_fusion = bf16[128,1024,64]{1,2,0:T(8,128)(2,1)} fusion(bf16[1024,66,64]{0,2,1:T(8,128)(2,1)} %bitcast.19, s32[1024]{0:T(1024)S(1)} %pad_clamp_fusion), kind=kCustom, calls=%fused_computation | custom fusion | bytes 33554944 | tf_op jit(solution)/shard_map/jit(_take)/gather | solution.py:12
  37.2 10.3 %bitcast_convert_fusion = bf16[16,1024,64]{1,2,0:T(8,128)(2,1)S(1)} fusion(bf16[16,8,1024,64]{2,3,1,0:T(8,128)(2,1)} %bitcast.20, pred[16,8]{1,0:T(8,128)(4,1)S(1)} %copy.11, bf16[16,64,8,64]{3,2,1,0:T(8,128)(2,1)} %reshape.22), kind=kOutput, calls=%fused_computation.6 | convolution fusion | flops 1083179008 | bytes 19923072 | tf_op jit(solution)/shard_map/frkc,rjkc->frj/dot_general | solution.py:14
  47.5 0.6 fusion.10
  48.1 22.5 %all-reduce = (f32[]{:T(128)}, f32[1024]{0:T(1024)S(1)}) all-reduce(f32[]{:T(128)} %convert_reduce_fusion, f32[1024]{0:T(1024)S(1)} %bitcast.22), channel_id=1, replica_groups=mesh['frame'=8,'coord'=4] {'frame'}, use_global_device_ids=true, to_apply=%region_1.2 | all-reduce | flops 1025 | bytes 8200 | tf_op jit(solution)/shard_map/psum | solution.py:24
  70.7 0.6 broadcast_divide_fusion.1
  71.3 0.0 copy-start.1
  71.3 1.9 multiply_convert_fusion
  73.2 0.0 all-gather.2.cloned.1.call-update
  73.2 0.0 reduce-scatter.2.cloned.1.call-start
  73.3 54.5 %all-gather.2.cloned.1.call-done = bf16[1024,4096]{0,1:T(8,128)(2,1)} async-done(((bf16[1024,1024]{0,1:T(8,128)(2,1)}), bf16[1024,4096]{0,1:T(8,128)(2,1)}) %all-gather.2.cloned.1.call-update) | async-done | bytes 8388624 | tf_op jit(solution)/shard_map/all_gather | solution.py:29
  127.8 16.2 %fusion.11 = f32[4096,1024]{1,0:T(8,128)} fusion(bf16[1024,4096]{0,1:T(8,128)(2,1)} %all-gather.2.cloned.1.call-done, bf16[1024,1024]{0,1:T(8,128)(2,1)} %multiply_convert_fusion), kind=kOutput, calls=%fused_computation.18 | convolution fusion | flops 8589934592 | bytes 27262976 | tf_op jit(solution)/shard_map/dot_general | solution.py:31
  143.9 0.0 reduce-scatter.2.cloned.1.call-update
  144.6 283.3 %reduce-scatter.2.cloned.1.call-done = f32[512,1024]{1,0:T(8,128)} async-done(((f32[4096,1024]{1,0:T(8,128)}), f32[512,1024]{1,0:T(8,128)}) %reduce-scatter.2.cloned.1.call-update) | async-done | bytes 2097168 | tf_op jit(solution)/shard_map/reduce_scatter | solution.py:30
  427.9 3.2 broadcast_divide_fusion
  (5 shorter events, 0.0 us)
Async XLA Ops:
  7.2 120.6 %all-gather.2.cloned.1.call-start = ((), (), s32[]{:S(2)}) async-start(), calls=%async_computation.1 | async-start | bytes 10485760 | tf_op jit(solution)/shard_map/all_gather | solution.py:29
  10.7 12.6 %copy-start = (bf16[1024,512]{1,0:T(8,128)(2,1)S(1)}, bf16[1024,512]{1,0:T(8,128)(2,1)}, u32[]{:S(2)}) copy-start(bf16[1024,512]{1,0:T(8,128)(2,1)} %param.5) | copy-start | bytes 3145732
  71.3 72.6 %copy-start.1 = (f32[1024]{0:T(1024)}, f32[1024]{0:T(1024)S(1)}, u32[]{:S(2)}) copy-start(f32[1024]{0:T(1024)S(1)} %broadcast_divide_fusion.1) | copy-start | bytes 12292
  73.2 354.7 %reduce-scatter.2.cloned.1.call-start = ((), (), s32[]{:S(2)}) async-start(), calls=%async_computation.2 | async-start | bytes 18874368 | tf_op jit(solution)/shard_map/reduce_scatter | solution.py:30
Sparse Core Ops, SparseCore 0:
  73.4 54.3 all-gather.1
  144.1 283.8 reduce-scatter.1
where the time goes:
time: 440 us; the launch traced here: 438 us
  waiting for transfers between devices  338 us (77%)
  matrix products  27.1 us (6%)
  local copies, waits for them, and re-layouts  26.5 us (6%)
  blocking collectives  22.5 us (5%)
  between operations  14.7 us (3%)
  other arithmetic  9.16 us (2%)
    reduce_scatter x1, waiting for transfers between devices, on_device(): lax.psum_scatter(lax.dot_general(centered_full, centered_mine, (((0,), (0...  283 us
    all_gather x1, waiting for transfers between devices, on_device(): centered_full = lax.all_gather(centered_mine, 'coord', axis=1, tiled=True)  54.5 us
    psum x1, blocking collectives, on_device(): count, col_sums = lax.psum((local_count, local_sums), 'frame')  22.5 us
    dot_general x1, matrix products, on_device(): lax.dot_general(centered_full, centered_mine, (((0,), (0,)), ((), ())), p...  16.2 us
    unnamed x5, local copies, waits for them, and re-layouts  12.4 us
    gather x1, local copies, waits for them, and re-layouts, project(): picked = jnp.take(blocks, col_blocks, axis=1)  11.8 us
    dot_general x1, matrix products, project(): jnp.einsum('frkc,rjkc->frj', picked, panel, preferred_element_type=jnp.fl...  10.3 us
  transfers between devices with their start and end apart: 2, of which 2 were waited for; matrix products, arithmetic and copies ran while one was open for 0% of the time, Pallas kernels for 0%

commit v1 on v0

v1 whole, which is shorter than its diff:
```python
import jax
import jax.numpy as jnp
from jax import lax
from jax.experimental import pallas as pl
from jax.experimental.pallas import tpu as pltpu
from jax.sharding import PartitionSpec as P

BLOCK = 64
CHUNKS = 4
F32, F16, BF16 = jnp.float32, jnp.float16, jnp.bfloat16


def project_kernel(cols_ref, frames_ref, values_ref, weight_ref, out_ref, sums_ref, dense_ref):
    row_blocks, nonzero = cols_ref.shape

    @pl.when(pl.program_id(0) == 0)
    def _():
        dense_ref[...] = jnp.zeros_like(dense_ref)
        sums_ref[...] = jnp.zeros_like(sums_ref)
        for r in range(row_blocks):
            block = values_ref[r * BLOCK : (r + 1) * BLOCK, :].astype(F32).T.astype(BF16)
            for k in range(nonzero):
                start = pl.multiple_of(cols_ref[r, k] * BLOCK, BLOCK)
                dense_ref[pl.ds(start, BLOCK), r * BLOCK : (r + 1) * BLOCK] = block[
                    k * BLOCK : (k + 1) * BLOCK, :
                ]

    product = jnp.dot(frames_ref[...], dense_ref[...], preferred_element_type=F32)
    coords = product.astype(BF16).astype(F32)
    out_ref[...] = coords.T.astype(BF16)
    weighted = coords * weight_ref[...]
    sums_ref[0:1, :] += jnp.sum(weighted, axis=0, keepdims=True)
    sums_ref[1:2, :] += jnp.sum(weighted * coords, axis=0, keepdims=True)


def project(frames, values, cols, weight):
    rows, cart = frames.shape
    width = values.shape[0]
    tile = min(256, rows)
    return pl.pallas_call(
        project_kernel,
        grid=(rows // tile,),
        in_specs=[
            pl.BlockSpec(memory_space=pltpu.SMEM),
            pl.BlockSpec((tile, cart), lambda i: (i, 0)),
            pl.BlockSpec(values.shape, lambda i: (0, 0)),
            pl.BlockSpec((tile, 1), lambda i: (i, 0)),
        ],
        out_specs=[
            pl.BlockSpec((width, tile), lambda i: (0, i)),
            pl.BlockSpec((8, width), lambda i: (0, 0)),
        ],
        out_shape=[
            jax.ShapeDtypeStruct((width, rows), BF16),
            jax.ShapeDtypeStruct((8, width), F32),
        ],
        scratch_shapes=[pltpu.VMEM((cart, width), BF16)],
        compiler_params=pltpu.CompilerParams(vmem_limit_bytes=48 * 2**20),
        cost_estimate=pl.CostEstimate(
            flops=2 * rows * cart * width, bytes_accessed=2 * rows * (cart + width), transcendentals=0
        ),
        name="project",
    )(cols, frames, values, weight[:, None])


def solution(mesh):
    n_f, n_c = mesh.shape["frame"], mesh.shape["coord"]
    m = n_f // n_c
    low = m.bit_length() - 1
    high = n_c.bit_length() - 1

    def swap(x, axis, bit):
        size = mesh.shape[axis]
        return lax.ppermute(x, axis, [(i, i ^ bit) for i in range(size)])

    def on_device(frames, b_values, b_cols, frame_window):
        f, c = lax.axis_index("frame"), lax.axis_index("coord")
        weight = frame_window.astype(F32)
        coords, sums = project(frames, b_values, b_cols, weight)
        width, depth = coords.shape
        rows = width // m // CHUNKS
        stats = jnp.concatenate([sums[:2], jnp.full((1, width), jnp.sum(weight))])
        for j in range(n_f.bit_length() - 1):
            stats = stats + swap(stats, "frame", 1 << j)
        count = stats[2, 0]
        mean = stats[0] / count
        spread = jnp.maximum(stats[1] - stats[0] * mean, 1e-5 * stats[1])
        scale = lax.rsqrt(jnp.maximum(jnp.max(spread), 1e-30)) * 173.0
        mine = (weight[None, :] * (coords.astype(F32) - mean[:, None])).astype(BF16)

        own = mine.reshape(m, CHUNKS, rows, depth)
        panels = [[own[:, k] for k in range(CHUNKS)]]
        scales = [scale]
        for d in range(1, n_c):
            if d % 2:
                panels.append([swap(p, "coord", 1) for p in panels[d - 1]])
                scales.append(swap(scales[d - 1], "coord", 1))
            else:
                panels.append([swap(p, "coord", d) for p in panels[0]])
                scales.append(swap(scale, "coord", d))

        flip = (f // m) ^ c

        def gram(items, factors):
            left = jnp.concatenate(items)
            g = lax.dot_general(left, mine, (((1,), (1,)), ((), ())), preferred_element_type=F32)
            g = g.reshape(len(items), rows, width)
            return g * jnp.stack(factors)[:, None, None]

        def task(k, pair, order):
            def part(index):
                e = 0
                delta = 0
                for pos, what in enumerate(order):
                    bit = (index >> (len(order) - 1 - pos)) & 1
                    if what == "d":
                        delta = bit
                    else:
                        e |= bit << what
                a = e ^ (f % m)
                pick = ((flip & 1) ^ delta) == 1
                row = [lax.dynamic_index_in_dim(panels[2 * pair + i][k], a, 0, keepdims=False) for i in (0, 1)]
                factor = jnp.where(pick, scales[2 * pair + 1], scales[2 * pair]) * scale
                return jnp.where(pick, row[1], row[0]), factor

            n = 1 << len(order)
            parts = [part(i) for i in range(n)]
            send = gram(*zip(*parts[n // 2 :])).astype(F16)
            keep = gram(*zip(*parts[: n // 2]))
            for pos, what in enumerate(order):
                if pos:
                    half = keep.shape[0] // 2
                    send, keep = keep[half:].astype(F16), keep[:half]
                keep = keep + swap(send, "frame", m if what == "d" else 1 << what).astype(F32)
            return keep[0]

        first = ["d"] + list(range(low))
        second = list(range(low)) + ["d"]
        done = []
        for k in range(CHUNKS):
            order = first if k == 0 else second
            held = [task(k, pair, order) for pair in range(n_c // 2)]
            for j in range(1, high):
                pick = ((flip >> j) & 1) == 1
                lo = [held[i] for i in range(len(held)) if i % 2 == 0]
                hi = [held[i] for i in range(len(held)) if i % 2 == 1]
                held = [
                    jnp.where(pick, h, l)
                    + swap(jnp.where(pick, l, h).astype(F16), "frame", m << j).astype(F32)
                    for l, h in zip(lo, hi)
                ]
            done.append(held[0])
        row_scale = jnp.stack(scales)[flip]
        covariance = jnp.concatenate(done) * (1.0 / (row_scale * scale * (count - 1.0)))
        return count, mean, covariance

    return jax.shard_map(
        on_device,
        mesh=mesh,
        in_specs=(P("frame", None), P("coord", None), P("coord", None), P("frame")),
        out_specs=(P(), P("coord"), P("frame", "coord")),
        check_vma=False,
    )
```

time: 440 us -> 217 us (0.49)
  waiting for transfers between devices: 338 us -> 111 us
  starting transfers between devices: 0.08 us -> 43.2 us
  blocking collectives: 22.5 us -> 0 us
  local copies, waits for them, and re-layouts: 26.5 us -> 6.06 us
  Pallas kernels: 0 us -> 14.6 us
  matrix products: 27.1 us -> 12.7 us
  other arithmetic: 9.16 us -> 20.3 us
  between operations: 14.7 us -> 7.16 us
    reduce_scatter x1 -> x0, waiting for transfers between devices: 283 us -> none  [on_device(): lax.psum_scatter(lax.dot_general(centered_full, centered_mine, (((0,), (0...]
    ppermute x0 -> x38, waiting for transfers between devices: none -> 111 us  [swap(): return lax.ppermute(x, axis, [(i, i ^ bit) for i in range(size)])]
    all_gather x1 -> x0, waiting for transfers between devices: 54.5 us -> none  [on_device(): centered_full = lax.all_gather(centered_mine, 'coord', axis=1, tiled=True)]
    ppermute x0 -> x38, starting transfers between devices: none -> 43.2 us  [swap(): return lax.ppermute(x, axis, [(i, i ^ bit) for i in range(size)])]
    psum x1 -> x0, blocking collectives: 22.5 us -> none  [on_device(): count, col_sums = lax.psum((local_count, local_sums), 'frame')]
    pallas_call x0 -> x1, Pallas kernels: none -> 14.6 us  [project(): pl.pallas_call(project_kernel, grid=(rows // tile,), in_specs=[pl.BlockSp...]
    dot_general x3 -> x16, matrix products: 27.1 us -> 12.7 us  [gram(): lax.dot_general(left, mine, (((1,), (1,)), ((), ())), preferred_element_t...]
    gather x1 -> x0, local copies, waits for them, and re-layouts: 11.8 us -> none  [project(): picked = jnp.take(blocks, col_blocks, axis=1)]
  transfers between devices with their start and end apart: 2 -> 38, of which waited for: 2 -> 21; matrix products, arithmetic and copies ran while one was open for 0% -> 12% of each run, Pallas kernels for 0% -> 0%
where the time goes in v1:
time: 217 us; the launch traced here: 215 us
  waiting for transfers between devices  111 us (51%)
  starting transfers between devices  43.2 us (20%)
  other arithmetic  20.3 us (9%)
  Pallas kernels  14.6 us (7%)
  matrix products  12.7 us (6%)
  between operations  7.16 us (3%)
  local copies, waits for them, and re-layouts  6.06 us (3%)
    ppermute x38, waiting for transfers between devices, swap(): return lax.ppermute(x, axis, [(i, i ^ bit) for i in range(size)])  111 us
    ppermute x38, starting transfers between devices, swap(): return lax.ppermute(x, axis, [(i, i ^ bit) for i in range(size)])  43.2 us
    pallas_call x1, Pallas kernels, project(): pl.pallas_call(project_kernel, grid=(rows // tile,), in_specs=[pl.BlockSp...  14.6 us
    dot_general x16, matrix products, gram(): lax.dot_general(left, mine, (((1,), (1,)), ((), ())), preferred_element_t...  12.7 us
    select_n x8, other arithmetic, part(): return (jnp.where(pick, row[1], row[0]), factor)  5.9 us
    unnamed x16, local copies, waits for them, and re-layouts  4.71 us
  transfers between devices with their start and end apart: 38, of which 21 were waited for; matrix products, arithmetic and copies ran while one was open for 12% of the time, Pallas kernels for 0%

profile of v1, /device:TPU:2, one launch (start us, length us, event | category | flops | bytes accessed | tf_op | source)
XLA Modules:
  0.0 215.2 jit_solution(6790940135715607731)
XLA Ops:
  4.8 14.6 %project.1 = (bf16[1024,1024]{1,0:T(8,128)(2,1)S(1)}, f32[8,1024]{1,0:T(8,128)S(1)}) custom-call(s32[16,8]{1,0:T(8,128)S(1)} %copy.11.cols_ref, bf16[1024,4224]{1,0:T(8,128)(2,1)} %frames_ref.1, bf16[1024,512]{1,0:T(8,128)(2,1)S(1)} %copy-done, f32[1024,1]{1,0:T(8,128)S(1)} %copy.12.weight_ref), custom_call_target="tpu_custom_call" | custom-call | flops 8858370048 | bytes 10747904 | tf_op jit(solution)/shard_map/project/pallas_call | solution.py:40
  21.7 2.2 %collective-permute-done = f32[3,1024]{1,0:T(4,128)S(1)} collective-permute-done((f32[3,1024]{1,0:T(4,128)S(1)}, f32[3,1024]{1,0:T(4,128)S(1)}, u32[]{:S(2)}, u32[]{:S(2)}) %collective-permute-start) | collective-permute-done | bytes 12320 | tf_op jit(solution)/shard_map/ppermute | solution.py:74
  26.2 2.2 %collective-permute-done.1 = f32[3,1024]{1,0:T(4,128)S(1)} collective-permute-done((f32[3,1024]{1,0:T(4,128)S(1)}, f32[3,1024]{1,0:T(4,128)S(1)}, u32[]{:S(2)}, u32[]{:S(2)}) %collective-permute-start.1) | collective-permute-done | bytes 12320 | tf_op jit(solution)/shard_map/ppermute | solution.py:74
  28.4 2.6 %collective-permute-start.2 = (f32[3,1024]{1,0:T(4,128)S(1)}, f32[3,1024]{1,0:T(4,128)S(1)}, u32[]{:S(2)}, u32[]{:S(2)}) collective-permute-start(f32[3,1024]{1,0:T(4,128)S(1)} %add.179), channel_id=1, source_target_pairs={{0,16},{4,20},{8,24},{12,28},{16,0},{20,4},{24,8},{28,12},{1,17},{... | collective-permute-start | bytes 36872 | tf_op jit(solution)/shard_map/ppermute | solution.py:74
  31.0 2.0 collective-permute-done.2
  39.7 10.5 %collective-permute-start.5 = (f32[]{:T(128)}, f32[]{:T(128)}, u32[]{:S(2)}, u32[]{:S(2)}) collective-permute-start(f32[]{:T(128)} %mul.77), channel_id=1, source_target_pairs={{0,2},{1,3},{2,0},{3,1},{4,6},{5,7},{6,4},{7,5},{8,10},{9,11},{10,... | collective-permute-start | bytes 20 | tf_op jit(solution)/shard_map/ppermute | solution.py:74
  58.3 2.0 pad_maximum_fusion.4
  81.1 4.8 %collective-permute-done.11 = f16[2,128,1024]{2,1,0:T(8,128)(2,1)S(1)} collective-permute-done((f16[2,128,1024]{2,1,0:T(8,128)(2,1)S(1)}, f16[2,128,1024]{2,1,0:T(8,128)(2,1)S(1)}, u32[]{:S(2)}, u32[]{:S(2)}) %collective-permute-start.11) | collective-permute-done | bytes 524320 | tf_op jit(solution)/shard_map/ppermute | solution.py:74
  88.5 3.4 %collective-permute-done.19 = f16[2,128,1024]{2,1,0:T(8,128)(2,1)S(1)} collective-permute-done((f16[2,128,1024]{2,1,0:T(8,128)(2,1)S(1)}, f16[2,128,1024]{2,1,0:T(8,128)(2,1)S(1)}, u32[]{:S(2)}, u32[]{:S(2)}) %collective-permute-start.19) | collective-permute-done | bytes 524320 | tf_op jit(solution)/shard_map/ppermute | solution.py:74
  91.9 11.2 %collective-permute-done.27 = f16[2,128,1024]{2,1,0:T(8,128)(2,1)S(1)} collective-permute-done((f16[2,128,1024]{2,1,0:T(8,128)(2,1)S(1)}, f16[2,128,1024]{2,1,0:T(8,128)(2,1)S(1)}, u32[]{:S(2)}, u32[]{:S(2)}) %collective-permute-start.27) | collective-permute-done | bytes 524320 | tf_op jit(solution)/shard_map/ppermute | solution.py:74
  104.7 9.7 %collective-permute-done.35 = f16[2,128,1024]{2,1,0:T(8,128)(2,1)S(1)} collective-permute-done((f16[2,128,1024]{2,1,0:T(8,128)(2,1)S(1)}, f16[2,128,1024]{2,1,0:T(8,128)(2,1)S(1)}, u32[]{:S(2)}, u32[]{:S(2)}) %collective-permute-start.35) | collective-permute-done | bytes 524320 | tf_op jit(solution)/shard_map/ppermute | solution.py:74
  127.0 2.2 %collective-permute-done.7 = f16[2,128,1024]{2,1,0:T(8,128)(2,1)S(1)} collective-permute-done((f16[2,128,1024]{2,1,0:T(8,128)(2,1)S(1)}, f16[2,128,1024]{2,1,0:T(8,128)(2,1)S(1)}, u32[]{:S(2)}, u32[]{:S(2)}) %collective-permute-start.7) | collective-permute-done | bytes 524320 | tf_op jit(solution)/shard_map/ppermute | solution.py:74
  131.0 5.6 %collective-permute-done.16 = f16[2,128,1024]{2,1,0:T(8,128)(2,1)S(1)} collective-permute-done((f16[2,128,1024]{2,1,0:T(8,128)(2,1)S(1)}, f16[2,128,1024]{2,1,0:T(8,128)(2,1)S(1)}, u32[]{:S(2)}, u32[]{:S(2)}) %collective-permute-start.16) | collective-permute-done | bytes 524320 | tf_op jit(solution)/shard_map/ppermute | solution.py:74
  137.0 10.8 %collective-permute-done.24 = f16[2,128,1024]{2,1,0:T(8,128)(2,1)S(1)} collective-permute-done((f16[2,128,1024]{2,1,0:T(8,128)(2,1)S(1)}, f16[2,128,1024]{2,1,0:T(8,128)(2,1)S(1)}, u32[]{:S(2)}, u32[]{:S(2)}) %collective-permute-start.24) | collective-permute-done | bytes 524320 | tf_op jit(solution)/shard_map/ppermute | solution.py:74
  148.3 8.0 %collective-permute-done.32 = f16[2,128,1024]{2,1,0:T(8,128)(2,1)S(1)} collective-permute-done((f16[2,128,1024]{2,1,0:T(8,128)(2,1)S(1)}, f16[2,128,1024]{2,1,0:T(8,128)(2,1)S(1)}, u32[]{:S(2)}, u32[]{:S(2)}) %collective-permute-start.32) | collective-permute-done | bytes 524320 | tf_op jit(solution)/shard_map/ppermute | solution.py:74
  159.3 3.4 %collective-permute-done.8 = f16[1,128,1024]{2,1,0:T(8,128)(2,1)S(1)} collective-permute-done((f16[1,128,1024]{2,1,0:T(8,128)(2,1)S(1)}, f16[1,128,1024]{2,1,0:T(8,128)(2,1)S(1)}, u32[]{:S(2)}, u32[]{:S(2)}) %collective-permute-start.8) | collective-permute-done | bytes 262176 | tf_op jit(solution)/shard_map/ppermute | solution.py:74
  164.9 8.8 %collective-permute-done.17 = f16[1,128,1024]{2,1,0:T(8,128)(2,1)S(1)} collective-permute-done((f16[1,128,1024]{2,1,0:T(8,128)(2,1)S(1)}, f16[1,128,1024]{2,1,0:T(8,128)(2,1)S(1)}, u32[]{:S(2)}, u32[]{:S(2)}) %collective-permute-start.17) | collective-permute-done | bytes 262176 | tf_op jit(solution)/shard_map/ppermute | solution.py:74
  174.4 2.4 %collective-permute-start.21 = (f16[128,1024]{1,0:T(8,128)(2,1)S(1)}, f16[128,1024]{1,0:T(8,128)(2,1)S(1)}, u32[]{:S(2)}, u32[]{:S(2)}) collective-permute-start(f16[128,1024]{1,0:T(8,128)(2,1)S(1)} %fusion.65), channel_id=1, source_target_pairs={{0,16},{4,20},{8,24},{12,28},{16,0},{20,4},{24,8},{28,12},{1,17},{... | collective-permute-start | bytes 786440 | tf_op jit(solution)/shard_map/ppermute | solution.py:74
  176.8 4.2 %collective-permute-done.25 = f16[1,128,1024]{2,1,0:T(8,128)(2,1)S(1)} collective-permute-done((f16[1,128,1024]{2,1,0:T(8,128)(2,1)S(1)}, f16[1,128,1024]{2,1,0:T(8,128)(2,1)S(1)}, u32[]{:S(2)}, u32[]{:S(2)}) %collective-permute-start.25) | collective-permute-done | bytes 262176 | tf_op jit(solution)/shard_map/ppermute | solution.py:74
  181.3 2.8 %collective-permute-done.33 = f16[1,128,1024]{2,1,0:T(8,128)(2,1)S(1)} collective-permute-done((f16[1,128,1024]{2,1,0:T(8,128)(2,1)S(1)}, f16[1,128,1024]{2,1,0:T(8,128)(2,1)S(1)}, u32[]{:S(2)}, u32[]{:S(2)}) %collective-permute-start.33) | collective-permute-done | bytes 262176 | tf_op jit(solution)/shard_map/ppermute | solution.py:74
  184.5 19.4 %collective-permute-done.13 = f16[128,1024]{1,0:T(8,128)(2,1)S(1)} collective-permute-done((f16[128,1024]{1,0:T(8,128)(2,1)S(1)}, f16[128,1024]{1,0:T(8,128)(2,1)S(1)}, u32[]{:S(2)}, u32[]{:S(2)}) %collective-permute-start.13) | collective-permute-done | bytes 262176 | tf_op jit(solution)/shard_map/ppermute | solution.py:74
  204.1 3.8 %collective-permute-done.21 = f16[128,1024]{1,0:T(8,128)(2,1)S(1)} collective-permute-done((f16[128,1024]{1,0:T(8,128)(2,1)S(1)}, f16[128,1024]{1,0:T(8,128)(2,1)S(1)}, u32[]{:S(2)}, u32[]{:S(2)}) %collective-permute-start.21) | collective-permute-done | bytes 262176 | tf_op jit(solution)/shard_map/ppermute | solution.py:74
  208.1 2.6 %collective-permute-done.29 = f16[128,1024]{1,0:T(8,128)(2,1)S(1)} collective-permute-done((f16[128,1024]{1,0:T(8,128)(2,1)S(1)}, f16[128,1024]{1,0:T(8,128)(2,1)S(1)}, u32[]{:S(2)}, u32[]{:S(2)}) %collective-permute-start.29) | collective-permute-done | bytes 262176 | tf_op jit(solution)/shard_map/ppermute | solution.py:74
  210.9 2.6 %collective-permute-done.37 = f16[128,1024]{1,0:T(8,128)(2,1)S(1)} collective-permute-done((f16[128,1024]{1,0:T(8,128)(2,1)S(1)}, f16[128,1024]{1,0:T(8,128)(2,1)S(1)}, u32[]{:S(2)}, u32[]{:S(2)}) %collective-permute-start.37) | collective-permute-done | bytes 262176 | tf_op jit(solution)/shard_map/ppermute | solution.py:74
  (137 shorter events, 66.3 us)
Async XLA Ops:
  37.7 24.1 %collective-permute-start.9 = (bf16[2,128,1024]{2,1,0:T(8,128)(2,1)}, bf16[2,128,1024]{2,1,0:T(8,128)(2,1)}, u32[]{:S(2)}, u32[]{:S(2)}) collective-permute-start(bf16[2,128,1024]{2,1,0:T(8,128)(2,1)} %get-tuple-element.11), channel_id=1, source_target_pairs={{0,1},{1,0},{2,3},{3,2},{4,5},{5,4},{6,7},{7,6},{8,9},{9,8},{10,11... | collective-permute-start | bytes 1572872 | tf_op jit(solution)/shard_map/ppermute | solution.py:74
  37.7 37.2 %collective-permute-start.3 = (bf16[2,128,1024]{2,1,0:T(8,128)(2,1)}, bf16[2,128,1024]{2,1,0:T(8,128)(2,1)}, u32[]{:S(2)}, u32[]{:S(2)}) collective-permute-start(bf16[2,128,1024]{2,1,0:T(8,128)(2,1)} %get-tuple-element.11), channel_id=1, source_target_pairs={{0,2},{1,3},{2,0},{3,1},{4,6},{5,7},{6,4},{7,5},{8,10},{9,11},{10,... | collective-permute-start | bytes 1572872 | tf_op jit(solution)/shard_map/ppermute | solution.py:74
  50.8 29.7 %collective-permute-start.30 = (bf16[2,128,1024]{2,1,0:T(8,128)(2,1)}, bf16[2,128,1024]{2,1,0:T(8,128)(2,1)}, u32[]{:S(2)}, u32[]{:S(2)}) collective-permute-start(bf16[2,128,1024]{2,1,0:T(8,128)(2,1)} %get-tuple-element.10), channel_id=1, source_target_pairs={{0,2},{1,3},{2,0},{3,1},{4,6},{5,7},{6,4},{7,5},{8,10},{9,11},{10,... | collective-permute-start | bytes 1572872 | tf_op jit(solution)/shard_map/ppermute | solution.py:74
  61.8 26.1 %collective-permute-start.22 = (bf16[2,128,1024]{2,1,0:T(8,128)(2,1)}, bf16[2,128,1024]{2,1,0:T(8,128)(2,1)S(1)}, u32[]{:S(2)}, u32[]{:S(2)}) collective-permute-start(bf16[2,128,1024]{2,1,0:T(8,128)(2,1)} %get-tuple-element.13), channel_id=1, source_target_pairs={{0,2},{1,3},{2,0},{3,1},{4,6},{5,7},{6,4},{7,5},{8,10},{9,11},{10,... | collective-permute-start | bytes 1572872 | tf_op jit(solution)/shard_map/ppermute | solution.py:74
  68.1 19.9 %collective-permute-start.14 = (bf16[2,128,1024]{2,1,0:T(8,128)(2,1)S(1)}, bf16[2,128,1024]{2,1,0:T(8,128)(2,1)S(1)}, u32[]{:S(2)}, u32[]{:S(2)}) collective-permute-start(bf16[2,128,1024]{2,1,0:T(8,128)(2,1)S(1)} %copy-done.4), channel_id=1, source_target_pairs={{0,2},{1,3},{2,0},{3,1},{4,6},{5,7},{6,4},{7,5},{8,10},{9,11},{10,... | collective-permute-start | bytes 1572872 | tf_op jit(solution)/shard_map/ppermute | solution.py:74
  80.6 22.6 %collective-permute-start.27 = (f16[2,128,1024]{2,1,0:T(8,128)(2,1)S(1)}, f16[2,128,1024]{2,1,0:T(8,128)(2,1)S(1)}, u32[]{:S(2)}, u32[]{:S(2)}) collective-permute-start(f16[2,128,1024]{2,1,0:T(8,128)(2,1)S(1)} %get-tuple-element.55), channel_id=1, source_target_pairs={{0,4},{4,0},{8,12},{12,8},{16,20},{20,16},{24,28},{28,24},{1,5},{5... | collective-permute-start | bytes 1572872 | tf_op jit(solution)/shard_map/ppermute | solution.py:74
  85.9 28.4 %collective-permute-start.35 = (f16[2,128,1024]{2,1,0:T(8,128)(2,1)S(1)}, f16[2,128,1024]{2,1,0:T(8,128)(2,1)S(1)}, u32[]{:S(2)}, u32[]{:S(2)}) collective-permute-start(f16[2,128,1024]{2,1,0:T(8,128)(2,1)S(1)} %get-tuple-element.56), channel_id=1, source_target_pairs={{0,4},{4,0},{8,12},{12,8},{16,20},{20,16},{24,28},{28,24},{1,5},{5... | collective-permute-start | bytes 1572872 | tf_op jit(solution)/shard_map/ppermute | solution.py:74
  87.9 27.8 %collective-permute-start.31 = (bf16[2,128,1024]{2,1,0:T(8,128)(2,1)}, bf16[2,128,1024]{2,1,0:T(8,128)(2,1)S(1)}, u32[]{:S(2)}, u32[]{:S(2)}) collective-permute-start(bf16[2,128,1024]{2,1,0:T(8,128)(2,1)} %collective-permute-done.30), channel_id=1, source_target_pairs={{0,1},{1,0},{2,3},{3,2},{4,5},{5,4},{6,7},{7,6},{8,9},{9,8},{10,11... | collective-permute-start | bytes 1572872 | tf_op jit(solution)/shard_map/ppermute | solution.py:74
  88.0 31.2 %collective-permute-start.23 = (bf16[2,128,1024]{2,1,0:T(8,128)(2,1)S(1)}, bf16[2,128,1024]{2,1,0:T(8,128)(2,1)S(1)}, u32[]{:S(2)}, u32[]{:S(2)}) collective-permute-start(bf16[2,128,1024]{2,1,0:T(8,128)(2,1)S(1)} %collective-permute-done.22), channel_id=1, source_target_pairs={{0,1},{1,0},{2,3},{3,2},{4,5},{5,4},{6,7},{7,6},{8,9},{9,8},{10,11... | collective-permute-start | bytes 1572872 | tf_op jit(solution)/shard_map/ppermute | solution.py:74
  91.9 28.4 %collective-permute-start.15 = (bf16[2,128,1024]{2,1,0:T(8,128)(2,1)S(1)}, bf16[2,128,1024]{2,1,0:T(8,128)(2,1)S(1)}, u32[]{:S(2)}, u32[]{:S(2)}) collective-permute-start(bf16[2,128,1024]{2,1,0:T(8,128)(2,1)S(1)} %collective-permute-done.14), channel_id=1, source_target_pairs={{0,1},{1,0},{2,3},{3,2},{4,5},{5,4},{6,7},{7,6},{8,9},{9,8},{10,11... | collective-permute-start | bytes 1572872 | tf_op jit(solution)/shard_map/ppermute | solution.py:74
  103.1 55.6 %collective-permute-start.12 = (f16[1,128,1024]{2,1,0:T(8,128)(2,1)S(1)}, f16[1,128,1024]{2,1,0:T(8,128)(2,1)S(1)}, u32[]{:S(2)}, u32[]{:S(2)}) collective-permute-start(f16[1,128,1024]{2,1,0:T(8,128)(2,1)S(1)} %slice_convert_fusion.6), channel_id=1, source_target_pairs={{0,4},{4,0},{8,12},{12,8},{16,20},{20,16},{24,28},{28,24},{1,5},{5... | collective-permute-start | bytes 786440 | tf_op jit(solution)/shard_map/ppermute | solution.py:74
  115.7 47.6 %collective-permute-start.20 = (f16[1,128,1024]{2,1,0:T(8,128)(2,1)S(1)}, f16[1,128,1024]{2,1,0:T(8,128)(2,1)S(1)}, u32[]{:S(2)}, u32[]{:S(2)}) collective-permute-start(f16[1,128,1024]{2,1,0:T(8,128)(2,1)S(1)} %slice_convert_fusion.4), channel_id=1, source_target_pairs={{0,8},{4,12},{8,0},{12,4},{16,24},{20,28},{24,16},{28,20},{1,9},{5... | collective-permute-start | bytes 786440 | tf_op jit(solution)/shard_map/ppermute | solution.py:74
  121.7 14.9 %collective-permute-start.16 = (f16[2,128,1024]{2,1,0:T(8,128)(2,1)S(1)}, f16[2,128,1024]{2,1,0:T(8,128)(2,1)S(1)}, u32[]{:S(2)}, u32[]{:S(2)}) collective-permute-start(f16[2,128,1024]{2,1,0:T(8,128)(2,1)S(1)} %get-tuple-element.60), channel_id=1, source_target_pairs={{0,4},{4,0},{8,12},{12,8},{16,20},{20,16},{24,28},{28,24},{1,5},{5... | collective-permute-start | bytes 1572872 | tf_op jit(solution)/shard_map/ppermute | solution.py:74
  123.3 24.6 %collective-permute-start.24 = (f16[2,128,1024]{2,1,0:T(8,128)(2,1)S(1)}, f16[2,128,1024]{2,1,0:T(8,128)(2,1)S(1)}, u32[]{:S(2)}, u32[]{:S(2)}) collective-permute-start(f16[2,128,1024]{2,1,0:T(8,128)(2,1)S(1)} %get-tuple-element.61), channel_id=1, source_target_pairs={{0,4},{4,0},{8,12},{12,8},{16,20},{20,16},{24,28},{28,24},{1,5},{5... | collective-permute-start | bytes 1572872 | tf_op jit(solution)/shard_map/ppermute | solution.py:74
  129.2 27.1 %collective-permute-start.32 = (f16[2,128,1024]{2,1,0:T(8,128)(2,1)S(1)}, f16[2,128,1024]{2,1,0:T(8,128)(2,1)S(1)}, u32[]{:S(2)}, u32[]{:S(2)}) collective-permute-start(f16[2,128,1024]{2,1,0:T(8,128)(2,1)S(1)} %get-tuple-element.62), channel_id=1, source_target_pairs={{0,4},{4,0},{8,12},{12,8},{16,20},{20,16},{24,28},{28,24},{1,5},{5... | collective-permute-start | bytes 1572872 | tf_op jit(solution)/shard_map/ppermute | solution.py:74
  136.6 37.8 %collective-permute-start.28 = (f16[1,128,1024]{2,1,0:T(8,128)(2,1)S(1)}, f16[1,128,1024]{2,1,0:T(8,128)(2,1)S(1)}, u32[]{:S(2)}, u32[]{:S(2)}) collective-permute-start(f16[1,128,1024]{2,1,0:T(8,128)(2,1)S(1)} %slice_convert_fusion.2), channel_id=1, source_target_pairs={{0,8},{4,12},{8,0},{12,4},{16,24},{20,28},{24,16},{28,20},{1,9},{5... | collective-permute-start | bytes 786440 | tf_op jit(solution)/shard_map/ppermute | solution.py:74
  147.8 33.5 %collective-permute-start.36 = (f16[1,128,1024]{2,1,0:T(8,128)(2,1)S(1)}, f16[1,128,1024]{2,1,0:T(8,128)(2,1)S(1)}, u32[]{:S(2)}, u32[]{:S(2)}) collective-permute-start(f16[1,128,1024]{2,1,0:T(8,128)(2,1)S(1)} %slice_convert_fusion), channel_id=1, source_target_pairs={{0,8},{4,12},{8,0},{12,4},{16,24},{20,28},{24,16},{28,20},{1,9},{5... | collective-permute-start | bytes 786440 | tf_op jit(solution)/shard_map/ppermute | solution.py:74
  158.8 14.9 %collective-permute-start.17 = (f16[1,128,1024]{2,1,0:T(8,128)(2,1)S(1)}, f16[1,128,1024]{2,1,0:T(8,128)(2,1)S(1)}, u32[]{:S(2)}, u32[]{:S(2)}) collective-permute-start(f16[1,128,1024]{2,1,0:T(8,128)(2,1)S(1)} %slice_convert_fusion.5), channel_id=1, source_target_pairs={{0,8},{4,12},{8,0},{12,4},{16,24},{20,28},{24,16},{28,20},{1,9},{5... | collective-permute-start | bytes 786440 | tf_op jit(solution)/shard_map/ppermute | solution.py:74
  162.7 18.4 %collective-permute-start.25 = (f16[1,128,1024]{2,1,0:T(8,128)(2,1)S(1)}, f16[1,128,1024]{2,1,0:T(8,128)(2,1)S(1)}, u32[]{:S(2)}, u32[]{:S(2)}) collective-permute-start(f16[1,128,1024]{2,1,0:T(8,128)(2,1)S(1)} %slice_convert_fusion.3), channel_id=1, source_target_pairs={{0,8},{4,12},{8,0},{12,4},{16,24},{20,28},{24,16},{28,20},{1,9},{5... | collective-permute-start | bytes 786440 | tf_op jit(solution)/shard_map/ppermute | solution.py:74
  163.3 20.9 %collective-permute-start.33 = (f16[1,128,1024]{2,1,0:T(8,128)(2,1)S(1)}, f16[1,128,1024]{2,1,0:T(8,128)(2,1)S(1)}, u32[]{:S(2)}, u32[]{:S(2)}) collective-permute-start(f16[1,128,1024]{2,1,0:T(8,128)(2,1)S(1)} %slice_convert_fusion.1), channel_id=1, source_target_pairs={{0,8},{4,12},{8,0},{12,4},{16,24},{20,28},{24,16},{28,20},{1,9},{5... | collective-permute-start | bytes 786440 | tf_op jit(solution)/shard_map/ppermute | solution.py:74
  173.7 30.2 %collective-permute-start.13 = (f16[128,1024]{1,0:T(8,128)(2,1)S(1)}, f16[128,1024]{1,0:T(8,128)(2,1)S(1)}, u32[]{:S(2)}, u32[]{:S(2)}) collective-permute-start(f16[128,1024]{1,0:T(8,128)(2,1)S(1)} %fusion.64), channel_id=1, source_target_pairs={{0,16},{4,20},{8,24},{12,28},{16,0},{20,4},{24,8},{28,12},{1,17},{... | collective-permute-start | bytes 786440 | tf_op jit(solution)/shard_map/ppermute | solution.py:74
  174.4 33.5 %collective-permute-start.21 = (f16[128,1024]{1,0:T(8,128)(2,1)S(1)}, f16[128,1024]{1,0:T(8,128)(2,1)S(1)}, u32[]{:S(2)}, u32[]{:S(2)}) collective-permute-start(f16[128,1024]{1,0:T(8,128)(2,1)S(1)} %fusion.65), channel_id=1, source_target_pairs={{0,16},{4,20},{8,24},{12,28},{16,0},{20,4},{24,8},{28,12},{1,17},{... | collective-permute-start | bytes 786440 | tf_op jit(solution)/shard_map/ppermute | solution.py:74
  181.2 29.4 %collective-permute-start.29 = (f16[128,1024]{1,0:T(8,128)(2,1)S(1)}, f16[128,1024]{1,0:T(8,128)(2,1)S(1)}, u32[]{:S(2)}, u32[]{:S(2)}) collective-permute-start(f16[128,1024]{1,0:T(8,128)(2,1)S(1)} %fusion.66), channel_id=1, source_target_pairs={{0,16},{4,20},{8,24},{12,28},{16,0},{20,4},{24,8},{28,12},{1,17},{... | collective-permute-start | bytes 786440 | tf_op jit(solution)/shard_map/ppermute | solution.py:74
  184.3 29.2 %collective-permute-start.37 = (f16[128,1024]{1,0:T(8,128)(2,1)S(1)}, f16[128,1024]{1,0:T(8,128)(2,1)S(1)}, u32[]{:S(2)}, u32[]{:S(2)}) collective-permute-start(f16[128,1024]{1,0:T(8,128)(2,1)S(1)} %fusion.67), channel_id=1, source_target_pairs={{0,16},{4,20},{8,24},{12,28},{16,0},{20,4},{24,8},{28,12},{1,17},{... | collective-permute-start | bytes 786440 | tf_op jit(solution)/shard_map/ppermute | solution.py:74
  (21 other events, 173.1 us)

commit v2 on v0

v2 whole, which is shorter than its diff:
```python
import jax
import jax.numpy as jnp
from jax import lax
from jax.experimental import pallas as pl
from jax.experimental.pallas import tpu as pltpu
from jax.sharding import PartitionSpec as P

BLOCK = 64
CHUNKS = 4
F32, F16, BF16 = jnp.float32, jnp.float16, jnp.bfloat16


def project_kernel(cols_ref, frames_ref, values_ref, window_ref, out_ref, sums_ref, dense_ref):
    row_blocks, nonzero = cols_ref.shape

    @pl.when(pl.program_id(0) == 0)
    def _():
        dense_ref[...] = jnp.zeros_like(dense_ref)
        sums_ref[...] = jnp.zeros_like(sums_ref)
        for r in range(0, row_blocks, 2):
            block = values_ref[r * BLOCK : (r + 2) * BLOCK, :].T
            for h in range(2):
                for k in range(nonzero):
                    start = pl.multiple_of(cols_ref[r + h, k] * BLOCK, BLOCK)
                    dense_ref[pl.ds(start, BLOCK), (r + h) * BLOCK : (r + h + 1) * BLOCK] = block[
                        k * BLOCK : (k + 1) * BLOCK, h * BLOCK : (h + 1) * BLOCK
                    ]

    product = jnp.dot(frames_ref[...], dense_ref[...], preferred_element_type=F32)
    coords = product.astype(BF16)
    out_ref[...] = coords.T
    window = window_ref[...].astype(F32)
    weight = jnp.broadcast_to(window, (8, window.shape[1])).astype(BF16)
    sums_ref[0:1, :] += jnp.dot(weight, coords, preferred_element_type=F32)[0:1]
    sums_ref[1:2, :] += jnp.dot(weight, coords * coords, preferred_element_type=F32)[0:1]
    count = jnp.sum(window, axis=1, keepdims=True)
    sums_ref[2:3, :] += jnp.broadcast_to(count, (1, coords.shape[1]))


def project(frames, values, cols, window):
    rows, cart = frames.shape
    width = values.shape[0]
    tile = min(256, rows)
    return pl.pallas_call(
        project_kernel,
        grid=(rows // tile,),
        in_specs=[
            pl.BlockSpec(memory_space=pltpu.SMEM),
            pl.BlockSpec((tile, cart), lambda i: (i, 0)),
            pl.BlockSpec(values.shape, lambda i: (0, 0)),
            pl.BlockSpec((1, tile), lambda i: (0, i)),
        ],
        out_specs=[
            pl.BlockSpec((width, tile), lambda i: (0, i)),
            pl.BlockSpec((8, width), lambda i: (0, 0)),
        ],
        out_shape=[
            jax.ShapeDtypeStruct((width, rows), BF16),
            jax.ShapeDtypeStruct((8, width), F32),
        ],
        scratch_shapes=[pltpu.VMEM((cart, width), BF16)],
        compiler_params=pltpu.CompilerParams(vmem_limit_bytes=48 * 2**20),
        cost_estimate=pl.CostEstimate(
            flops=2 * rows * cart * width, bytes_accessed=2 * rows * (cart + width), transcendentals=0
        ),
        name="project",
    )(cols, frames, values, window[None, :])


def gram_kernel(which_ref, group_ref, first_ref, second_ref, mine_ref, out_ref):
    part = pl.program_id(0)

    def write(left):
        out_ref[0] = lax.dot_general(
            left, mine_ref[...], (((1,), (1,)), ((), ())), preferred_element_type=F32
        )

    @pl.when(which_ref[part] == 0)
    def _():
        write(first_ref[0])

    @pl.when(which_ref[part] != 0)
    def _():
        write(second_ref[0])


def gram(which, group, first, second, mine):
    n = which.shape[0]
    _, rows, depth = first.shape
    width = mine.shape[0]
    return pl.pallas_call(
        gram_kernel,
        grid_spec=pltpu.PrefetchScalarGridSpec(
            num_scalar_prefetch=2,
            grid=(n,),
            in_specs=[
                pl.BlockSpec((1, rows, depth), lambda i, which, group: (group[i], 0, 0)),
                pl.BlockSpec((1, rows, depth), lambda i, which, group: (group[i], 0, 0)),
                pl.BlockSpec((width, depth), lambda i, which, group: (0, 0)),
            ],
            out_specs=pl.BlockSpec((1, rows, width), lambda i, which, group: (i, 0, 0)),
        ),
        out_shape=jax.ShapeDtypeStruct((n, rows, width), F32),
        compiler_params=pltpu.CompilerParams(vmem_limit_bytes=24 * 2**20),
        cost_estimate=pl.CostEstimate(flops=0, bytes_accessed=0, transcendentals=0),
        name="gram",
    )(which, group, first, second, mine)


def after(x, *gates):
    return lax.optimization_barrier((x,) + gates)[0] if gates else x


def solution(mesh):
    n_f, n_c = mesh.shape["frame"], mesh.shape["coord"]
    m = n_f // n_c
    low = m.bit_length() - 1
    high = n_c.bit_length() - 1
    n_pairs = n_c // 2

    def swap(x, axis, bit):
        return lax.ppermute(x, axis, [(i, i ^ bit) for i in range(mesh.shape[axis])])

    def on_device(frames, b_values, b_cols, frame_window):
        f, c = lax.axis_index("frame"), lax.axis_index("coord")
        coords, sums = project(frames, b_values, b_cols, frame_window)
        width, depth = coords.shape
        rows = width // m // CHUNKS
        for j in range(n_f.bit_length() - 1):
            sums = sums + swap(sums, "frame", 1 << j)
        count = sums[2, 0]
        mean = sums[0] / count
        spread = jnp.maximum(sums[1] - sums[0] * mean, 0.05 * sums[1] * (1.0 / 1024.0))
        largest = jnp.maximum(jnp.max(spread), 1e-30)
        scale = jnp.exp2(jnp.floor(0.5 * jnp.log2(16384.0 / largest)))
        weight = frame_window.astype(F32)
        centered = (weight[None, :] * (coords.astype(F32) - mean[:, None])).astype(BF16)
        mine = (centered.astype(F32) * scale).astype(BF16)

        flip = (f // m) ^ c
        own = mine.reshape(m, CHUNKS, rows, depth)
        panels = {}
        for k in range(CHUNKS):
            panels[0, k] = own[:, k]

        def near(k, *gates):
            panels[1, k] = swap(after(panels[0, k], *gates), "coord", 1)
            return panels[1, k]

        def far(k, *gates):
            for d in range(2, n_c, 2):
                panels[d, k] = swap(after(panels[0, k], *gates), "coord", d)
            return [panels[d, k] for d in range(2, n_c, 2)]

        def far_near(k, *gates):
            for d in range(2, n_c, 2):
                panels[d + 1, k] = swap(after(panels[d, k], *gates), "coord", 1)
            return [panels[d + 1, k] for d in range(2, n_c, 2)]

        class Task:
            def __init__(self, k, pair, order):
                self.order, self.at = order, 0
                n = 1 << len(order)
                which, group = [], []
                for index in range(n):
                    e, delta = 0, 0
                    for pos, what in enumerate(order):
                        bit = (index >> (len(order) - 1 - pos)) & 1
                        if what == "d":
                            delta = bit
                        else:
                            e |= bit << what
                    which.append((flip & 1) ^ delta)
                    group.append(e ^ (f % m))
                both = gram(
                    jnp.stack(which), jnp.stack(group), panels[2 * pair, k], panels[2 * pair + 1, k], mine
                )
                self.send = both[n // 2 :].astype(F16)
                self.keep = both[: n // 2]

            def step(self, *gates):
                what = self.order[self.at]
                if self.at:
                    half = self.keep.shape[0] // 2
                    self.send, self.keep = self.keep[half:].astype(F16), self.keep[:half]
                got = swap(after(self.send, *gates), "frame", m if what == "d" else 1 << what)
                self.keep = self.keep + got.astype(F32)
                self.at += 1
                return got

            def low_steps(self, *gates):
                for _ in range(low):
                    got = self.step(*gates)
                return got

        def tasks(k, far_pairs, order):
            return [Task(k, pair, order) for pair in (range(1, n_pairs) if far_pairs else range(1))]

        def low_steps(group, *gates):
            return [t.low_steps(*gates) for t in group]

        def d_step(group, *gates):
            return [t.step(*gates) for t in group]

        done = {}

        def top_steps(k, *gates):
            parts = [t.keep[0] for t in held[k, 0] + held[k, 1]]
            last = None
            for j in range(1, high):
                pick = ((flip >> j) & 1) == 1
                after_step = []
                for l, h in zip(parts[0::2], parts[1::2]):
                    last = swap(after(jnp.where(pick, l, h).astype(F16), *gates), "frame", m << j)
                    after_step.append(jnp.where(pick, h, l) + last.astype(F32))
                parts = after_step
            done[k] = parts[0]
            return last

        bits = list(range(low))
        low_first, d_first = bits + ["d"], ["d"] + bits
        held = {}
        x1 = far(1)
        near(1)
        near(2)
        near(0)
        near(3)
        x0 = far(0, panels[1, 1])

        def sends(k, far_pairs):
            return [t.send for t in held[k, far_pairs]]

        held[1, 0] = tasks(1, False, low_first)
        y0 = low_steps(held[1, 0])
        held[2, 0] = tasks(2, False, low_first)
        y1 = low_steps(held[2, 0])
        held[0, 0] = tasks(0, False, d_first)
        z00 = d_step(held[0, 0], *sends(1, 0))
        held[3, 0] = tasks(3, False, low_first)

        b0 = y0 + z00 + x1 + sends(2, 0)
        y2 = low_steps(held[0, 0], *b0)
        z10 = d_step(held[1, 0], *b0)
        c1 = far_near(1, *b0)
        x2 = far(2, *b0)
        held[1, 1] = tasks(1, True, low_first)

        b1 = y1 + z10 + x0 + c1 + sends(1, 1)
        c0 = far_near(0, *b1)
        z20 = d_step(held[2, 0], *b1)
        y3 = low_steps(held[1, 1], *b1)
        x3 = far(3, *b1)
        held[0, 1] = tasks(0, True, d_first)

        b2 = y2 + c0 + sends(0, 1) + sends(3, 0)
        z01 = d_step(held[0, 1], *b2)
        y4 = low_steps(held[3, 0], *b2)

        b3 = y3 + z20 + x2
        c2 = far_near(2, *b3)
        z11 = d_step(held[1, 1], *b3)
        held[2, 1] = tasks(2, True, low_first)

        b3b = z01 + z11
        y5 = low_steps(held[0, 1], *b3b)
        t1 = top_steps(1, *b3b)

        b4 = y4 + x3 + c2 + sends(2, 1)
        c3 = far_near(3, *b4)
        z30 = d_step(held[3, 0], *b4)
        y6 = low_steps(held[2, 1], *b4)
        held[3, 1] = tasks(3, True, low_first)

        b5 = y5 + z30 + [t1] + c3 + sends(3, 1)
        t0 = top_steps(0, *b5)
        y7 = low_steps(held[3, 1], *b5)

        b6 = y6
        z21 = d_step(held[2, 1], *b6)
        b6b = z21
        top_steps(2, *b6b)
        b7 = y7
        d_step(held[3, 1], *b7)
        top_steps(3)

        scales = [jnp.full((8, 128), scale)]
        for d in range(1, n_c):
            scales.append(swap(after(scales[d & ~1 if d % 2 else 0], *b4), "coord", 1 if d % 2 else d))
        row_scale = jnp.stack([s[0, 0] for s in scales])[flip]
        factor = 1.0 / (row_scale * scale * (count - 1.0))
        covariance = jnp.concatenate([done[k] * factor for k in range(CHUNKS)])
        return count, mean, covariance

    return jax.shard_map(
        on_device,
        mesh=mesh,
        in_specs=(P("frame", None), P("coord", None), P("coord", None), P("frame")),
        out_specs=(P(), P("coord"), P("frame", "coord")),
        check_vma=False,
    )
```

time: 440 us -> 187 us (0.42)
  waiting for transfers between devices: 338 us -> 67.6 us
  Pallas kernels: 0 us -> 49.6 us
  starting transfers between devices: 0.08 us -> 35.8 us
  matrix products: 27.1 us -> 0 us
  blocking collectives: 22.5 us -> 0 us
  local copies, waits for them, and re-layouts: 26.5 us -> 8.89 us
  between operations: 14.7 us -> 3.32 us
  other arithmetic: 9.16 us -> 18.4 us
    reduce_scatter x1 -> x0, waiting for transfers between devices: 283 us -> none  [on_device(): lax.psum_scatter(lax.dot_general(centered_full, centered_mine, (((0,), (0...]
    ppermute x0 -> x38, waiting for transfers between devices: none -> 67.6 us  [swap(): lax.ppermute(x, axis, [(i, i ^ bit) for i in range(mesh.shape[axis])])]
    all_gather x1 -> x0, waiting for transfers between devices: 54.5 us -> none  [on_device(): centered_full = lax.all_gather(centered_mine, 'coord', axis=1, tiled=True)]
    pallas_call x0 -> x9, Pallas kernels: none -> 49.6 us  [the longest x8 36.1 us: gram(): pl.pallas_call(gram_kernel, grid_spec=pltpu.PrefetchScalarGridSpec(num_sc...]
    ppermute x0 -> x38, starting transfers between devices: none -> 35.8 us  [swap(): lax.ppermute(x, axis, [(i, i ^ bit) for i in range(mesh.shape[axis])])]
    dot_general x3 -> x0, matrix products: 27.1 us -> none  [the longest x1 16.2 us: on_device(): lax.dot_general(centered_full, centered_mine, (((0,), (0,)), ((), ())), p...]
    psum x1 -> x0, blocking collectives: 22.5 us -> none  [on_device(): count, col_sums = lax.psum((local_count, local_sums), 'frame')]
    gather x1 -> x0, local copies, waits for them, and re-layouts: 11.8 us -> none  [project(): picked = jnp.take(blocks, col_blocks, axis=1)]
  transfers between devices with their start and end apart: 2 -> 38, of which waited for: 2 -> 16; matrix products, arithmetic and copies ran while one was open for 0% -> 8% of each run, Pallas kernels for 0% -> 20%
where the time goes in v2:
time: 187 us; the launch traced here: 184 us
  waiting for transfers between devices  67.6 us (36%)
  Pallas kernels  49.6 us (27%)
  starting transfers between devices  35.8 us (19%)
  other arithmetic  18.4 us (10%)
  local copies, waits for them, and re-layouts  8.89 us (5%)
  between operations  3.32 us (2%)
    ppermute x38, waiting for transfers between devices, swap(): lax.ppermute(x, axis, [(i, i ^ bit) for i in range(mesh.shape[axis])])  67.6 us
    pallas_call x8, Pallas kernels, gram(): pl.pallas_call(gram_kernel, grid_spec=pltpu.PrefetchScalarGridSpec(num_sc...  36.1 us
    ppermute x38, starting transfers between devices, swap(): lax.ppermute(x, axis, [(i, i ^ bit) for i in range(mesh.shape[axis])])  35.8 us
    pallas_call x1, Pallas kernels, project(): pl.pallas_call(project_kernel, grid=(rows // tile,), in_specs=[pl.BlockSp...  13.5 us
    unnamed x43, local copies, waits for them, and re-layouts  5.05 us
  transfers between devices with their start and end apart: 38, of which 16 were waited for; matrix products, arithmetic and copies ran while one was open for 8% of the time, Pallas kernels for 20%

profile of v2, /device:TPU:2, one launch (start us, length us, event | category | flops | bytes accessed | tf_op | source)
XLA Modules:
  0.0 183.5 jit_solution(17348093374864999808)
XLA Ops:
  3.3 13.5 %project.1 = (bf16[1024,1024]{1,0:T(8,128)(2,1)S(1)}, f32[8,1024]{1,0:T(8,128)S(1)}) custom-call(s32[16,8]{1,0:T(8,128)S(1)} %copy.7.cols_ref, bf16[1024,4224]{1,0:T(8,128)(2,1)} %frames_ref.1, bf16[1024,512]{1,0:T(8,128)(2,1)S(1)} %copy-done.4, s32[1,1024]{1,0:T(1,128)S(1)} %bitcast.55), custom_call_target="tpu_custom_call" | custom-call | flops 8858370048 | bytes 10747904 | tf_op jit(solution)/shard_map/project/pallas_call | solution.py:44
  19.6 2.4 %collective-permute-done = f32[8,1024]{1,0:T(8,128)S(1)} collective-permute-done((f32[8,1024]{1,0:T(8,128)S(1)}, f32[8,1024]{1,0:T(8,128)S(1)}, u32[]{:S(2)}, u32[]{:S(2)}) %collective-permute-start) | collective-permute-done | bytes 32800 | tf_op jit(solution)/shard_map/ppermute | solution.py:122
  23.6 2.3 %collective-permute-done.1 = f32[8,1024]{1,0:T(8,128)S(1)} collective-permute-done((f32[8,1024]{1,0:T(8,128)S(1)}, f32[8,1024]{1,0:T(8,128)S(1)}, u32[]{:S(2)}, u32[]{:S(2)}) %collective-permute-start.1) | collective-permute-done | bytes 32800 | tf_op jit(solution)/shard_map/ppermute | solution.py:122
  26.0 2.6 %collective-permute-start.2 = (f32[8,1024]{1,0:T(8,128)S(1)}, f32[8,1024]{1,0:T(8,128)S(1)}, u32[]{:S(2)}, u32[]{:S(2)}) collective-permute-start(f32[8,1024]{1,0:T(8,128)S(1)} %add.110), channel_id=1, source_target_pairs={{0,16},{4,20},{8,24},{12,28},{16,0},{20,4},{24,8},{28,12},{1,17},{... | collective-permute-start | bytes 98312 | tf_op jit(solution)/shard_map/ppermute | solution.py:122
  28.5 2.2 %collective-permute-done.2 = f32[8,1024]{1,0:T(8,128)S(1)} collective-permute-done((f32[8,1024]{1,0:T(8,128)S(1)}, f32[8,1024]{1,0:T(8,128)S(1)}, u32[]{:S(2)}, u32[]{:S(2)}) %collective-permute-start.2) | collective-permute-done | bytes 32800 | tf_op jit(solution)/shard_map/ppermute | solution.py:122
  33.4 2.3 %multiply_convert_fusion.mine_ref = bf16[1024,1024]{1,0:T(8,128)(2,1)S(1)} fusion(bf16[1024,1024]{1,0:T(8,128)(2,1)} %copy-done.2, f32[]{:T(128)} %exp2.7, f32[1024]{0:T(1024)S(1)} %get-tuple-element.60, f32[1024]{0:T(1024)S(1)} %convert_element_type.115), kind=kLoop, calls=%fused_computation | loop fusion | flops 7340032 | bytes 4202500 | tf_op jit(solution)/shard_map/convert_element_type | solution.py:138
  40.8 5.2 %gram.9 = f32[4,128,1024]{2,1,0:T(8,128)S(1)} custom-call(s32[4]{0:T(128)S(1)} %get-tuple-element.67.which_ref, s32[4]{0:T(128)S(1)} %get-tuple-element.68.group_ref, bf16[2,128,1024]{2,1,0:T(8,128)(2,1)} %get-tuple-element.63.first_ref, bf16[2,128,1024]{2,1,0:T(8,128)(2,1)} %collective-permute-done.3.second_ref, ...), custom_call_target="tpu_custom_call" | custom-call | tf_op jit(solution)/shard_map/gram/pallas_call | solution.py:91
  47.7 5.2 %gram.10 = f32[4,128,1024]{2,1,0:T(8,128)S(1)} custom-call(s32[4]{0:T(128)S(1)} %get-tuple-element.69.which_ref, s32[4]{0:T(128)S(1)} %get-tuple-element.70.group_ref, bf16[2,128,1024]{2,1,0:T(8,128)(2,1)} %get-tuple-element.33.first_ref, bf16[2,128,1024]{2,1,0:T(8,128)(2,1)} %collective-permute-done.8.second_ref, ...), custom_call_target="tpu_custom_call" | custom-call | tf_op jit(solution)/shard_map/gram/pallas_call | solution.py:91
  54.6 3.9 %gram.8 = f32[4,128,1024]{2,1,0:T(8,128)S(1)} custom-call(s32[4]{0:T(128)S(1)} %get-tuple-element.67.which_ref, s32[4]{0:T(128)S(1)} %get-tuple-element.68.group_ref, bf16[2,128,1024]{2,1,0:T(8,128)(2,1)S(1)} %get-tuple-element.42.first_ref, bf16[2,128,1024]{2,1,0:T(8,128)(2,1)S(1)} %collective-permute-done.5.second_ref, ...), custom_call_target="tpu_custom_call" | custom-call | tf_op jit(solution)/shard_map/gram/pallas_call | solution.py:91
  59.2 3.9 %gram.13 = f32[4,128,1024]{2,1,0:T(8,128)S(1)} custom-call(s32[4]{0:T(128)S(1)} %get-tuple-element.67.which_ref, s32[4]{0:T(128)S(1)} %get-tuple-element.68.group_ref, bf16[2,128,1024]{2,1,0:T(8,128)(2,1)S(1)} %get-tuple-element.46.first_ref, bf16[2,128,1024]{2,1,0:T(8,128)(2,1)S(1)} %collective-permute-done.15.second_ref, ...), custom_call_target="tpu_custom_call" | custom-call | tf_op jit(solution)/shard_map/gram/pallas_call | solution.py:91
  63.2 3.2 %collective-permute-done.9 = f16[2,128,1024]{2,1,0:T(8,128)(2,1)S(1)} collective-permute-done((f16[2,128,1024]{2,1,0:T(8,128)(2,1)S(1)}, f16[2,128,1024]{2,1,0:T(8,128)(2,1)S(1)}, u32[]{:S(2)}, u32[]{:S(2)}) %collective-permute-start.9) | collective-permute-done | bytes 524320 | tf_op jit(solution)/shard_map/ppermute | solution.py:122
  68.8 2.9 %collective-permute-done.6 = f16[2,128,1024]{2,1,0:T(8,128)(2,1)S(1)} collective-permute-done((f16[2,128,1024]{2,1,0:T(8,128)(2,1)S(1)}, f16[2,128,1024]{2,1,0:T(8,128)(2,1)S(1)}, u32[]{:S(2)}, u32[]{:S(2)}) %collective-permute-start.6) | collective-permute-done | bytes 524320 | tf_op jit(solution)/shard_map/ppermute | solution.py:122
  73.0 5.0 %gram.11 = f32[4,128,1024]{2,1,0:T(8,128)S(1)} custom-call(s32[4]{0:T(128)S(1)} %get-tuple-element.67.which_ref, s32[4]{0:T(128)S(1)} %get-tuple-element.68.group_ref, bf16[2,128,1024]{2,1,0:T(8,128)(2,1)} %collective-permute-done.10.first_ref, bf16[2,128,1024]{2,1,0:T(8,128)(2,1)S(1)} %collective-permute-done.12.second_ref, ...), custom_call_target="tpu_custom_call" | custom-call | tf_op jit(solution)/shard_map/gram/pallas_call | solution.py:91
  84.7 9.2 %collective-permute-done.17 = f16[2,128,1024]{2,1,0:T(8,128)(2,1)S(1)} collective-permute-done((f16[2,128,1024]{2,1,0:T(8,128)(2,1)S(1)}, f16[2,128,1024]{2,1,0:T(8,128)(2,1)S(1)}, u32[]{:S(2)}, u32[]{:S(2)}) %collective-permute-start.17) | collective-permute-done | bytes 524320 | tf_op jit(solution)/shard_map/ppermute | solution.py:122
  95.2 4.1 %gram.12 = f32[4,128,1024]{2,1,0:T(8,128)S(1)} custom-call(s32[4]{0:T(128)S(1)} %get-tuple-element.69.which_ref, s32[4]{0:T(128)S(1)} %get-tuple-element.70.group_ref, bf16[2,128,1024]{2,1,0:T(8,128)(2,1)S(1)} %collective-permute-done.4.first_ref, bf16[2,128,1024]{2,1,0:T(8,128)(2,1)S(1)} %collective-permute-done.13.second_ref, ...), custom_call_target="tpu_custom_call" | custom-call | tf_op jit(solution)/shard_map/gram/pallas_call | solution.py:91
  102.9 3.9 %gram.14 = f32[4,128,1024]{2,1,0:T(8,128)S(1)} custom-call(s32[4]{0:T(128)S(1)} %get-tuple-element.67.which_ref, s32[4]{0:T(128)S(1)} %get-tuple-element.68.group_ref, bf16[2,128,1024]{2,1,0:T(8,128)(2,1)S(1)} %collective-permute-done.19.first_ref, bf16[2,128,1024]{2,1,0:T(8,128)(2,1)S(1)} %collective-permute-done.24.second_ref, ...), custom_call_target="tpu_custom_call" | custom-call | tf_op jit(solution)/shard_map/gram/pallas_call | solution.py:91
  107.8 6.0 %collective-permute-done.22 = f16[2,128,1024]{2,1,0:T(8,128)(2,1)S(1)} collective-permute-done((f16[2,128,1024]{2,1,0:T(8,128)(2,1)S(1)}, f16[2,128,1024]{2,1,0:T(8,128)(2,1)S(1)}, u32[]{:S(2)}, u32[]{:S(2)}) %collective-permute-start.22) | collective-permute-done | bytes 524320 | tf_op jit(solution)/shard_map/ppermute | solution.py:122
  115.3 2.8 %collective-permute-start.26 = (f16[128,1024]{1,0:T(8,128)(2,1)}, f16[128,1024]{1,0:T(8,128)(2,1)}, u32[]{:S(2)}, u32[]{:S(2)}) collective-permute-start(f16[128,1024]{1,0:T(8,128)(2,1)} %fusion.5), channel_id=1, source_target_pairs={{0,16},{4,20},{8,24},{12,28},{16,0},{20,4},{24,8},{28,12},{1,17},{... | collective-permute-start | bytes 786440 | tf_op jit(solution)/shard_map/ppermute | solution.py:122
  127.0 4.1 %collective-permute-done.26 = f16[128,1024]{1,0:T(8,128)(2,1)} collective-permute-done((f16[128,1024]{1,0:T(8,128)(2,1)}, f16[128,1024]{1,0:T(8,128)(2,1)}, u32[]{:S(2)}, u32[]{:S(2)}) %collective-permute-start.26) | collective-permute-done | bytes 262176 | tf_op jit(solution)/shard_map/ppermute | solution.py:122
  135.6 5.0 %gram.15 = f32[4,128,1024]{2,1,0:T(8,128)S(1)} custom-call(s32[4]{0:T(128)S(1)} %get-tuple-element.67.which_ref, s32[4]{0:T(128)S(1)} %get-tuple-element.68.group_ref, bf16[2,128,1024]{2,1,0:T(8,128)(2,1)} %collective-permute-done.23.first_ref, bf16[2,128,1024]{2,1,0:T(8,128)(2,1)S(1)} %collective-permute-done.27.second_ref, ...), custom_call_target="tpu_custom_call" | custom-call | tf_op jit(solution)/shard_map/gram/pallas_call | solution.py:91
  146.6 6.4 %collective-permute-done.35 = f16[2,128,1024]{2,1,0:T(8,128)(2,1)S(1)} collective-permute-done((f16[2,128,1024]{2,1,0:T(8,128)(2,1)S(1)}, f16[2,128,1024]{2,1,0:T(8,128)(2,1)S(1)}, u32[]{:S(2)}, u32[]{:S(2)}) %collective-permute-start.35) | collective-permute-done | bytes 524320 | tf_op jit(solution)/shard_map/ppermute | solution.py:122
  154.8 7.6 %collective-permute-done.28 = f16[128,1024]{1,0:T(8,128)(2,1)S(1)} collective-permute-done((f16[128,1024]{1,0:T(8,128)(2,1)S(1)}, f16[128,1024]{1,0:T(8,128)(2,1)S(1)}, u32[]{:S(2)}, u32[]{:S(2)}) %collective-permute-start.28) | collective-permute-done | bytes 262176 | tf_op jit(solution)/shard_map/ppermute | solution.py:122
  163.6 9.2 %collective-permute-done.36 = f16[1,128,1024]{2,1,0:T(8,128)(2,1)S(1)} collective-permute-done((f16[1,128,1024]{2,1,0:T(8,128)(2,1)S(1)}, f16[1,128,1024]{2,1,0:T(8,128)(2,1)S(1)}, u32[]{:S(2)}, u32[]{:S(2)}) %collective-permute-start.36) | collective-permute-done | bytes 262176 | tf_op jit(solution)/shard_map/ppermute | solution.py:122
  173.2 8.5 %collective-permute-done.37 = f16[128,1024]{1,0:T(8,128)(2,1)S(1)} collective-permute-done((f16[128,1024]{1,0:T(8,128)(2,1)S(1)}, f16[128,1024]{1,0:T(8,128)(2,1)S(1)}, u32[]{:S(2)}, u32[]{:S(2)}) %collective-permute-start.37) | collective-permute-done | bytes 262176 | tf_op jit(solution)/shard_map/ppermute | solution.py:122
  (154 shorter events, 58.9 us)
Async XLA Ops:
  37.6 25.6 %collective-permute-start.10 = (bf16[2,128,1024]{2,1,0:T(8,128)(2,1)}, bf16[2,128,1024]{2,1,0:T(8,128)(2,1)}, u32[]{:S(2)}, u32[]{:S(2)}) collective-permute-start(bf16[2,128,1024]{2,1,0:T(8,128)(2,1)} %get-tuple-element.63.first_ref), channel_id=1, source_target_pairs={{0,2},{1,3},{2,0},{3,1},{4,6},{5,7},{6,4},{7,5},{8,10},{9,11},{10,... | collective-permute-start | bytes 1572872 | tf_op jit(solution)/shard_map/ppermute | solution.py:122
  38.4 14.5 %collective-permute-start.5 = (bf16[2,128,1024]{2,1,0:T(8,128)(2,1)S(1)}, bf16[2,128,1024]{2,1,0:T(8,128)(2,1)S(1)}, u32[]{:S(2)}, u32[]{:S(2)}) collective-permute-start(bf16[2,128,1024]{2,1,0:T(8,128)(2,1)S(1)} %get-tuple-element.42.first_ref), channel_id=1, source_target_pairs={{0,1},{1,0},{2,3},{3,2},{4,5},{5,4},{6,7},{7,6},{8,9},{9,8},{10,11... | collective-permute-start | bytes 1572872 | tf_op jit(solution)/shard_map/ppermute | solution.py:122
  38.5 20.1 %collective-permute-start.15 = (bf16[2,128,1024]{2,1,0:T(8,128)(2,1)S(1)}, bf16[2,128,1024]{2,1,0:T(8,128)(2,1)S(1)}, u32[]{:S(2)}, u32[]{:S(2)}) collective-permute-start(bf16[2,128,1024]{2,1,0:T(8,128)(2,1)S(1)} %get-tuple-element.46.first_ref), channel_id=1, source_target_pairs={{0,1},{1,0},{2,3},{3,2},{4,5},{5,4},{6,7},{7,6},{8,9},{9,8},{10,11... | collective-permute-start | bytes 1572872 | tf_op jit(solution)/shard_map/ppermute | solution.py:122
  39.2 38.9 %collective-permute-start.4 = (bf16[2,128,1024]{2,1,0:T(8,128)(2,1)}, bf16[2,128,1024]{2,1,0:T(8,128)(2,1)S(1)}, u32[]{:S(2)}, u32[]{:S(2)}) collective-permute-start(bf16[2,128,1024]{2,1,0:T(8,128)(2,1)} %get-tuple-element.33.first_ref), channel_id=1, source_target_pairs={{0,2},{1,3},{2,0},{3,1},{4,6},{5,7},{6,4},{7,5},{8,10},{9,11},{10,... | collective-permute-start | bytes 1572872 | tf_op jit(solution)/shard_map/ppermute | solution.py:122
  46.1 17.1 %collective-permute-start.7 = (f16[2,128,1024]{2,1,0:T(8,128)(2,1)S(1)}, f16[2,128,1024]{2,1,0:T(8,128)(2,1)S(1)}, u32[]{:S(2)}, u32[]{:S(2)}) collective-permute-start(f16[2,128,1024]{2,1,0:T(8,128)(2,1)S(1)} %slice_convert_fusion.6), channel_id=1, source_target_pairs={{0,4},{4,0},{8,12},{12,8},{16,20},{20,16},{24,28},{28,24},{1,5},{5... | collective-permute-start | bytes 1572872 | tf_op jit(solution)/shard_map/ppermute | solution.py:122
  53.0 13.4 %collective-permute-start.9 = (f16[2,128,1024]{2,1,0:T(8,128)(2,1)S(1)}, f16[2,128,1024]{2,1,0:T(8,128)(2,1)S(1)}, u32[]{:S(2)}, u32[]{:S(2)}) collective-permute-start(f16[2,128,1024]{2,1,0:T(8,128)(2,1)S(1)} %slice_convert_fusion.5), channel_id=1, source_target_pairs={{0,8},{4,12},{8,0},{12,4},{16,24},{20,28},{24,16},{28,20},{1,9},{5... | collective-permute-start | bytes 1572872 | tf_op jit(solution)/shard_map/ppermute | solution.py:122
  58.6 13.1 %collective-permute-start.6 = (f16[2,128,1024]{2,1,0:T(8,128)(2,1)S(1)}, f16[2,128,1024]{2,1,0:T(8,128)(2,1)S(1)}, u32[]{:S(2)}, u32[]{:S(2)}) collective-permute-start(f16[2,128,1024]{2,1,0:T(8,128)(2,1)S(1)} %slice_convert_fusion.7), channel_id=1, source_target_pairs={{0,4},{4,0},{8,12},{12,8},{16,20},{20,16},{24,28},{28,24},{1,5},{5... | collective-permute-start | bytes 1572872 | tf_op jit(solution)/shard_map/ppermute | solution.py:122
  66.6 11.5 %collective-permute-start.11 = (f16[1,128,1024]{2,1,0:T(8,128)(2,1)S(1)}, f16[1,128,1024]{2,1,0:T(8,128)(2,1)S(1)}, u32[]{:S(2)}, u32[]{:S(2)}) collective-permute-start(f16[1,128,1024]{2,1,0:T(8,128)(2,1)S(1)} %slice_convert_fusion.15), channel_id=1, source_target_pairs={{0,8},{4,12},{8,0},{12,4},{16,24},{20,28},{24,16},{28,20},{1,9},{5... | collective-permute-start | bytes 786440 | tf_op jit(solution)/shard_map/ppermute | solution.py:122
  68.3 14.7 %collective-permute-start.19 = (bf16[2,128,1024]{2,1,0:T(8,128)(2,1)S(1)}, bf16[2,128,1024]{2,1,0:T(8,128)(2,1)S(1)}, u32[]{:S(2)}, u32[]{:S(2)}) collective-permute-start(bf16[2,128,1024]{2,1,0:T(8,128)(2,1)S(1)} %get-tuple-element.42.first_ref), channel_id=1, source_target_pairs={{0,2},{1,3},{2,0},{3,1},{4,6},{5,7},{6,4},{7,5},{8,10},{9,11},{10,... | collective-permute-start | bytes 1572872 | tf_op jit(solution)/shard_map/ppermute | solution.py:122
  79.0 14.9 %collective-permute-start.17 = (f16[2,128,1024]{2,1,0:T(8,128)(2,1)S(1)}, f16[2,128,1024]{2,1,0:T(8,128)(2,1)S(1)}, u32[]{:S(2)}, u32[]{:S(2)}) collective-permute-start(f16[2,128,1024]{2,1,0:T(8,128)(2,1)S(1)} %slice_convert_fusion.4), channel_id=1, source_target_pairs={{0,4},{4,0},{8,12},{12,8},{16,20},{20,16},{24,28},{28,24},{1,5},{5... | collective-permute-start | bytes 1572872 | tf_op jit(solution)/shard_map/ppermute | solution.py:122
  80.7 18.6 %collective-permute-start.14 = (f16[1,128,1024]{2,1,0:T(8,128)(2,1)S(1)}, f16[1,128,1024]{2,1,0:T(8,128)(2,1)S(1)}, u32[]{:S(2)}, u32[]{:S(2)}) collective-permute-start(f16[1,128,1024]{2,1,0:T(8,128)(2,1)S(1)} %slice_convert_fusion.14), channel_id=1, source_target_pairs={{0,4},{4,0},{8,12},{12,8},{16,20},{20,16},{24,28},{28,24},{1,5},{5... | collective-permute-start | bytes 786440 | tf_op jit(solution)/shard_map/ppermute | solution.py:122
  81.3 26.5 %collective-permute-start.23 = (bf16[2,128,1024]{2,1,0:T(8,128)(2,1)S(1)}, bf16[2,128,1024]{2,1,0:T(8,128)(2,1)}, u32[]{:S(2)}, u32[]{:S(2)}) collective-permute-start(bf16[2,128,1024]{2,1,0:T(8,128)(2,1)S(1)} %get-tuple-element.46.first_ref), channel_id=1, source_target_pairs={{0,2},{1,3},{2,0},{3,1},{4,6},{5,7},{6,4},{7,5},{8,10},{9,11},{10,... | collective-permute-start | bytes 1572872 | tf_op jit(solution)/shard_map/ppermute | solution.py:122
  83.0 12.2 %collective-permute-start.13 = (bf16[2,128,1024]{2,1,0:T(8,128)(2,1)S(1)}, bf16[2,128,1024]{2,1,0:T(8,128)(2,1)S(1)}, u32[]{:S(2)}, u32[]{:S(2)}) collective-permute-start(bf16[2,128,1024]{2,1,0:T(8,128)(2,1)S(1)} %collective-permute-done.4.first_ref), channel_id=1, source_target_pairs={{0,1},{1,0},{2,3},{3,2},{4,5},{5,4},{6,7},{7,6},{8,9},{9,8},{10,11... | collective-permute-start | bytes 1572872 | tf_op jit(solution)/shard_map/ppermute | solution.py:122
  99.4 14.4 %collective-permute-start.22 = (f16[2,128,1024]{2,1,0:T(8,128)(2,1)S(1)}, f16[2,128,1024]{2,1,0:T(8,128)(2,1)S(1)}, u32[]{:S(2)}, u32[]{:S(2)}) collective-permute-start(f16[2,128,1024]{2,1,0:T(8,128)(2,1)S(1)} %slice_convert_fusion.2), channel_id=1, source_target_pairs={{0,4},{4,0},{8,12},{12,8},{16,20},{20,16},{24,28},{28,24},{1,5},{5... | collective-permute-start | bytes 1572872 | tf_op jit(solution)/shard_map/ppermute | solution.py:122
  100.4 14.9 %collective-permute-start.16 = (f16[2,128,1024]{2,1,0:T(8,128)(2,1)S(1)}, f16[2,128,1024]{2,1,0:T(8,128)(2,1)S(1)}, u32[]{:S(2)}, u32[]{:S(2)}) collective-permute-start(f16[2,128,1024]{2,1,0:T(8,128)(2,1)S(1)} %slice_convert_fusion.3), channel_id=1, source_target_pairs={{0,8},{4,12},{8,0},{12,4},{16,24},{20,28},{24,16},{28,20},{1,9},{5... | collective-permute-start | bytes 1572872 | tf_op jit(solution)/shard_map/ppermute | solution.py:122
  115.3 15.8 %collective-permute-start.26 = (f16[128,1024]{1,0:T(8,128)(2,1)}, f16[128,1024]{1,0:T(8,128)(2,1)}, u32[]{:S(2)}, u32[]{:S(2)}) collective-permute-start(f16[128,1024]{1,0:T(8,128)(2,1)} %fusion.5), channel_id=1, source_target_pairs={{0,16},{4,20},{8,24},{12,28},{16,0},{20,4},{24,8},{28,12},{1,17},{... | collective-permute-start | bytes 786440 | tf_op jit(solution)/shard_map/ppermute | solution.py:122
  118.1 15.1 %collective-permute-start.32 = (f16[2,128,1024]{2,1,0:T(8,128)(2,1)}, f16[2,128,1024]{2,1,0:T(8,128)(2,1)}, u32[]{:S(2)}, u32[]{:S(2)}) collective-permute-start(f16[2,128,1024]{2,1,0:T(8,128)(2,1)} %slice_convert_fusion.1), channel_id=1, source_target_pairs={{0,4},{4,0},{8,12},{12,8},{16,20},{20,16},{24,28},{28,24},{1,5},{5... | collective-permute-start | bytes 1572872 | tf_op jit(solution)/shard_map/ppermute | solution.py:122
  120.0 20.6 %collective-permute-start.21 = (f16[1,128,1024]{2,1,0:T(8,128)(2,1)}, f16[1,128,1024]{2,1,0:T(8,128)(2,1)}, u32[]{:S(2)}, u32[]{:S(2)}) collective-permute-start(f16[1,128,1024]{2,1,0:T(8,128)(2,1)} %slice_convert_fusion.13), channel_id=1, source_target_pairs={{0,4},{4,0},{8,12},{12,8},{16,20},{20,16},{24,28},{28,24},{1,5},{5... | collective-permute-start | bytes 786440 | tf_op jit(solution)/shard_map/ppermute | solution.py:122
  121.8 18.8 %collective-permute-start.25 = (f16[1,128,1024]{2,1,0:T(8,128)(2,1)}, f16[1,128,1024]{2,1,0:T(8,128)(2,1)S(1)}, u32[]{:S(2)}, u32[]{:S(2)}) collective-permute-start(f16[1,128,1024]{2,1,0:T(8,128)(2,1)} %slice_convert_fusion.10), channel_id=1, source_target_pairs={{0,8},{4,12},{8,0},{12,4},{16,24},{20,28},{24,16},{28,20},{1,9},{5... | collective-permute-start | bytes 786440 | tf_op jit(solution)/shard_map/ppermute | solution.py:122
  123.4 12.1 %collective-permute-start.27 = (bf16[2,128,1024]{2,1,0:T(8,128)(2,1)}, bf16[2,128,1024]{2,1,0:T(8,128)(2,1)S(1)}, u32[]{:S(2)}, u32[]{:S(2)}) collective-permute-start(bf16[2,128,1024]{2,1,0:T(8,128)(2,1)} %collective-permute-done.23.first_ref), channel_id=1, source_target_pairs={{0,1},{1,0},{2,3},{3,2},{4,5},{5,4},{6,7},{7,6},{8,9},{9,8},{10,11... | collective-permute-start | bytes 1572872 | tf_op jit(solution)/shard_map/ppermute | solution.py:122
  140.6 12.3 %collective-permute-start.35 = (f16[2,128,1024]{2,1,0:T(8,128)(2,1)S(1)}, f16[2,128,1024]{2,1,0:T(8,128)(2,1)S(1)}, u32[]{:S(2)}, u32[]{:S(2)}) collective-permute-start(f16[2,128,1024]{2,1,0:T(8,128)(2,1)S(1)} %slice_convert_fusion), channel_id=1, source_target_pairs={{0,4},{4,0},{8,12},{12,8},{16,20},{20,16},{24,28},{28,24},{1,5},{5... | collective-permute-start | bytes 1572872 | tf_op jit(solution)/shard_map/ppermute | solution.py:122
  143.4 19.0 %collective-permute-start.28 = (f16[128,1024]{1,0:T(8,128)(2,1)S(1)}, f16[128,1024]{1,0:T(8,128)(2,1)S(1)}, u32[]{:S(2)}, u32[]{:S(2)}) collective-permute-start(f16[128,1024]{1,0:T(8,128)(2,1)S(1)} %fusion.4), channel_id=1, source_target_pairs={{0,16},{4,20},{8,24},{12,28},{16,0},{20,4},{24,8},{28,12},{1,17},{... | collective-permute-start | bytes 786440 | tf_op jit(solution)/shard_map/ppermute | solution.py:122
  145.5 27.6 %collective-permute-start.34 = (f16[128,1024]{1,0:T(8,128)(2,1)S(1)}, f16[128,1024]{1,0:T(8,128)(2,1)S(1)}, u32[]{:S(2)}, u32[]{:S(2)}) collective-permute-start(f16[128,1024]{1,0:T(8,128)(2,1)S(1)} %fusion.6), channel_id=1, source_target_pairs={{0,16},{4,20},{8,24},{12,28},{16,0},{20,4},{24,8},{28,12},{1,17},{... | collective-permute-start | bytes 786440 | tf_op jit(solution)/shard_map/ppermute | solution.py:122
  153.1 19.6 %collective-permute-start.36 = (f16[1,128,1024]{2,1,0:T(8,128)(2,1)S(1)}, f16[1,128,1024]{2,1,0:T(8,128)(2,1)S(1)}, u32[]{:S(2)}, u32[]{:S(2)}) collective-permute-start(f16[1,128,1024]{2,1,0:T(8,128)(2,1)S(1)} %slice_convert_fusion.8), channel_id=1, source_target_pairs={{0,8},{4,12},{8,0},{12,4},{16,24},{20,28},{24,16},{28,20},{1,9},{5... | collective-permute-start | bytes 786440 | tf_op jit(solution)/shard_map/ppermute | solution.py:122
  (35 other events, 276.5 us)

commit v3 on v2

--- a/solution.py
+++ b/solution.py
@@ -6,7 +6,7 @@
 from jax.sharding import PartitionSpec as P
 
 BLOCK = 64
-CHUNKS = 4
+CHUNKS = 2
 F32, F16, BF16 = jnp.float32, jnp.float16, jnp.bfloat16
 
 
@@ -67,7 +67,7 @@
     )(cols, frames, values, window[None, :])
 
 
-def gram_kernel(which_ref, group_ref, first_ref, second_ref, mine_ref, out_ref):
+def gram_kernel(which_ref, group_ref, half_ref, first_ref, second_ref, mine_ref, out_ref):
     part = pl.program_id(0)
 
     def write(left):
@@ -84,27 +84,92 @@
         write(second_ref[0])
 
 
-def gram(which, group, first, second, mine):
+def gram(which, group, half, first, second, mine):
     n = which.shape[0]
     _, rows, depth = first.shape
-    width = mine.shape[0]
+    width = mine.shape[0] // 2
     return pl.pallas_call(
         gram_kernel,
         grid_spec=pltpu.PrefetchScalarGridSpec(
-            num_scalar_prefetch=2,
+            num_scalar_prefetch=3,
             grid=(n,),
             in_specs=[
-                pl.BlockSpec((1, rows, depth), lambda i, which, group: (group[i], 0, 0)),
-                pl.BlockSpec((1, rows, depth), lambda i, which, group: (group[i], 0, 0)),
-                pl.BlockSpec((width, depth), lambda i, which, group: (0, 0)),
+                pl.BlockSpec((1, rows, depth), lambda i, which, group, half: (group[i], 0, 0)),
+                pl.BlockSpec((1, rows, depth), lambda i, which, group, half: (group[i], 0, 0)),
+                pl.BlockSpec((width, depth), lambda i, which, group, half: (half[i], 0)),
             ],
-            out_specs=pl.BlockSpec((1, rows, width), lambda i, which, group: (i, 0, 0)),
+            out_specs=pl.BlockSpec((1, rows, width), lambda i, which, group, half: (i, 0, 0)),
         ),
         out_shape=jax.ShapeDtypeStruct((n, rows, width), F32),
         compiler_params=pltpu.CompilerParams(vmem_limit_bytes=24 * 2**20),
         cost_estimate=pl.CostEstimate(flops=0, bytes_accessed=0, transcendentals=0),
         name="gram",
-    )(which, group, first, second, mine)
+    )(which, group, half, first, second, mine)
+
+
+def assemble_kernel(flags_ref, direct_ref, mirror_ref, diagonal_ref, factor_ref, out_ref):
+    groups, _, group_width = mirror_ref.shape
+    half_width = direct_ref.shape[1]
+    factor = factor_ref[0:1, 0:1]
+    second = flags_ref[0] != 0
+
+    def write(begin, value):
+        out_ref[:, begin : begin + value.shape[1]] = value * factor
+
+    def write_other(begin):
+        @pl.when(flags_ref[1] != 0)
+        def _():
+            write(begin, diagonal_ref[...])
+
+        @pl.when(flags_ref[1] == 0)
+        def _():
+            for pos in range(groups):
+                write(begin + pos * group_width, mirror_ref[pos ^ flags_ref[2]].T)
+
+    @pl.when(second)
+    def _():
+        write(half_width, direct_ref[...])
+        write_other(0)
+
+    @pl.when(jnp.logical_not(second))
+    def _():
+        write(0, direct_ref[...])
+        write_other(half_width)
+
+
+def assemble(flags, direct, mirror, diagonal, factor):
+    rows, half_width = direct.shape
+    return pl.pallas_call(
+        assemble_kernel,
+        in_specs=[pl.BlockSpec(memory_space=pltpu.SMEM)]
+        + [pl.BlockSpec(memory_space=pltpu.VMEM)] * 4,
+        out_specs=pl.BlockSpec(memory_space=pltpu.VMEM),
+        out_shape=jax.ShapeDtypeStruct((rows, 2 * half_width), F32),
+        compiler_params=pltpu.CompilerParams(vmem_limit_bytes=32 * 2**20),
+        name="assemble",
+    )(flags, direct, mirror, diagonal, factor)
+
+
+def moments_kernel(sums_ref, out_ref):
+    total, squares, count = sums_ref[0:1, :], sums_ref[1:2, :], sums_ref[2:3, :]
+    mean = total / count
+    spread = jnp.maximum(squares - total * mean, squares * (0.05 / 1024.0))
+    largest = jnp.maximum(jnp.max(spread, axis=1, keepdims=True), 1e-30)
+    scale = jnp.exp2(jnp.floor(0.5 * jnp.log2(16384.0 / largest)))
+    out_ref[...] = jnp.zeros_like(out_ref)
+    out_ref[0:1, :] = mean
+    out_ref[1:2, :] = jnp.broadcast_to(scale, mean.shape)
+    out_ref[2:3, :] = count
+
+
+def moments(sums):
+    return pl.pallas_call(
+        moments_kernel,
+        in_specs=[pl.BlockSpec(memory_space=pltpu.VMEM)],
+        out_specs=pl.BlockSpec(memory_space=pltpu.VMEM),
+        out_shape=jax.ShapeDtypeStruct(sums.shape, F32),
+        name="moments",
+    )(sums)
 
 
 def after(x, *gates):
@@ -126,18 +191,33 @@
         coords, sums = project(frames, b_values, b_cols, frame_window)
         width, depth = coords.shape
         rows = width // m // CHUNKS
+        raw = coords.reshape(m, CHUNKS, rows, depth)
+        raw_far = {(d, 0): swap(raw[:, 0], "coord", d) for d in range(2, n_c, 2)}
         for j in range(n_f.bit_length() - 1):
             sums = sums + swap(sums, "frame", 1 << j)
-        count = sums[2, 0]
-        mean = sums[0] / count
-        spread = jnp.maximum(sums[1] - sums[0] * mean, 0.05 * sums[1] * (1.0 / 1024.0))
-        largest = jnp.maximum(jnp.max(spread), 1e-30)
-        scale = jnp.exp2(jnp.floor(0.5 * jnp.log2(16384.0 / largest)))
+        pack = moments(sums)
+        mean, scale, count = pack[0], pack[1, 0], pack[2, 0]
         weight = frame_window.astype(F32)
-        centered = (weight[None, :] * (coords.astype(F32) - mean[:, None])).astype(BF16)
-        mine = (centered.astype(F32) * scale).astype(BF16)
+
+        def center(x, mean, scale):
+            centered = (weight * (x.astype(F32) - mean[..., None])).astype(BF16)
+            return (centered.astype(F32) * scale).astype(BF16)
+
+        mine = center(coords, mean, scale)
+        packs = {0: pack, 1: swap(pack, "coord", 1)}
+        for d in range(2, n_c, 2):
+            packs[d] = swap(pack, "coord", d)
+            for k in range(1, CHUNKS):
+                raw_far[d, k] = swap(after(raw[:, k], pack), "coord", d)
+            packs[d + 1] = swap(packs[d], "coord", 1)
 
         flip = (f // m) ^ c
+        a = f % m
+        top = low - 1
+
+        def direct_half(group, d):
+            return (group >> top) ^ ((c ^ d) > c).astype(jnp.int32)
+
         own = mine.reshape(m, CHUNKS, rows, depth)
         panels = {}
         for k in range(CHUNKS):
@@ -149,7 +229,8 @@
 
         def far(k, *gates):
             for d in range(2, n_c, 2):
-                panels[d, k] = swap(after(panels[0, k], *gates), "coord", d)
+                mean_k = packs[d][0].reshape(m, CHUNKS, rows)[:, k]
+                panels[d, k] = center(after(raw_far[d, k], *gates), mean_k, packs[d][1, 0])
             return [panels[d, k] for d in range(2, n_c, 2)]
 
         def far_near(k, *gates):
@@ -161,7 +242,7 @@
             def __init__(self, k, pair, order):
                 self.order, self.at = order, 0
                 n = 1 << len(order)
-                which, group = [], []
+                which, group, half = [], [], []
                 for index in range(n):
                     e, delta = 0, 0
                     for pos, what in enumerate(order):
@@ -171,9 +252,15 @@
                         else:
                             e |= bit << what
                     which.append((flip & 1) ^ delta)
-                    group.append(e ^ (f % m))
+                    group.append(e ^ a)
+                    half.append(direct_half(group[-1], 2 * pair + which[-1]))
                 both = gram(
-                    jnp.stack(which), jnp.stack(group), panels[2 * pair, k], panels[2 * pair + 1, k], mine
+                    jnp.stack(which),
+                    jnp.stack(group),
+                    jnp.stack(half),
+                    panels[2 * pair, k],
+                    panels[2 * pair + 1, k],
+                    mine,
                 )
                 self.send = both[n // 2 :].astype(F16)
                 self.keep = both[: n // 2]
@@ -217,78 +304,112 @@
             done[k] = parts[0]
             return last
 
-        bits = list(range(low))
-        low_first, d_first = bits + ["d"], ["d"] + bits
+        def directed(x, pairs, *gates):
+            return lax.ppermute(after(x, *gates), ("frame", "coord"), pairs)
+
+        class Diagonal:
+            def __init__(self):
+                group = [e ^ a for e in range(m)]
+                whole = mine.reshape(m, CHUNKS * rows, depth)
+                half = [(g >> top) ^ 1 for g in group]
+                zero = jnp.zeros((m,), jnp.int32)
+                both = gram(zero, jnp.stack(group), jnp.stack(half), whole, whole, mine)
+                self.keep, self.send = both[: m // 2], both[m // 2 :].astype(F16)
+
+            def low_steps(self, *gates):
+                for j in reversed(range(low)):
+                    if j < top:
+                        half = self.keep.shape[0] // 2
+                        self.keep, self.send = self.keep[:half], self.keep[half:].astype(F16)
+                    got = swap(after(self.send, *gates), "frame", 1 << j)
+                    self.keep = self.keep + got.astype(F32)
+                return [got]
+
+            def panel_step(self, j, *gates):
+                pairs = []
+                for g in range(n_f):
+                    for d in range(n_c):
+                        if (((g // m) ^ d) & ((2 << j) - 1)) == 1 << j:
+                            pairs.append((g * n_c + d, (g ^ (m << j)) * n_c + d))
+                got = directed(self.keep.astype(F16), pairs, *gates)
+                self.keep = self.keep + got.astype(F32)
+                return [got]
+
+        mirrored = {}
+
+        def mirror(k, *gates):
+            group_width = CHUNKS * rows
+            for i in range(m // 2):
+                pairs = []
+                for r in range(n_c):
+                    for g in range(m):
+                        for d in range(n_c):
+                            if r != d:
+                                there = (((g >> top) ^ (r > d)) << top) | ((g & (m // 2 - 1)) ^ i)
+                                pairs.append(((r * m + g) * n_c + d, (d * m + there) * n_c + r))
+                begin = ((a & (m // 2 - 1)) ^ i) * group_width
+                block = done[k] if m == 2 else lax.dynamic_slice_in_dim(done[k], begin, group_width, 1)
+                mirrored[i, k] = directed(block.astype(F16), pairs, *gates)
+            return [mirrored[i, k] for i in range(m // 2)]
+
+        low_first = list(reversed(range(low))) + ["d"]
+        d_first = ["d"] + list(reversed(range(low)))
         held = {}
-        x1 = far(1)
-        near(1)
-        near(2)
-        near(0)
-        near(3)
-        x0 = far(0, panels[1, 1])
 
         def sends(k, far_pairs):
             return [t.send for t in held[k, far_pairs]]
 
+        row_scale = pack[:, :128]
+        for d in range(1, n_c):
+            row_scale = jnp.where(flip == d, packs[d][:, :128], row_scale)
+        row_scale = row_scale[1:2]
+        factor = 1.0 / (row_scale * scale * (count - 1.0))
+
+        near(0)
+        near(1)
+        diagonal = Diagonal()
+        ye = diagonal.low_steps()
+        held[0, 0] = tasks(0, False, d_first)
+        z00 = d_step(held[0, 0], diagonal.send)
         held[1, 0] = tasks(1, False, low_first)
-        y0 = low_steps(held[1, 0])
-        held[2, 0] = tasks(2, False, low_first)
-        y1 = low_steps(held[2, 0])
-        held[0, 0] = tasks(0, False, d_first)
-        z00 = d_step(held[0, 0], *sends(1, 0))
-        held[3, 0] = tasks(3, False, low_first)
-
-        b0 = y0 + z00 + x1 + sends(2, 0)
-        y2 = low_steps(held[0, 0], *b0)
-        z10 = d_step(held[1, 0], *b0)
-        c1 = far_near(1, *b0)
-        x2 = far(2, *b0)
+        y10 = low_steps(held[1, 0], *sends(0, 0))
+        far(0)
+        far_near(0)
+        held[0, 1] = tasks(0, True, d_first)
+
+        ze = diagonal.panel_step(0, *(ye + sends(0, 0) + sends(1, 0)))
+        b0 = ye + z00 + sends(1, 0) + sends(0, 1)
+        y00 = low_steps(held[0, 0], *b0)
+        z01 = d_step(held[0, 1], *b0)
+        for j in range(1, high):
+            te = diagonal.panel_step(j, *(ze + b0))
+        far(1, *b0)
+        far_near(1)
         held[1, 1] = tasks(1, True, low_first)
 
-        b1 = y1 + z10 + x0 + c1 + sends(1, 1)
-        c0 = far_near(0, *b1)
-        z20 = d_step(held[2, 0], *b1)
-        y3 = low_steps(held[1, 1], *b1)
-        x3 = far(3, *b1)
-        held[0, 1] = tasks(0, True, d_first)
-
-        b2 = y2 + c0 + sends(0, 1) + sends(3, 0)
-        z01 = d_step(held[0, 1], *b2)
-        y4 = low_steps(held[3, 0], *b2)
-
-        b3 = y3 + z20 + x2
-        c2 = far_near(2, *b3)
+        b1 = z01 + y10 + y00 + te + sends(1, 1) + [factor]
+        y01 = low_steps(held[0, 1], *b1)
+        y11 = low_steps(held[1, 1], *y01)
+        z10 = d_step(held[1, 0], *y01)
+
+        t0 = top_steps(0, *y01)
+
+        b3 = y11 + [t0] + z10
         z11 = d_step(held[1, 1], *b3)
-        held[2, 1] = tasks(2, True, low_first)
-
-        b3b = z01 + z11
-        y5 = low_steps(held[0, 1], *b3b)
-        t1 = top_steps(1, *b3b)
-
-        b4 = y4 + x3 + c2 + sends(2, 1)
-        c3 = far_near(3, *b4)
-        z30 = d_step(held[3, 0], *b4)
-        y6 = low_steps(held[2, 1], *b4)
-        held[3, 1] = tasks(3, True, low_first)
-
-        b5 = y5 + z30 + [t1] + c3 + sends(3, 1)
-        t0 = top_steps(0, *b5)
-        y7 = low_steps(held[3, 1], *b5)
-
-        b6 = y6
-        z21 = d_step(held[2, 1], *b6)
-        b6b = z21
-        top_steps(2, *b6b)
-        b7 = y7
-        d_step(held[3, 1], *b7)
-        top_steps(3)
-
-        scales = [jnp.full((8, 128), scale)]
-        for d in range(1, n_c):
-            scales.append(swap(after(scales[d & ~1 if d % 2 else 0], *b4), "coord", 1 if d % 2 else d))
-        row_scale = jnp.stack([s[0, 0] for s in scales])[flip]
-        factor = 1.0 / (row_scale * scale * (count - 1.0))
-        covariance = jnp.concatenate([done[k] * factor for k in range(CHUNKS)])
+        m0 = mirror(0)
+        top_steps(1, *(z11 + m0))
+        mirror(1)
+
+        direct = jnp.concatenate([done[k] for k in range(CHUNKS)])
+        blocks = jnp.stack(
+            [jnp.concatenate([mirrored[i, k] for k in range(CHUNKS)]).astype(F32) for i in range(m // 2)]
+        )
+        flags = jnp.stack(
+            [direct_half(a, flip), (flip == 0).astype(jnp.int32), a & (m // 2 - 1)]
+        )
+        covariance = assemble(
+            flags, direct, blocks, diagonal.keep[0], factor
+        )
         return count, mean, covariance
 
     return jax.shard_map(

time: 187 us -> 168 us (0.90); the launches traced: 184 us -> 167 us
  Pallas kernels: 49.6 us -> 31.6 us
  waiting for transfers between devices: 67.6 us -> 65.6 us
  other arithmetic: 18.4 us -> 20.3 us
    ppermute x38 -> x23, waiting for transfers between devices: 67.6 us -> 40.8 us  [swap(): lax.ppermute(x, axis, [(i, i ^ bit) for i in range(mesh.shape[axis])])]
    ppermute x0 -> x4, waiting for transfers between devices: none -> 24.8 us  [directed(): return lax.ppermute(after(x, *gates), ('frame', 'coord'), pairs)]
    pallas_call x8 -> x5, Pallas kernels: 36.1 us -> 14.3 us  [gram(): pl.pallas_call(gram_kernel, grid_spec=pltpu.PrefetchScalarGridSpec(num_sc...]
    ppermute x0 -> x4, starting transfers between devices: none -> 12.1 us  [directed(): return lax.ppermute(after(x, *gates), ('frame', 'coord'), pairs)]
    ppermute x38 -> x23, starting transfers between devices: 35.8 us -> 25.3 us  [swap(): lax.ppermute(x, axis, [(i, i ^ bit) for i in range(mesh.shape[axis])])]
    convert_element_type x1 -> x8, other arithmetic: 2.27 us -> 11.5 us  [the longest x3 6.11 us: center(): return (centered.astype(F32) * scale).astype(BF16)]
    pallas_call x0 -> x2, Pallas kernels: none -> 3.83 us  [the longest x1 2.36 us: assemble(): pl.pallas_call(assemble_kernel, in_specs=[pl.BlockSpec(memory_space=pltpu...]
    mul x4 -> x0, other arithmetic: 3.13 us -> none  [on_device(): covariance = jnp.concatenate([done[k] * factor for k in range(CHUNKS)])]
  transfers between devices with their start and end apart: 38 -> 27, of which waited for: 16 -> 13; matrix products, arithmetic and copies ran while one was open for 8% -> 14% of each run, Pallas kernels for 20% -> 9%
where the time goes in v3:
time: 168 us; the launch traced here: 167 us
  waiting for transfers between devices  65.6 us (39%)
  starting transfers between devices  37.4 us (22%)
  Pallas kernels  31.6 us (19%)
  other arithmetic  20.3 us (12%)
  local copies, waits for them, and re-layouts  10.1 us (6%)
  between operations  1.84 us (1%)
    ppermute x23, waiting for transfers between devices, swap(): lax.ppermute(x, axis, [(i, i ^ bit) for i in range(mesh.shape[axis])])  40.8 us
    ppermute x23, starting transfers between devices, swap(): lax.ppermute(x, axis, [(i, i ^ bit) for i in range(mesh.shape[axis])])  25.3 us
    ppermute x4, waiting for transfers between devices, directed(): return lax.ppermute(after(x, *gates), ('frame', 'coord'), pairs)  24.8 us
    pallas_call x5, Pallas kernels, gram(): pl.pallas_call(gram_kernel, grid_spec=pltpu.PrefetchScalarGridSpec(num_sc...  14.3 us
    pallas_call x1, Pallas kernels, project(): pl.pallas_call(project_kernel, grid=(rows // tile,), in_specs=[pl.BlockSp...  13.5 us
    ppermute x4, starting transfers between devices, directed(): return lax.ppermute(after(x, *gates), ('frame', 'coord'), pairs)  12.1 us
    convert_element_type x3, other arithmetic, center(): return (centered.astype(F32) * scale).astype(BF16)  6.11 us
    unnamed x45, local copies, waits for them, and re-layouts  4.83 us
  transfers between devices with their start and end apart: 27, of which 13 were waited for; matrix products, arithmetic and copies ran while one was open for 14% of the time, Pallas kernels for 9%

profile of v3, /device:TPU:2, one launch (start us, length us, event | category | flops | bytes accessed | tf_op | source)
XLA Modules:
  0.0 166.9 jit_solution(13953415325443196108)
XLA Ops:
  3.3 13.5 %project.1 = (bf16[1024,1024]{1,0:T(8,128)(2,1)S(1)}, f32[8,1024]{1,0:T(8,128)S(1)}) custom-call(s32[16,8]{1,0:T(8,128)S(1)} %copy.10.cols_ref, bf16[1024,4224]{1,0:T(8,128)(2,1)} %frames_ref.1, bf16[1024,512]{1,0:T(8,128)(2,1)S(1)} %copy-done.9, s32[1,1024]{1,0:T(1,128)S(1)} %bitcast.64), custom_call_target="tpu_custom_call" | custom-call | flops 8858370048 | bytes 10747904 | tf_op jit(solution)/shard_map/project/pallas_call | solution.py:44
  22.5 2.3 %collective-permute-done.1 = f32[8,1024]{1,0:T(8,128)S(1)} collective-permute-done((f32[8,1024]{1,0:T(8,128)S(1)}, f32[8,1024]{1,0:T(8,128)S(1)}, u32[]{:S(2)}, u32[]{:S(2)}) %collective-permute-start.1) | collective-permute-done | bytes 32800 | tf_op jit(solution)/shard_map/ppermute | solution.py:187
  24.8 2.6 %collective-permute-start.2 = (f32[8,1024]{1,0:T(8,128)S(1)}, f32[8,1024]{1,0:T(8,128)S(1)}, u32[]{:S(2)}, u32[]{:S(2)}) collective-permute-start(f32[8,1024]{1,0:T(8,128)S(1)} %add.67), channel_id=1, source_target_pairs={{0,16},{4,20},{8,24},{12,28},{16,0},{20,4},{24,8},{28,12},{1,17},{... | collective-permute-start | bytes 98312 | tf_op jit(solution)/shard_map/ppermute | solution.py:187
  27.5 2.1 %collective-permute-done.2 = f32[8,1024]{1,0:T(8,128)S(1)} collective-permute-done((f32[8,1024]{1,0:T(8,128)S(1)}, f32[8,1024]{1,0:T(8,128)S(1)}, u32[]{:S(2)}, u32[]{:S(2)}) %collective-permute-start.2) | collective-permute-done | bytes 32800 | tf_op jit(solution)/shard_map/ppermute | solution.py:187
  35.2 2.9 %multiply_convert_fusion.mine_ref = bf16[1024,1024]{1,0:T(8,128)(2,1)S(1)} fusion(bf16[1024,1024]{1,0:T(8,128)(2,1)} %copy-done.3, f32[]{:T(128)} %bitcast.16, f32[1024]{0:T(1024)S(1)} %bitcast.67, f32[1024]{0:T(1024)S(1)} %convert_element_type.152), kind=kLoop, calls=%fused_computation | loop fusion | flops 7340032 | bytes 4202500 | tf_op jit(solution)/shard_map/convert_element_type | solution.py:204
  48.6 2.2 %multiply_convert_fusion.4.first_ref = bf16[2,256,1024]{2,1,0:T(8,128)(2,1)S(1)} fusion(bf16[2,256,1024]{2,1,0:T(8,128)(2,1)} %collective-permute-done.3, f32[]{:T(128)} %bitcast.15, f32[2,256]{1,0:T(2,128)S(1)} %bitcast.70, f32[1024]{0:T(1024)S(1)} %convert_element_type.152), kind=kLoop, calls=%fused_computation.4 | loop fusion | flops 3670016 | bytes 2103300 | tf_op jit(solution)/shard_map/convert_element_type | solution.py:204
  50.9 4.6 %gram.7 = f32[4,256,512]{2,1,0:T(8,128)S(1)} custom-call(s32[4]{0:T(128)S(1)} %get-tuple-element.49.which_ref, s32[4]{0:T(128)S(1)} %get-tuple-element.50.group_ref, s32[4]{0:T(128)S(1)} %add_add_fusion.3.half_ref, bf16[2,256,1024]{2,1,0:T(8,128)(2,1)} %get-tuple-element.42.first_ref, bf16[2,256,1024]{2,1,0:T(8,128)(2,1)} %collective-permute-done.7.second_ref, ...), custom_call_target="tpu_custom_call" | custom-call | tf_op jit(solution)/shard_map/gram/pallas_call | solution.py:91
  58.5 2.5 %gram.8 = f32[4,256,512]{2,1,0:T(8,128)S(1)} custom-call(s32[4]{0:T(128)S(1)} %get-tuple-element.51.which_ref, s32[4]{0:T(128)S(1)} %get-tuple-element.52.group_ref, s32[4]{0:T(128)S(1)} %add_add_fusion.6.half_ref, bf16[2,256,1024]{2,1,0:T(8,128)(2,1)S(1)} %get-tuple-element.41.first_ref, bf16[2,256,1024]{2,1,0:T(8,128)(2,1)S(1)} %collective-permute-done.9.second_ref, ...), custom_call_target="tpu_custom_call" | custom-call | tf_op jit(solution)/shard_map/gram/pallas_call | solution.py:91
  63.3 6.8 %collective-permute-done.8 = f16[2,256,512]{2,1,0:T(8,128)(2,1)S(1)} collective-permute-done((f16[2,256,512]{2,1,0:T(8,128)(2,1)S(1)}, f16[2,256,512]{2,1,0:T(8,128)(2,1)S(1)}, u32[]{:S(2)}, u32[]{:S(2)}) %collective-permute-start.8) | collective-permute-done | bytes 524320 | tf_op jit(solution)/shard_map/ppermute | solution.py:187
  70.2 2.5 %gram.5 = f32[4,256,512]{2,1,0:T(8,128)S(1)} custom-call(s32[4]{0:T(128)S(1)} %get-tuple-element.49.which_ref, s32[4]{0:T(128)S(1)} %get-tuple-element.50.group_ref, s32[4]{0:T(128)S(1)} %add_add_fusion.2.half_ref, bf16[2,256,1024]{2,1,0:T(8,128)(2,1)S(1)} %multiply_convert_fusion.4.first_ref, bf16[2,256,1024]{2,1,0:T(8,128)(2,1)S(1)} %collective-permute-done.5.second_ref, ...), custom_call_target="tpu_custom_call" | custom-call | tf_op jit(solution)/shard_map/gram/pallas_call | solution.py:91
  78.3 5.3 %collective-permute-start.14 = (f16[1,512,512]{2,1,0:T(8,128)(2,1)S(1)}, f16[1,512,512]{2,1,0:T(8,128)(2,1)}, u32[]{:S(2)}, u32[]{:S(2)}) collective-permute-start(f16[1,512,512]{2,1,0:T(8,128)(2,1)S(1)} %fusion), channel_id=1, source_target_pairs={{2,18},{6,22},{11,27},{15,31},{16,0},{20,4},{25,9},{29,13}} | collective-permute-start | bytes 1572872 | tf_op jit(solution)/shard_map/ppermute | solution.py:308
  83.6 3.2 %collective-permute-done.10 = f16[2,256,512]{2,1,0:T(8,128)(2,1)S(1)} collective-permute-done((f16[2,256,512]{2,1,0:T(8,128)(2,1)S(1)}, f16[2,256,512]{2,1,0:T(8,128)(2,1)S(1)}, u32[]{:S(2)}, u32[]{:S(2)}) %collective-permute-start.10) | collective-permute-done | bytes 524320 | tf_op jit(solution)/shard_map/ppermute | solution.py:187
  87.9 2.5 %gram.9 = f32[4,256,512]{2,1,0:T(8,128)S(1)} custom-call(s32[4]{0:T(128)S(1)} %get-tuple-element.51.which_ref, s32[4]{0:T(128)S(1)} %get-tuple-element.52.group_ref, s32[4]{0:T(128)S(1)} %add_add_fusion.7.half_ref, bf16[2,256,1024]{2,1,0:T(8,128)(2,1)S(1)} %multiply_convert_fusion.2.first_ref, bf16[2,256,1024]{2,1,0:T(8,128)(2,1)S(1)} %collective-permute-done.16.second_ref, ...), custom_call_target="tpu_custom_call" | custom-call | tf_op jit(solution)/shard_map/gram/pallas_call | solution.py:91
  93.4 6.9 %collective-permute-done.19 = f16[1,256,512]{2,1,0:T(8,128)(2,1)S(1)} collective-permute-done((f16[1,256,512]{2,1,0:T(8,128)(2,1)}, f16[1,256,512]{2,1,0:T(8,128)(2,1)S(1)}, u32[]{:S(2)}, u32[]{:S(2)}) %collective-permute-start.19) | collective-permute-done | bytes 262176 | tf_op jit(solution)/shard_map/ppermute | solution.py:187
  102.8 4.8 %collective-permute-start.20 = (f16[256,512]{1,0:T(8,128)(2,1)S(1)}, f16[256,512]{1,0:T(8,128)(2,1)S(1)}, u32[]{:S(2)}, u32[]{:S(2)}) collective-permute-start(f16[256,512]{1,0:T(8,128)(2,1)S(1)} %fusion.2), channel_id=1, source_target_pairs={{0,16},{4,20},{8,24},{12,28},{16,0},{20,4},{24,8},{28,12},{1,17},{... | collective-permute-start | bytes 786440 | tf_op jit(solution)/shard_map/ppermute | solution.py:187
  107.6 2.5 %collective-permute-start.22 = (f16[1,256,512]{2,1,0:T(8,128)(2,1)S(1)}, f16[1,256,512]{2,1,0:T(8,128)(2,1)S(1)}, u32[]{:S(2)}, u32[]{:S(2)}) collective-permute-start(f16[1,256,512]{2,1,0:T(8,128)(2,1)S(1)} %slice_convert_fusion.5), channel_id=1, source_target_pairs={{0,8},{4,12},{8,0},{12,4},{16,24},{20,28},{24,16},{28,20},{1,9},{5... | collective-permute-start | bytes 786440 | tf_op jit(solution)/shard_map/ppermute | solution.py:187
  110.1 2.4 %collective-permute-done.21 = f16[2,256,512]{2,1,0:T(8,128)(2,1)S(1)} collective-permute-done((f16[2,256,512]{2,1,0:T(8,128)(2,1)S(1)}, f16[2,256,512]{2,1,0:T(8,128)(2,1)S(1)}, u32[]{:S(2)}, u32[]{:S(2)}) %collective-permute-start.21) | collective-permute-done | bytes 524320 | tf_op jit(solution)/shard_map/ppermute | solution.py:187
  112.7 4.8 %collective-permute-done.20 = f16[256,512]{1,0:T(8,128)(2,1)S(1)} collective-permute-done((f16[256,512]{1,0:T(8,128)(2,1)S(1)}, f16[256,512]{1,0:T(8,128)(2,1)S(1)}, u32[]{:S(2)}, u32[]{:S(2)}) %collective-permute-start.20) | collective-permute-done | bytes 262176 | tf_op jit(solution)/shard_map/ppermute | solution.py:187
  120.3 3.1 %collective-permute-start.24 = (f16[256,512]{1,0:T(8,128)(2,1)S(1)}, f16[256,512]{1,0:T(8,128)(2,1)S(1)}, u32[]{:S(2)}, u32[]{:S(2)}) collective-permute-start(f16[256,512]{1,0:T(8,128)(2,1)S(1)} %get-tuple-element.37), channel_id=1, source_target_pairs={{1,8},{2,16},{3,24},{5,12},{6,20},{7,28},{8,5},{10,17},{11,25},{12... | collective-permute-start | bytes 786440 | tf_op jit(solution)/shard_map/ppermute | solution.py:308
  124.1 13.3 %collective-permute-done.24 = f16[256,512]{1,0:T(8,128)(2,1)S(1)} collective-permute-done((f16[256,512]{1,0:T(8,128)(2,1)S(1)}, f16[256,512]{1,0:T(8,128)(2,1)S(1)}, u32[]{:S(2)}, u32[]{:S(2)}) %collective-permute-start.24) | collective-permute-done | bytes 262176 | tf_op jit(solution)/shard_map/ppermute | solution.py:308
  137.4 9.9 %collective-permute-done.25 = f16[256,512]{1,0:T(8,128)(2,1)S(1)} collective-permute-done((f16[256,512]{1,0:T(8,128)(2,1)S(1)}, f16[256,512]{1,0:T(8,128)(2,1)S(1)}, u32[]{:S(2)}, u32[]{:S(2)}) %collective-permute-start.25) | collective-permute-done | bytes 262176 | tf_op jit(solution)/shard_map/ppermute | solution.py:187
  148.9 2.4 %collective-permute-start.26 = (f16[256,512]{1,0:T(8,128)(2,1)S(1)}, f16[256,512]{1,0:T(8,128)(2,1)S(1)}, u32[]{:S(2)}, u32[]{:S(2)}) collective-permute-start(f16[256,512]{1,0:T(8,128)(2,1)S(1)} %get-tuple-element.35), channel_id=1, source_target_pairs={{1,8},{2,16},{3,24},{5,12},{6,20},{7,28},{8,5},{10,17},{11,25},{12... | collective-permute-start | bytes 786440 | tf_op jit(solution)/shard_map/ppermute | solution.py:308
  152.9 11.5 %collective-permute-done.26 = f16[256,512]{1,0:T(8,128)(2,1)S(1)} collective-permute-done((f16[256,512]{1,0:T(8,128)(2,1)S(1)}, f16[256,512]{1,0:T(8,128)(2,1)S(1)}, u32[]{:S(2)}, u32[]{:S(2)}) %collective-permute-start.26) | collective-permute-done | bytes 262176 | tf_op jit(solution)/shard_map/ppermute | solution.py:308
  164.6 2.4 %assemble.1 = f32[512,1024]{1,0:T(8,128)} custom-call(s32[3]{0:T(128)S(1)} %pad_add_fusion.flags_ref, f32[512,512]{1,0:T(8,128)S(1)} %pad_maximum_fusion.direct_ref, f32[1,512,512]{2,1,0:T(8,128)S(1)} %maximum_convert_fusion.mirror_ref, f32[512,512]{1,0:T(8,128)S(1)} %add_bitcast_fusion.diagonal_ref, f32[1,128]{1,0:T(1,128)S(1)} %multiply_divide_fusion.factor_ref), custom_call_target="tpu_custom_call" | custom-call | tf_op jit(solution)/shard_map/assemble/pallas_call | solution.py:142
  (131 shorter events, 48.1 us)
Async XLA Ops:
  19.9 28.7 %collective-permute-start.3 = (bf16[2,256,1024]{2,1,0:T(8,128)(2,1)}, bf16[2,256,1024]{2,1,0:T(8,128)(2,1)}, u32[]{:S(2)}, u32[]{:S(2)}) collective-permute-start(bf16[2,256,1024]{2,1,0:T(8,128)(2,1)} %get-tuple-element.39), channel_id=1, source_target_pairs={{0,2},{1,3},{2,0},{3,1},{4,6},{5,7},{6,4},{7,5},{8,10},{9,11},{10,... | collective-permute-start | bytes 3145736 | tf_op jit(solution)/shard_map/ppermute | solution.py:187
  24.8 4.8 %collective-permute-start.2 = (f32[8,1024]{1,0:T(8,128)S(1)}, f32[8,1024]{1,0:T(8,128)S(1)}, u32[]{:S(2)}, u32[]{:S(2)}) collective-permute-start(f32[8,1024]{1,0:T(8,128)S(1)} %add.67), channel_id=1, source_target_pairs={{0,16},{4,20},{8,24},{12,28},{16,0},{20,4},{24,8},{28,12},{1,17},{... | collective-permute-start | bytes 98312 | tf_op jit(solution)/shard_map/ppermute | solution.py:187
  33.8 12.4 %collective-permute-start.18 = (f32[8,1024]{1,0:T(8,128)}, f32[8,1024]{1,0:T(8,128)S(1)}, u32[]{:S(2)}, u32[]{:S(2)}) collective-permute-start(f32[8,1024]{1,0:T(8,128)} %moments.1), channel_id=1, source_target_pairs={{0,1},{1,0},{2,3},{3,2},{4,5},{5,4},{6,7},{7,6},{8,9},{9,8},{10,11... | collective-permute-start | bytes 98312 | tf_op jit(solution)/shard_map/ppermute | solution.py:187
  33.8 11.7 %collective-permute-start.4 = (f32[8,1024]{1,0:T(8,128)}, f32[8,1024]{1,0:T(8,128)S(1)}, u32[]{:S(2)}, u32[]{:S(2)}) collective-permute-start(f32[8,1024]{1,0:T(8,128)} %moments.1), channel_id=1, source_target_pairs={{0,2},{1,3},{2,0},{3,1},{4,6},{5,7},{6,4},{7,5},{8,10},{9,11},{10,... | collective-permute-start | bytes 98312 | tf_op jit(solution)/shard_map/ppermute | solution.py:187
  41.3 16.0 %collective-permute-start.6 = (f16[1,512,512]{2,1,0:T(8,128)(2,1)}, f16[1,512,512]{2,1,0:T(8,128)(2,1)}, u32[]{:S(2)}, u32[]{:S(2)}) collective-permute-start(f16[1,512,512]{2,1,0:T(8,128)(2,1)} %slice_convert_fusion.3), channel_id=1, source_target_pairs={{0,4},{4,0},{8,12},{12,8},{16,20},{20,16},{24,28},{28,24},{1,5},{5... | collective-permute-start | bytes 1572872 | tf_op jit(solution)/shard_map/ppermute | solution.py:187
  43.0 7.9 %collective-permute-start.7 = (bf16[2,256,1024]{2,1,0:T(8,128)(2,1)}, bf16[2,256,1024]{2,1,0:T(8,128)(2,1)}, u32[]{:S(2)}, u32[]{:S(2)}) collective-permute-start(bf16[2,256,1024]{2,1,0:T(8,128)(2,1)} %get-tuple-element.42.first_ref), channel_id=1, source_target_pairs={{0,1},{1,0},{2,3},{3,2},{4,5},{5,4},{6,7},{7,6},{8,9},{9,8},{10,11... | collective-permute-start | bytes 3145736 | tf_op jit(solution)/shard_map/ppermute | solution.py:187
  46.1 12.4 %collective-permute-start.9 = (bf16[2,256,1024]{2,1,0:T(8,128)(2,1)S(1)}, bf16[2,256,1024]{2,1,0:T(8,128)(2,1)S(1)}, u32[]{:S(2)}, u32[]{:S(2)}) collective-permute-start(bf16[2,256,1024]{2,1,0:T(8,128)(2,1)S(1)} %get-tuple-element.41.first_ref), channel_id=1, source_target_pairs={{0,1},{1,0},{2,3},{3,2},{4,5},{5,4},{6,7},{7,6},{8,9},{9,8},{10,11... | collective-permute-start | bytes 3145736 | tf_op jit(solution)/shard_map/ppermute | solution.py:187
  46.7 26.1 %collective-permute-start.15 = (bf16[2,256,1024]{2,1,0:T(8,128)(2,1)}, bf16[2,256,1024]{2,1,0:T(8,128)(2,1)S(1)}, u32[]{:S(2)}, u32[]{:S(2)}) collective-permute-start(bf16[2,256,1024]{2,1,0:T(8,128)(2,1)} %get-tuple-element.27), channel_id=1, source_target_pairs={{0,2},{1,3},{2,0},{3,1},{4,6},{5,7},{6,4},{7,5},{8,10},{9,11},{10,... | collective-permute-start | bytes 3145736 | tf_op jit(solution)/shard_map/ppermute | solution.py:187
  50.8 19.4 %collective-permute-start.5 = (bf16[2,256,1024]{2,1,0:T(8,128)(2,1)S(1)}, bf16[2,256,1024]{2,1,0:T(8,128)(2,1)S(1)}, u32[]{:S(2)}, u32[]{:S(2)}) collective-permute-start(bf16[2,256,1024]{2,1,0:T(8,128)(2,1)S(1)} %multiply_convert_fusion.4.first_ref), channel_id=1, source_target_pairs={{0,1},{1,0},{2,3},{3,2},{4,5},{5,4},{6,7},{7,6},{8,9},{9,8},{10,11... | collective-permute-start | bytes 3145736 | tf_op jit(solution)/shard_map/ppermute | solution.py:187
  55.6 14.4 %collective-permute-start.8 = (f16[2,256,512]{2,1,0:T(8,128)(2,1)S(1)}, f16[2,256,512]{2,1,0:T(8,128)(2,1)S(1)}, u32[]{:S(2)}, u32[]{:S(2)}) collective-permute-start(f16[2,256,512]{2,1,0:T(8,128)(2,1)S(1)} %slice_convert_fusion.2), channel_id=1, source_target_pairs={{0,8},{4,12},{8,0},{12,4},{16,24},{20,28},{24,16},{28,20},{1,9},{5... | collective-permute-start | bytes 1572872 | tf_op jit(solution)/shard_map/ppermute | solution.py:187
  61.2 14.9 %collective-permute-start.13 = (f16[1,512,512]{2,1,0:T(8,128)(2,1)S(1)}, f16[1,512,512]{2,1,0:T(8,128)(2,1)S(1)}, u32[]{:S(2)}, u32[]{:S(2)}) collective-permute-start(f16[1,512,512]{2,1,0:T(8,128)(2,1)S(1)} %fusion.1), channel_id=1, source_target_pairs={{1,9},{3,11},{5,13},{7,15},{8,0},{10,2},{12,4},{14,6},{17,25},{19,... | collective-permute-start | bytes 1572872 | tf_op jit(solution)/shard_map/ppermute | solution.py:308
  62.5 29.4 %collective-permute-start.11 = (f16[2,256,512]{2,1,0:T(8,128)(2,1)S(1)}, f16[2,256,512]{2,1,0:T(8,128)(2,1)S(1)}, u32[]{:S(2)}, u32[]{:S(2)}) collective-permute-start(f16[2,256,512]{2,1,0:T(8,128)(2,1)S(1)} %slice_convert_fusion.1), channel_id=1, source_target_pairs={{0,4},{4,0},{8,12},{12,8},{16,20},{20,16},{24,28},{28,24},{1,5},{5... | collective-permute-start | bytes 1572872 | tf_op jit(solution)/shard_map/ppermute | solution.py:187
  72.9 14.0 %collective-permute-start.10 = (f16[2,256,512]{2,1,0:T(8,128)(2,1)S(1)}, f16[2,256,512]{2,1,0:T(8,128)(2,1)S(1)}, u32[]{:S(2)}, u32[]{:S(2)}) collective-permute-start(f16[2,256,512]{2,1,0:T(8,128)(2,1)S(1)} %slice_convert_fusion.4), channel_id=1, source_target_pairs={{0,8},{4,12},{8,0},{12,4},{16,24},{20,28},{24,16},{28,20},{1,9},{5... | collective-permute-start | bytes 1572872 | tf_op jit(solution)/shard_map/ppermute | solution.py:187
  75.9 12.0 %collective-permute-start.16 = (bf16[2,256,1024]{2,1,0:T(8,128)(2,1)S(1)}, bf16[2,256,1024]{2,1,0:T(8,128)(2,1)S(1)}, u32[]{:S(2)}, u32[]{:S(2)}) collective-permute-start(bf16[2,256,1024]{2,1,0:T(8,128)(2,1)S(1)} %multiply_convert_fusion.2.first_ref), channel_id=1, source_target_pairs={{0,1},{1,0},{2,3},{3,2},{4,5},{5,4},{6,7},{7,6},{8,9},{9,8},{10,11... | collective-permute-start | bytes 3145736 | tf_op jit(solution)/shard_map/ppermute | solution.py:187
  77.5 14.4 %collective-permute-start.12 = (f16[1,256,512]{2,1,0:T(8,128)(2,1)S(1)}, f16[1,256,512]{2,1,0:T(8,128)(2,1)S(1)}, u32[]{:S(2)}, u32[]{:S(2)}) collective-permute-start(f16[1,256,512]{2,1,0:T(8,128)(2,1)S(1)} %slice_convert_fusion.7), channel_id=1, source_target_pairs={{0,4},{4,0},{8,12},{12,8},{16,20},{20,16},{24,28},{28,24},{1,5},{5... | collective-permute-start | bytes 786440 | tf_op jit(solution)/shard_map/ppermute | solution.py:187
  78.3 14.4 %collective-permute-start.14 = (f16[1,512,512]{2,1,0:T(8,128)(2,1)S(1)}, f16[1,512,512]{2,1,0:T(8,128)(2,1)}, u32[]{:S(2)}, u32[]{:S(2)}) collective-permute-start(f16[1,512,512]{2,1,0:T(8,128)(2,1)S(1)} %fusion), channel_id=1, source_target_pairs={{2,18},{6,22},{11,27},{15,31},{16,0},{20,4},{25,9},{29,13}} | collective-permute-start | bytes 1572872 | tf_op jit(solution)/shard_map/ppermute | solution.py:308
  92.7 7.6 %collective-permute-start.19 = (f16[1,256,512]{2,1,0:T(8,128)(2,1)}, f16[1,256,512]{2,1,0:T(8,128)(2,1)S(1)}, u32[]{:S(2)}, u32[]{:S(2)}) collective-permute-start(f16[1,256,512]{2,1,0:T(8,128)(2,1)} %slice_convert_fusion.8), channel_id=1, source_target_pairs={{0,4},{4,0},{8,12},{12,8},{16,20},{20,16},{24,28},{28,24},{1,5},{5... | collective-permute-start | bytes 786440 | tf_op jit(solution)/shard_map/ppermute | solution.py:187
  100.3 12.1 %collective-permute-start.21 = (f16[2,256,512]{2,1,0:T(8,128)(2,1)S(1)}, f16[2,256,512]{2,1,0:T(8,128)(2,1)S(1)}, u32[]{:S(2)}, u32[]{:S(2)}) collective-permute-start(f16[2,256,512]{2,1,0:T(8,128)(2,1)S(1)} %slice_convert_fusion), channel_id=1, source_target_pairs={{0,4},{4,0},{8,12},{12,8},{16,20},{20,16},{24,28},{28,24},{1,5},{5... | collective-permute-start | bytes 1572872 | tf_op jit(solution)/shard_map/ppermute | solution.py:187
  102.8 14.7 %collective-permute-start.20 = (f16[256,512]{1,0:T(8,128)(2,1)S(1)}, f16[256,512]{1,0:T(8,128)(2,1)S(1)}, u32[]{:S(2)}, u32[]{:S(2)}) collective-permute-start(f16[256,512]{1,0:T(8,128)(2,1)S(1)} %fusion.2), channel_id=1, source_target_pairs={{0,16},{4,20},{8,24},{12,28},{16,0},{20,4},{24,8},{28,12},{1,17},{... | collective-permute-start | bytes 786440 | tf_op jit(solution)/shard_map/ppermute | solution.py:187
  107.6 9.9 %collective-permute-start.22 = (f16[1,256,512]{2,1,0:T(8,128)(2,1)S(1)}, f16[1,256,512]{2,1,0:T(8,128)(2,1)S(1)}, u32[]{:S(2)}, u32[]{:S(2)}) collective-permute-start(f16[1,256,512]{2,1,0:T(8,128)(2,1)S(1)} %slice_convert_fusion.5), channel_id=1, source_target_pairs={{0,8},{4,12},{8,0},{12,4},{16,24},{20,28},{24,16},{28,20},{1,9},{5... | collective-permute-start | bytes 786440 | tf_op jit(solution)/shard_map/ppermute | solution.py:187
  117.5 6.4 %collective-permute-start.23 = (f16[1,256,512]{2,1,0:T(8,128)(2,1)S(1)}, f16[1,256,512]{2,1,0:T(8,128)(2,1)S(1)}, u32[]{:S(2)}, u32[]{:S(2)}) collective-permute-start(f16[1,256,512]{2,1,0:T(8,128)(2,1)S(1)} %slice_convert_fusion.6), channel_id=1, source_target_pairs={{0,8},{4,12},{8,0},{12,4},{16,24},{20,28},{24,16},{28,20},{1,9},{5... | collective-permute-start | bytes 786440 | tf_op jit(solution)/shard_map/ppermute | solution.py:187
  120.3 17.1 %collective-permute-start.24 = (f16[256,512]{1,0:T(8,128)(2,1)S(1)}, f16[256,512]{1,0:T(8,128)(2,1)S(1)}, u32[]{:S(2)}, u32[]{:S(2)}) collective-permute-start(f16[256,512]{1,0:T(8,128)(2,1)S(1)} %get-tuple-element.37), channel_id=1, source_target_pairs={{1,8},{2,16},{3,24},{5,12},{6,20},{7,28},{8,5},{10,17},{11,25},{12... | collective-permute-start | bytes 786440 | tf_op jit(solution)/shard_map/ppermute | solution.py:308
  137.4 10.0 %collective-permute-start.25 = (f16[256,512]{1,0:T(8,128)(2,1)S(1)}, f16[256,512]{1,0:T(8,128)(2,1)S(1)}, u32[]{:S(2)}, u32[]{:S(2)}) collective-permute-start(f16[256,512]{1,0:T(8,128)(2,1)S(1)} %fusion.3), channel_id=1, source_target_pairs={{0,16},{4,20},{8,24},{12,28},{16,0},{20,4},{24,8},{28,12},{1,17},{... | collective-permute-start | bytes 786440 | tf_op jit(solution)/shard_map/ppermute | solution.py:187
  148.9 15.6 %collective-permute-start.26 = (f16[256,512]{1,0:T(8,128)(2,1)S(1)}, f16[256,512]{1,0:T(8,128)(2,1)S(1)}, u32[]{:S(2)}, u32[]{:S(2)}) collective-permute-start(f16[256,512]{1,0:T(8,128)(2,1)S(1)} %get-tuple-element.35), channel_id=1, source_target_pairs={{1,8},{2,16},{3,24},{5,12},{6,20},{7,28},{8,5},{10,17},{11,25},{12... | collective-permute-start | bytes 786440 | tf_op jit(solution)/shard_map/ppermute | solution.py:308
  (24 other events, 209.5 us)

commit v4 on v3

--- a/solution.py
+++ b/solution.py
@@ -153,7 +153,7 @@
 def moments_kernel(sums_ref, out_ref):
     total, squares, count = sums_ref[0:1, :], sums_ref[1:2, :], sums_ref[2:3, :]
     mean = total / count
-    spread = jnp.maximum(squares - total * mean, squares * (0.05 / 1024.0))
+    spread = jnp.maximum(squares - total * mean, 0.0) + squares * (1.0 / 128.0)
     largest = jnp.maximum(jnp.max(spread, axis=1, keepdims=True), 1e-30)
     scale = jnp.exp2(jnp.floor(0.5 * jnp.log2(16384.0 / largest)))
     out_ref[...] = jnp.zeros_like(out_ref)

time: 168 us -> 168 us (level)
  no operation moved by 1% of the time
where the time goes in v4:
time: 168 us; the launch traced here: 167 us
  waiting for transfers between devices  65.6 us (39%)
  starting transfers between devices  37.4 us (22%)
  Pallas kernels  31.6 us (19%)
  other arithmetic  20.3 us (12%)
  local copies, waits for them, and re-layouts  10.1 us (6%)
  between operations  1.84 us (1%)
    ppermute x23, waiting for transfers between devices, swap(): lax.ppermute(x, axis, [(i, i ^ bit) for i in range(mesh.shape[axis])])  40.8 us
    ppermute x23, starting transfers between devices, swap(): lax.ppermute(x, axis, [(i, i ^ bit) for i in range(mesh.shape[axis])])  25.3 us
    ppermute x4, waiting for transfers between devices, directed(): return lax.ppermute(after(x, *gates), ('frame', 'coord'), pairs)  24.8 us
    pallas_call x5, Pallas kernels, gram(): pl.pallas_call(gram_kernel, grid_spec=pltpu.PrefetchScalarGridSpec(num_sc...  14.3 us
    pallas_call x1, Pallas kernels, project(): pl.pallas_call(project_kernel, grid=(rows // tile,), in_specs=[pl.BlockSp...  13.5 us
    ppermute x4, starting transfers between devices, directed(): return lax.ppermute(after(x, *gates), ('frame', 'coord'), pairs)  12.1 us
    convert_element_type x3, other arithmetic, center(): return (centered.astype(F32) * scale).astype(BF16)  6.11 us
    unnamed x45, local copies, waits for them, and re-layouts  4.83 us
  transfers between devices with their start and end apart: 27, of which 13 were waited for; matrix products, arithmetic and copies ran while one was open for 14% of the time, Pallas kernels for 9%

profile of v4, /device:TPU:2, one launch (start us, length us, event | category | flops | bytes accessed | tf_op | source)
XLA Modules:
  0.0 166.9 jit_solution(8450704207932862540)
XLA Ops:
  3.3 13.5 %project.1 = (bf16[1024,1024]{1,0:T(8,128)(2,1)S(1)}, f32[8,1024]{1,0:T(8,128)S(1)}) custom-call(s32[16,8]{1,0:T(8,128)S(1)} %copy.10.cols_ref, bf16[1024,4224]{1,0:T(8,128)(2,1)} %frames_ref.1, bf16[1024,512]{1,0:T(8,128)(2,1)S(1)} %copy-done.9, s32[1,1024]{1,0:T(1,128)S(1)} %bitcast.64), custom_call_target="tpu_custom_call" | custom-call | flops 8858370048 | bytes 10747904 | tf_op jit(solution)/shard_map/project/pallas_call | solution.py:44
  22.5 2.3 %collective-permute-done.1 = f32[8,1024]{1,0:T(8,128)S(1)} collective-permute-done((f32[8,1024]{1,0:T(8,128)S(1)}, f32[8,1024]{1,0:T(8,128)S(1)}, u32[]{:S(2)}, u32[]{:S(2)}) %collective-permute-start.1) | collective-permute-done | bytes 32800 | tf_op jit(solution)/shard_map/ppermute | solution.py:187
  24.8 2.6 %collective-permute-start.2 = (f32[8,1024]{1,0:T(8,128)S(1)}, f32[8,1024]{1,0:T(8,128)S(1)}, u32[]{:S(2)}, u32[]{:S(2)}) collective-permute-start(f32[8,1024]{1,0:T(8,128)S(1)} %add.67), channel_id=1, source_target_pairs={{0,16},{4,20},{8,24},{12,28},{16,0},{20,4},{24,8},{28,12},{1,17},{... | collective-permute-start | bytes 98312 | tf_op jit(solution)/shard_map/ppermute | solution.py:187
  27.5 2.1 %collective-permute-done.2 = f32[8,1024]{1,0:T(8,128)S(1)} collective-permute-done((f32[8,1024]{1,0:T(8,128)S(1)}, f32[8,1024]{1,0:T(8,128)S(1)}, u32[]{:S(2)}, u32[]{:S(2)}) %collective-permute-start.2) | collective-permute-done | bytes 32800 | tf_op jit(solution)/shard_map/ppermute | solution.py:187
  35.2 2.9 %multiply_convert_fusion.mine_ref = bf16[1024,1024]{1,0:T(8,128)(2,1)S(1)} fusion(bf16[1024,1024]{1,0:T(8,128)(2,1)} %copy-done.3, f32[]{:T(128)} %bitcast.16, f32[1024]{0:T(1024)S(1)} %bitcast.67, f32[1024]{0:T(1024)S(1)} %convert_element_type.152), kind=kLoop, calls=%fused_computation | loop fusion | flops 7340032 | bytes 4202500 | tf_op jit(solution)/shard_map/convert_element_type | solution.py:204
  48.6 2.2 %multiply_convert_fusion.4.first_ref = bf16[2,256,1024]{2,1,0:T(8,128)(2,1)S(1)} fusion(bf16[2,256,1024]{2,1,0:T(8,128)(2,1)} %collective-permute-done.3, f32[]{:T(128)} %bitcast.15, f32[2,256]{1,0:T(2,128)S(1)} %bitcast.70, f32[1024]{0:T(1024)S(1)} %convert_element_type.152), kind=kLoop, calls=%fused_computation.4 | loop fusion | flops 3670016 | bytes 2103300 | tf_op jit(solution)/shard_map/convert_element_type | solution.py:204
  50.9 4.6 %gram.7 = f32[4,256,512]{2,1,0:T(8,128)S(1)} custom-call(s32[4]{0:T(128)S(1)} %get-tuple-element.49.which_ref, s32[4]{0:T(128)S(1)} %get-tuple-element.50.group_ref, s32[4]{0:T(128)S(1)} %add_add_fusion.3.half_ref, bf16[2,256,1024]{2,1,0:T(8,128)(2,1)} %get-tuple-element.42.first_ref, bf16[2,256,1024]{2,1,0:T(8,128)(2,1)} %collective-permute-done.7.second_ref, ...), custom_call_target="tpu_custom_call" | custom-call | tf_op jit(solution)/shard_map/gram/pallas_call | solution.py:91
  58.5 2.5 %gram.8 = f32[4,256,512]{2,1,0:T(8,128)S(1)} custom-call(s32[4]{0:T(128)S(1)} %get-tuple-element.51.which_ref, s32[4]{0:T(128)S(1)} %get-tuple-element.52.group_ref, s32[4]{0:T(128)S(1)} %add_add_fusion.6.half_ref, bf16[2,256,1024]{2,1,0:T(8,128)(2,1)S(1)} %get-tuple-element.41.first_ref, bf16[2,256,1024]{2,1,0:T(8,128)(2,1)S(1)} %collective-permute-done.9.second_ref, ...), custom_call_target="tpu_custom_call" | custom-call | tf_op jit(solution)/shard_map/gram/pallas_call | solution.py:91
  63.3 6.8 %collective-permute-done.8 = f16[2,256,512]{2,1,0:T(8,128)(2,1)S(1)} collective-permute-done((f16[2,256,512]{2,1,0:T(8,128)(2,1)S(1)}, f16[2,256,512]{2,1,0:T(8,128)(2,1)S(1)}, u32[]{:S(2)}, u32[]{:S(2)}) %collective-permute-start.8) | collective-permute-done | bytes 524320 | tf_op jit(solution)/shard_map/ppermute | solution.py:187
  70.2 2.5 %gram.5 = f32[4,256,512]{2,1,0:T(8,128)S(1)} custom-call(s32[4]{0:T(128)S(1)} %get-tuple-element.49.which_ref, s32[4]{0:T(128)S(1)} %get-tuple-element.50.group_ref, s32[4]{0:T(128)S(1)} %add_add_fusion.2.half_ref, bf16[2,256,1024]{2,1,0:T(8,128)(2,1)S(1)} %multiply_convert_fusion.4.first_ref, bf16[2,256,1024]{2,1,0:T(8,128)(2,1)S(1)} %collective-permute-done.5.second_ref, ...), custom_call_target="tpu_custom_call" | custom-call | tf_op jit(solution)/shard_map/gram/pallas_call | solution.py:91
  78.3 5.3 %collective-permute-start.14 = (f16[1,512,512]{2,1,0:T(8,128)(2,1)S(1)}, f16[1,512,512]{2,1,0:T(8,128)(2,1)}, u32[]{:S(2)}, u32[]{:S(2)}) collective-permute-start(f16[1,512,512]{2,1,0:T(8,128)(2,1)S(1)} %fusion), channel_id=1, source_target_pairs={{2,18},{6,22},{11,27},{15,31},{16,0},{20,4},{25,9},{29,13}} | collective-permute-start | bytes 1572872 | tf_op jit(solution)/shard_map/ppermute | solution.py:308
  83.6 3.2 %collective-permute-done.10 = f16[2,256,512]{2,1,0:T(8,128)(2,1)S(1)} collective-permute-done((f16[2,256,512]{2,1,0:T(8,128)(2,1)S(1)}, f16[2,256,512]{2,1,0:T(8,128)(2,1)S(1)}, u32[]{:S(2)}, u32[]{:S(2)}) %collective-permute-start.10) | collective-permute-done | bytes 524320 | tf_op jit(solution)/shard_map/ppermute | solution.py:187
  87.9 2.5 %gram.9 = f32[4,256,512]{2,1,0:T(8,128)S(1)} custom-call(s32[4]{0:T(128)S(1)} %get-tuple-element.51.which_ref, s32[4]{0:T(128)S(1)} %get-tuple-element.52.group_ref, s32[4]{0:T(128)S(1)} %add_add_fusion.7.half_ref, bf16[2,256,1024]{2,1,0:T(8,128)(2,1)S(1)} %multiply_convert_fusion.2.first_ref, bf16[2,256,1024]{2,1,0:T(8,128)(2,1)S(1)} %collective-permute-done.16.second_ref, ...), custom_call_target="tpu_custom_call" | custom-call | tf_op jit(solution)/shard_map/gram/pallas_call | solution.py:91
  93.4 6.9 %collective-permute-done.19 = f16[1,256,512]{2,1,0:T(8,128)(2,1)S(1)} collective-permute-done((f16[1,256,512]{2,1,0:T(8,128)(2,1)}, f16[1,256,512]{2,1,0:T(8,128)(2,1)S(1)}, u32[]{:S(2)}, u32[]{:S(2)}) %collective-permute-start.19) | collective-permute-done | bytes 262176 | tf_op jit(solution)/shard_map/ppermute | solution.py:187
  102.8 4.8 %collective-permute-start.20 = (f16[256,512]{1,0:T(8,128)(2,1)S(1)}, f16[256,512]{1,0:T(8,128)(2,1)S(1)}, u32[]{:S(2)}, u32[]{:S(2)}) collective-permute-start(f16[256,512]{1,0:T(8,128)(2,1)S(1)} %fusion.2), channel_id=1, source_target_pairs={{0,16},{4,20},{8,24},{12,28},{16,0},{20,4},{24,8},{28,12},{1,17},{... | collective-permute-start | bytes 786440 | tf_op jit(solution)/shard_map/ppermute | solution.py:187
  107.6 2.5 %collective-permute-start.22 = (f16[1,256,512]{2,1,0:T(8,128)(2,1)S(1)}, f16[1,256,512]{2,1,0:T(8,128)(2,1)S(1)}, u32[]{:S(2)}, u32[]{:S(2)}) collective-permute-start(f16[1,256,512]{2,1,0:T(8,128)(2,1)S(1)} %slice_convert_fusion.5), channel_id=1, source_target_pairs={{0,8},{4,12},{8,0},{12,4},{16,24},{20,28},{24,16},{28,20},{1,9},{5... | collective-permute-start | bytes 786440 | tf_op jit(solution)/shard_map/ppermute | solution.py:187
  110.1 2.4 %collective-permute-done.21 = f16[2,256,512]{2,1,0:T(8,128)(2,1)S(1)} collective-permute-done((f16[2,256,512]{2,1,0:T(8,128)(2,1)S(1)}, f16[2,256,512]{2,1,0:T(8,128)(2,1)S(1)}, u32[]{:S(2)}, u32[]{:S(2)}) %collective-permute-start.21) | collective-permute-done | bytes 524320 | tf_op jit(solution)/shard_map/ppermute | solution.py:187
  112.7 4.8 %collective-permute-done.20 = f16[256,512]{1,0:T(8,128)(2,1)S(1)} collective-permute-done((f16[256,512]{1,0:T(8,128)(2,1)S(1)}, f16[256,512]{1,0:T(8,128)(2,1)S(1)}, u32[]{:S(2)}, u32[]{:S(2)}) %collective-permute-start.20) | collective-permute-done | bytes 262176 | tf_op jit(solution)/shard_map/ppermute | solution.py:187
  120.3 3.1 %collective-permute-start.24 = (f16[256,512]{1,0:T(8,128)(2,1)S(1)}, f16[256,512]{1,0:T(8,128)(2,1)S(1)}, u32[]{:S(2)}, u32[]{:S(2)}) collective-permute-start(f16[256,512]{1,0:T(8,128)(2,1)S(1)} %get-tuple-element.37), channel_id=1, source_target_pairs={{1,8},{2,16},{3,24},{5,12},{6,20},{7,28},{8,5},{10,17},{11,25},{12... | collective-permute-start | bytes 786440 | tf_op jit(solution)/shard_map/ppermute | solution.py:308
  124.1 13.3 %collective-permute-done.24 = f16[256,512]{1,0:T(8,128)(2,1)S(1)} collective-permute-done((f16[256,512]{1,0:T(8,128)(2,1)S(1)}, f16[256,512]{1,0:T(8,128)(2,1)S(1)}, u32[]{:S(2)}, u32[]{:S(2)}) %collective-permute-start.24) | collective-permute-done | bytes 262176 | tf_op jit(solution)/shard_map/ppermute | solution.py:308
  137.4 9.9 %collective-permute-done.25 = f16[256,512]{1,0:T(8,128)(2,1)S(1)} collective-permute-done((f16[256,512]{1,0:T(8,128)(2,1)S(1)}, f16[256,512]{1,0:T(8,128)(2,1)S(1)}, u32[]{:S(2)}, u32[]{:S(2)}) %collective-permute-start.25) | collective-permute-done | bytes 262176 | tf_op jit(solution)/shard_map/ppermute | solution.py:187
  148.9 2.4 %collective-permute-start.26 = (f16[256,512]{1,0:T(8,128)(2,1)S(1)}, f16[256,512]{1,0:T(8,128)(2,1)S(1)}, u32[]{:S(2)}, u32[]{:S(2)}) collective-permute-start(f16[256,512]{1,0:T(8,128)(2,1)S(1)} %get-tuple-element.35), channel_id=1, source_target_pairs={{1,8},{2,16},{3,24},{5,12},{6,20},{7,28},{8,5},{10,17},{11,25},{12... | collective-permute-start | bytes 786440 | tf_op jit(solution)/shard_map/ppermute | solution.py:308
  152.9 11.5 %collective-permute-done.26 = f16[256,512]{1,0:T(8,128)(2,1)S(1)} collective-permute-done((f16[256,512]{1,0:T(8,128)(2,1)S(1)}, f16[256,512]{1,0:T(8,128)(2,1)S(1)}, u32[]{:S(2)}, u32[]{:S(2)}) %collective-permute-start.26) | collective-permute-done | bytes 262176 | tf_op jit(solution)/shard_map/ppermute | solution.py:308
  164.6 2.4 %assemble.1 = f32[512,1024]{1,0:T(8,128)} custom-call(s32[3]{0:T(128)S(1)} %pad_add_fusion.flags_ref, f32[512,512]{1,0:T(8,128)S(1)} %pad_maximum_fusion.direct_ref, f32[1,512,512]{2,1,0:T(8,128)S(1)} %maximum_convert_fusion.mirror_ref, f32[512,512]{1,0:T(8,128)S(1)} %add_bitcast_fusion.diagonal_ref, f32[1,128]{1,0:T(1,128)S(1)} %multiply_divide_fusion.factor_ref), custom_call_target="tpu_custom_call" | custom-call | tf_op jit(solution)/shard_map/assemble/pallas_call | solution.py:142
  (131 shorter events, 48.1 us)
Async XLA Ops:
  19.9 28.7 %collective-permute-start.3 = (bf16[2,256,1024]{2,1,0:T(8,128)(2,1)}, bf16[2,256,1024]{2,1,0:T(8,128)(2,1)}, u32[]{:S(2)}, u32[]{:S(2)}) collective-permute-start(bf16[2,256,1024]{2,1,0:T(8,128)(2,1)} %get-tuple-element.39), channel_id=1, source_target_pairs={{0,2},{1,3},{2,0},{3,1},{4,6},{5,7},{6,4},{7,5},{8,10},{9,11},{10,... | collective-permute-start | bytes 3145736 | tf_op jit(solution)/shard_map/ppermute | solution.py:187
  24.8 4.8 %collective-permute-start.2 = (f32[8,1024]{1,0:T(8,128)S(1)}, f32[8,1024]{1,0:T(8,128)S(1)}, u32[]{:S(2)}, u32[]{:S(2)}) collective-permute-start(f32[8,1024]{1,0:T(8,128)S(1)} %add.67), channel_id=1, source_target_pairs={{0,16},{4,20},{8,24},{12,28},{16,0},{20,4},{24,8},{28,12},{1,17},{... | collective-permute-start | bytes 98312 | tf_op jit(solution)/shard_map/ppermute | solution.py:187
  33.8 12.4 %collective-permute-start.18 = (f32[8,1024]{1,0:T(8,128)}, f32[8,1024]{1,0:T(8,128)S(1)}, u32[]{:S(2)}, u32[]{:S(2)}) collective-permute-start(f32[8,1024]{1,0:T(8,128)} %moments.1), channel_id=1, source_target_pairs={{0,1},{1,0},{2,3},{3,2},{4,5},{5,4},{6,7},{7,6},{8,9},{9,8},{10,11... | collective-permute-start | bytes 98312 | tf_op jit(solution)/shard_map/ppermute | solution.py:187
  33.8 11.7 %collective-permute-start.4 = (f32[8,1024]{1,0:T(8,128)}, f32[8,1024]{1,0:T(8,128)S(1)}, u32[]{:S(2)}, u32[]{:S(2)}) collective-permute-start(f32[8,1024]{1,0:T(8,128)} %moments.1), channel_id=1, source_target_pairs={{0,2},{1,3},{2,0},{3,1},{4,6},{5,7},{6,4},{7,5},{8,10},{9,11},{10,... | collective-permute-start | bytes 98312 | tf_op jit(solution)/shard_map/ppermute | solution.py:187
  41.3 16.0 %collective-permute-start.6 = (f16[1,512,512]{2,1,0:T(8,128)(2,1)}, f16[1,512,512]{2,1,0:T(8,128)(2,1)}, u32[]{:S(2)}, u32[]{:S(2)}) collective-permute-start(f16[1,512,512]{2,1,0:T(8,128)(2,1)} %slice_convert_fusion.3), channel_id=1, source_target_pairs={{0,4},{4,0},{8,12},{12,8},{16,20},{20,16},{24,28},{28,24},{1,5},{5... | collective-permute-start | bytes 1572872 | tf_op jit(solution)/shard_map/ppermute | solution.py:187
  43.0 7.9 %collective-permute-start.7 = (bf16[2,256,1024]{2,1,0:T(8,128)(2,1)}, bf16[2,256,1024]{2,1,0:T(8,128)(2,1)}, u32[]{:S(2)}, u32[]{:S(2)}) collective-permute-start(bf16[2,256,1024]{2,1,0:T(8,128)(2,1)} %get-tuple-element.42.first_ref), channel_id=1, source_target_pairs={{0,1},{1,0},{2,3},{3,2},{4,5},{5,4},{6,7},{7,6},{8,9},{9,8},{10,11... | collective-permute-start | bytes 3145736 | tf_op jit(solution)/shard_map/ppermute | solution.py:187
  46.1 12.4 %collective-permute-start.9 = (bf16[2,256,1024]{2,1,0:T(8,128)(2,1)S(1)}, bf16[2,256,1024]{2,1,0:T(8,128)(2,1)S(1)}, u32[]{:S(2)}, u32[]{:S(2)}) collective-permute-start(bf16[2,256,1024]{2,1,0:T(8,128)(2,1)S(1)} %get-tuple-element.41.first_ref), channel_id=1, source_target_pairs={{0,1},{1,0},{2,3},{3,2},{4,5},{5,4},{6,7},{7,6},{8,9},{9,8},{10,11... | collective-permute-start | bytes 3145736 | tf_op jit(solution)/shard_map/ppermute | solution.py:187
  46.7 26.1 %collective-permute-start.15 = (bf16[2,256,1024]{2,1,0:T(8,128)(2,1)}, bf16[2,256,1024]{2,1,0:T(8,128)(2,1)S(1)}, u32[]{:S(2)}, u32[]{:S(2)}) collective-permute-start(bf16[2,256,1024]{2,1,0:T(8,128)(2,1)} %get-tuple-element.27), channel_id=1, source_target_pairs={{0,2},{1,3},{2,0},{3,1},{4,6},{5,7},{6,4},{7,5},{8,10},{9,11},{10,... | collective-permute-start | bytes 3145736 | tf_op jit(solution)/shard_map/ppermute | solution.py:187
  50.8 19.4 %collective-permute-start.5 = (bf16[2,256,1024]{2,1,0:T(8,128)(2,1)S(1)}, bf16[2,256,1024]{2,1,0:T(8,128)(2,1)S(1)}, u32[]{:S(2)}, u32[]{:S(2)}) collective-permute-start(bf16[2,256,1024]{2,1,0:T(8,128)(2,1)S(1)} %multiply_convert_fusion.4.first_ref), channel_id=1, source_target_pairs={{0,1},{1,0},{2,3},{3,2},{4,5},{5,4},{6,7},{7,6},{8,9},{9,8},{10,11... | collective-permute-start | bytes 3145736 | tf_op jit(solution)/shard_map/ppermute | solution.py:187
  55.6 14.4 %collective-permute-start.8 = (f16[2,256,512]{2,1,0:T(8,128)(2,1)S(1)}, f16[2,256,512]{2,1,0:T(8,128)(2,1)S(1)}, u32[]{:S(2)}, u32[]{:S(2)}) collective-permute-start(f16[2,256,512]{2,1,0:T(8,128)(2,1)S(1)} %slice_convert_fusion.2), channel_id=1, source_target_pairs={{0,8},{4,12},{8,0},{12,4},{16,24},{20,28},{24,16},{28,20},{1,9},{5... | collective-permute-start | bytes 1572872 | tf_op jit(solution)/shard_map/ppermute | solution.py:187
  61.2 14.9 %collective-permute-start.13 = (f16[1,512,512]{2,1,0:T(8,128)(2,1)S(1)}, f16[1,512,512]{2,1,0:T(8,128)(2,1)S(1)}, u32[]{:S(2)}, u32[]{:S(2)}) collective-permute-start(f16[1,512,512]{2,1,0:T(8,128)(2,1)S(1)} %fusion.1), channel_id=1, source_target_pairs={{1,9},{3,11},{5,13},{7,15},{8,0},{10,2},{12,4},{14,6},{17,25},{19,... | collective-permute-start | bytes 1572872 | tf_op jit(solution)/shard_map/ppermute | solution.py:308
  62.5 29.4 %collective-permute-start.11 = (f16[2,256,512]{2,1,0:T(8,128)(2,1)S(1)}, f16[2,256,512]{2,1,0:T(8,128)(2,1)S(1)}, u32[]{:S(2)}, u32[]{:S(2)}) collective-permute-start(f16[2,256,512]{2,1,0:T(8,128)(2,1)S(1)} %slice_convert_fusion.1), channel_id=1, source_target_pairs={{0,4},{4,0},{8,12},{12,8},{16,20},{20,16},{24,28},{28,24},{1,5},{5... | collective-permute-start | bytes 1572872 | tf_op jit(solution)/shard_map/ppermute | solution.py:187
  72.9 14.0 %collective-permute-start.10 = (f16[2,256,512]{2,1,0:T(8,128)(2,1)S(1)}, f16[2,256,512]{2,1,0:T(8,128)(2,1)S(1)}, u32[]{:S(2)}, u32[]{:S(2)}) collective-permute-start(f16[2,256,512]{2,1,0:T(8,128)(2,1)S(1)} %slice_convert_fusion.4), channel_id=1, source_target_pairs={{0,8},{4,12},{8,0},{12,4},{16,24},{20,28},{24,16},{28,20},{1,9},{5... | collective-permute-start | bytes 1572872 | tf_op jit(solution)/shard_map/ppermute | solution.py:187
  75.9 12.0 %collective-permute-start.16 = (bf16[2,256,1024]{2,1,0:T(8,128)(2,1)S(1)}, bf16[2,256,1024]{2,1,0:T(8,128)(2,1)S(1)}, u32[]{:S(2)}, u32[]{:S(2)}) collective-permute-start(bf16[2,256,1024]{2,1,0:T(8,128)(2,1)S(1)} %multiply_convert_fusion.2.first_ref), channel_id=1, source_target_pairs={{0,1},{1,0},{2,3},{3,2},{4,5},{5,4},{6,7},{7,6},{8,9},{9,8},{10,11... | collective-permute-start | bytes 3145736 | tf_op jit(solution)/shard_map/ppermute | solution.py:187
  77.5 14.4 %collective-permute-start.12 = (f16[1,256,512]{2,1,0:T(8,128)(2,1)S(1)}, f16[1,256,512]{2,1,0:T(8,128)(2,1)S(1)}, u32[]{:S(2)}, u32[]{:S(2)}) collective-permute-start(f16[1,256,512]{2,1,0:T(8,128)(2,1)S(1)} %slice_convert_fusion.7), channel_id=1, source_target_pairs={{0,4},{4,0},{8,12},{12,8},{16,20},{20,16},{24,28},{28,24},{1,5},{5... | collective-permute-start | bytes 786440 | tf_op jit(solution)/shard_map/ppermute | solution.py:187
  78.3 14.4 %collective-permute-start.14 = (f16[1,512,512]{2,1,0:T(8,128)(2,1)S(1)}, f16[1,512,512]{2,1,0:T(8,128)(2,1)}, u32[]{:S(2)}, u32[]{:S(2)}) collective-permute-start(f16[1,512,512]{2,1,0:T(8,128)(2,1)S(1)} %fusion), channel_id=1, source_target_pairs={{2,18},{6,22},{11,27},{15,31},{16,0},{20,4},{25,9},{29,13}} | collective-permute-start | bytes 1572872 | tf_op jit(solution)/shard_map/ppermute | solution.py:308
  92.7 7.6 %collective-permute-start.19 = (f16[1,256,512]{2,1,0:T(8,128)(2,1)}, f16[1,256,512]{2,1,0:T(8,128)(2,1)S(1)}, u32[]{:S(2)}, u32[]{:S(2)}) collective-permute-start(f16[1,256,512]{2,1,0:T(8,128)(2,1)} %slice_convert_fusion.8), channel_id=1, source_target_pairs={{0,4},{4,0},{8,12},{12,8},{16,20},{20,16},{24,28},{28,24},{1,5},{5... | collective-permute-start | bytes 786440 | tf_op jit(solution)/shard_map/ppermute | solution.py:187
  100.3 12.1 %collective-permute-start.21 = (f16[2,256,512]{2,1,0:T(8,128)(2,1)S(1)}, f16[2,256,512]{2,1,0:T(8,128)(2,1)S(1)}, u32[]{:S(2)}, u32[]{:S(2)}) collective-permute-start(f16[2,256,512]{2,1,0:T(8,128)(2,1)S(1)} %slice_convert_fusion), channel_id=1, source_target_pairs={{0,4},{4,0},{8,12},{12,8},{16,20},{20,16},{24,28},{28,24},{1,5},{5... | collective-permute-start | bytes 1572872 | tf_op jit(solution)/shard_map/ppermute | solution.py:187
  102.8 14.7 %collective-permute-start.20 = (f16[256,512]{1,0:T(8,128)(2,1)S(1)}, f16[256,512]{1,0:T(8,128)(2,1)S(1)}, u32[]{:S(2)}, u32[]{:S(2)}) collective-permute-start(f16[256,512]{1,0:T(8,128)(2,1)S(1)} %fusion.2), channel_id=1, source_target_pairs={{0,16},{4,20},{8,24},{12,28},{16,0},{20,4},{24,8},{28,12},{1,17},{... | collective-permute-start | bytes 786440 | tf_op jit(solution)/shard_map/ppermute | solution.py:187
  107.6 9.9 %collective-permute-start.22 = (f16[1,256,512]{2,1,0:T(8,128)(2,1)S(1)}, f16[1,256,512]{2,1,0:T(8,128)(2,1)S(1)}, u32[]{:S(2)}, u32[]{:S(2)}) collective-permute-start(f16[1,256,512]{2,1,0:T(8,128)(2,1)S(1)} %slice_convert_fusion.5), channel_id=1, source_target_pairs={{0,8},{4,12},{8,0},{12,4},{16,24},{20,28},{24,16},{28,20},{1,9},{5... | collective-permute-start | bytes 786440 | tf_op jit(solution)/shard_map/ppermute | solution.py:187
  117.5 6.4 %collective-permute-start.23 = (f16[1,256,512]{2,1,0:T(8,128)(2,1)S(1)}, f16[1,256,512]{2,1,0:T(8,128)(2,1)S(1)}, u32[]{:S(2)}, u32[]{:S(2)}) collective-permute-start(f16[1,256,512]{2,1,0:T(8,128)(2,1)S(1)} %slice_convert_fusion.6), channel_id=1, source_target_pairs={{0,8},{4,12},{8,0},{12,4},{16,24},{20,28},{24,16},{28,20},{1,9},{5... | collective-permute-start | bytes 786440 | tf_op jit(solution)/shard_map/ppermute | solution.py:187
  120.3 17.1 %collective-permute-start.24 = (f16[256,512]{1,0:T(8,128)(2,1)S(1)}, f16[256,512]{1,0:T(8,128)(2,1)S(1)}, u32[]{:S(2)}, u32[]{:S(2)}) collective-permute-start(f16[256,512]{1,0:T(8,128)(2,1)S(1)} %get-tuple-element.37), channel_id=1, source_target_pairs={{1,8},{2,16},{3,24},{5,12},{6,20},{7,28},{8,5},{10,17},{11,25},{12... | collective-permute-start | bytes 786440 | tf_op jit(solution)/shard_map/ppermute | solution.py:308
  137.4 10.0 %collective-permute-start.25 = (f16[256,512]{1,0:T(8,128)(2,1)S(1)}, f16[256,512]{1,0:T(8,128)(2,1)S(1)}, u32[]{:S(2)}, u32[]{:S(2)}) collective-permute-start(f16[256,512]{1,0:T(8,128)(2,1)S(1)} %fusion.3), channel_id=1, source_target_pairs={{0,16},{4,20},{8,24},{12,28},{16,0},{20,4},{24,8},{28,12},{1,17},{... | collective-permute-start | bytes 786440 | tf_op jit(solution)/shard_map/ppermute | solution.py:187
  148.9 15.6 %collective-permute-start.26 = (f16[256,512]{1,0:T(8,128)(2,1)S(1)}, f16[256,512]{1,0:T(8,128)(2,1)S(1)}, u32[]{:S(2)}, u32[]{:S(2)}) collective-permute-start(f16[256,512]{1,0:T(8,128)(2,1)S(1)} %get-tuple-element.35), channel_id=1, source_target_pairs={{1,8},{2,16},{3,24},{5,12},{6,20},{7,28},{8,5},{10,17},{11,25},{12... | collective-permute-start | bytes 786440 | tf_op jit(solution)/shard_map/ppermute | solution.py:308
  (24 other events, 209.5 us)

commit v5 on v4

--- a/solution.py
+++ b/solution.py
@@ -1,3 +1,5 @@
+import functools
+
 import jax
 import jax.numpy as jnp
 from jax import lax
@@ -172,6 +174,38 @@
     )(sums)
 
 
+def center_kernel(chunk, chunks, x_ref, pack_ref, window_ref, out_ref, turned_ref):
+    group = pl.program_id(0)
+    rows = x_ref.shape[1]
+
+    @pl.when(group == 0)
+    def _():
+        turned_ref[...] = pack_ref[...].T
+
+    at = turned_ref[pl.ds(pl.multiple_of((group * chunks + chunk) * rows, 8), rows), :]
+    centered = window_ref[...].astype(F32) * (x_ref[0].astype(F32) - at[:, 0:1])
+    out_ref[0] = (centered.astype(BF16).astype(F32) * at[:, 1:2]).astype(BF16)
+
+
+def center(x, pack, window, chunk, chunks):
+    groups, rows, depth = x.shape
+    return pl.pallas_call(
+        functools.partial(center_kernel, chunk, chunks),
+        grid=(groups,),
+        in_specs=[
+            pl.BlockSpec((1, rows, depth), lambda i: (i, 0, 0)),
+            pl.BlockSpec(pack.shape, lambda i: (0, 0)),
+            pl.BlockSpec((1, depth), lambda i: (0, 0)),
+        ],
+        out_specs=pl.BlockSpec((1, rows, depth), lambda i: (i, 0, 0)),
+        out_shape=jax.ShapeDtypeStruct(x.shape, BF16),
+        scratch_shapes=[pltpu.VMEM((pack.shape[1], 8), F32)],
+        compiler_params=pltpu.CompilerParams(vmem_limit_bytes=16 * 2**20),
+        cost_estimate=pl.CostEstimate(flops=0, bytes_accessed=0, transcendentals=0),
+        name="center",
+    )(x, pack, window)
+
+
 def after(x, *gates):
     return lax.optimization_barrier((x,) + gates)[0] if gates else x
 
@@ -199,18 +233,13 @@
         mean, scale, count = pack[0], pack[1, 0], pack[2, 0]
         weight = frame_window.astype(F32)
 
-        def center(x, mean, scale):
+        def center_far(x, mean, scale):
             centered = (weight * (x.astype(F32) - mean[..., None])).astype(BF16)
             return (centered.astype(F32) * scale).astype(BF16)
 
-        mine = center(coords, mean, scale)
-        packs = {0: pack, 1: swap(pack, "coord", 1)}
-        for d in range(2, n_c, 2):
-            packs[d] = swap(pack, "coord", d)
-            for k in range(1, CHUNKS):
-                raw_far[d, k] = swap(after(raw[:, k], pack), "coord", d)
-            packs[d + 1] = swap(packs[d], "coord", 1)
-
+        mine = center(
+            coords.reshape(m * CHUNKS, rows, depth), pack, frame_window[None, :], 0, 1
+        ).reshape(width, depth)
         flip = (f // m) ^ c
         a = f % m
         top = low - 1
@@ -230,7 +259,7 @@
         def far(k, *gates):
             for d in range(2, n_c, 2):
                 mean_k = packs[d][0].reshape(m, CHUNKS, rows)[:, k]
-                panels[d, k] = center(after(raw_far[d, k], *gates), mean_k, packs[d][1, 0])
+                panels[d, k] = center_far(after(raw_far[d, k], *gates), mean_k, packs[d][1, 0])
             return [panels[d, k] for d in range(2, n_c, 2)]
 
         def far_near(k, *gates):
@@ -359,16 +388,24 @@
         def sends(k, far_pairs):
             return [t.send for t in held[k, far_pairs]]
 
+        diagonal = Diagonal()
+        ye = diagonal.low_steps()
+        first = diagonal.send
+        packs = {0: pack, 1: swap(after(pack, first), "coord", 1)}
+        for d in range(2, n_c, 2):
+            packs[d] = swap(after(pack, first), "coord", d)
+            for k in range(1, CHUNKS):
+                raw_far[d, k] = swap(after(raw[:, k], pack), "coord", d)
+            packs[d + 1] = swap(packs[d], "coord", 1)
+
         row_scale = pack[:, :128]
         for d in range(1, n_c):
             row_scale = jnp.where(flip == d, packs[d][:, :128], row_scale)
         row_scale = row_scale[1:2]
         factor = 1.0 / (row_scale * scale * (count - 1.0))
 
-        near(0)
-        near(1)
-        diagonal = Diagonal()
-        ye = diagonal.low_steps()
+        near(0, first)
+        near(1, first)
         held[0, 0] = tasks(0, False, d_first)
         z00 = d_step(held[0, 0], diagonal.send)
         held[1, 0] = tasks(1, False, low_first)
@@ -387,9 +424,9 @@
         far_near(1)
         held[1, 1] = tasks(1, True, low_first)
 
-        b1 = z01 + y10 + y00 + te + sends(1, 1) + [factor]
+        b1 = z01 + y10 + y00 + [factor]
         y01 = low_steps(held[0, 1], *b1)
-        y11 = low_steps(held[1, 1], *y01)
+        y11 = low_steps(held[1, 1], *(y01 + te))
         z10 = d_step(held[1, 0], *y01)
 
         t0 = top_steps(0, *y01)

time: 168 us -> 163 us (0.970)
  other arithmetic: 20.3 us -> 15.1 us
    ppermute x4, waiting for transfers between devices: 24.8 us -> 28.1 us  [directed(): return lax.ppermute(after(x, *gates), ('frame', 'coord'), pairs)]
    ppermute x23, waiting for transfers between devices: 40.8 us -> 37.9 us  [swap(): lax.ppermute(x, axis, [(i, i ^ bit) for i in range(mesh.shape[axis])])]
    convert_element_type x3 -> x2, other arithmetic: 6.11 us -> 3.18 us  [center_far(): return (centered.astype(F32) * scale).astype(BF16)]
    unnamed x45 -> x41, local copies, waits for them, and re-layouts: 4.83 us -> 5.77 us
  transfers between devices with their start and end apart: 27 -> 27, of which waited for: 13 -> 15; matrix products, arithmetic and copies ran while one was open for 14% -> 11% of each run, Pallas kernels for 9% -> 11%
where the time goes in v5:
time: 163 us
  waiting for transfers between devices  66 us (40%)
  starting transfers between devices  36 us (22%)
  Pallas kernels  32.9 us (20%)
  other arithmetic  15.1 us (9%)
  local copies, waits for them, and re-layouts  10.9 us (7%)
  between operations  1.78 us (1%)
    ppermute x23, waiting for transfers between devices, swap(): lax.ppermute(x, axis, [(i, i ^ bit) for i in range(mesh.shape[axis])])  37.9 us
    ppermute x4, waiting for transfers between devices, directed(): return lax.ppermute(after(x, *gates), ('frame', 'coord'), pairs)  28.1 us
    ppermute x23, starting transfers between devices, swap(): lax.ppermute(x, axis, [(i, i ^ bit) for i in range(mesh.shape[axis])])  25.2 us
    pallas_call x5, Pallas kernels, gram(): pl.pallas_call(gram_kernel, grid_spec=pltpu.PrefetchScalarGridSpec(num_sc...  14.3 us
    pallas_call x1, Pallas kernels, project(): pl.pallas_call(project_kernel, grid=(rows // tile,), in_specs=[pl.BlockSp...  13.5 us
    ppermute x4, starting transfers between devices, directed(): return lax.ppermute(after(x, *gates), ('frame', 'coord'), pairs)  10.8 us
    unnamed x41, local copies, waits for them, and re-layouts  5.77 us
  transfers between devices with their start and end apart: 27, of which 15 were waited for; matrix products, arithmetic and copies ran while one was open for 11% of the time, Pallas kernels for 11%

profile of v5, /device:TPU:2, one launch (start us, length us, event | category | flops | bytes accessed | tf_op | source)
XLA Modules:
  0.0 162.7 jit_solution(7930325322227310345)
XLA Ops:
  3.3 13.5 %project.1 = (bf16[1024,1024]{1,0:T(8,128)(2,1)S(1)}, f32[8,1024]{1,0:T(8,128)S(1)}) custom-call(s32[16,8]{1,0:T(8,128)S(1)} %copy.8.cols_ref, bf16[1024,4224]{1,0:T(8,128)(2,1)} %frames_ref.1, bf16[1024,512]{1,0:T(8,128)(2,1)S(1)} %copy-done.9, s32[1,1024]{1,0:T(1,128)S(1)} %bitcast.72), custom_call_target="tpu_custom_call" | custom-call | flops 8858370048 | bytes 10747904 | tf_op jit(solution)/shard_map/project/pallas_call | solution.py:46
  22.5 2.3 %collective-permute-done.1 = f32[8,1024]{1,0:T(8,128)S(1)} collective-permute-done((f32[8,1024]{1,0:T(8,128)S(1)}, f32[8,1024]{1,0:T(8,128)S(1)}, u32[]{:S(2)}, u32[]{:S(2)}) %collective-permute-start.1) | collective-permute-done | bytes 32800 | tf_op jit(solution)/shard_map/ppermute | solution.py:221
  24.8 2.6 %collective-permute-start.2 = (f32[8,1024]{1,0:T(8,128)S(1)}, f32[8,1024]{1,0:T(8,128)S(1)}, u32[]{:S(2)}, u32[]{:S(2)}) collective-permute-start(f32[8,1024]{1,0:T(8,128)S(1)} %add.67), channel_id=1, source_target_pairs={{0,16},{4,20},{8,24},{12,28},{16,0},{20,4},{24,8},{28,12},{1,17},{... | collective-permute-start | bytes 98312 | tf_op jit(solution)/shard_map/ppermute | solution.py:221
  27.5 2.1 %collective-permute-done.2 = f32[8,1024]{1,0:T(8,128)S(1)} collective-permute-done((f32[8,1024]{1,0:T(8,128)S(1)}, f32[8,1024]{1,0:T(8,128)S(1)}, u32[]{:S(2)}, u32[]{:S(2)}) %collective-permute-start.2) | collective-permute-done | bytes 32800 | tf_op jit(solution)/shard_map/ppermute | solution.py:221
  36.7 2.1 %gram.5 = f32[2,512,512]{2,1,0:T(8,128)S(1)} custom-call(s32[2]{0:T(128)S(1)} %broadcast_1_which_ref.2.which_ref, s32[2]{0:T(128)S(1)} %get-tuple-element.53.group_ref, s32[2]{0:T(128)S(1)} %get-tuple-element.54.half_ref, bf16[2,512,1024]{2,1,0:T(8,128)(2,1)S(1)} %bitcast.63, bf16[2,512,1024]{2,1,0:T(8,128)(2,1)S(1)} %bitcast.64, bf16[1024,1024]{1,0:T(8,128)(2,1)S(1)} %bitcast.62), custom_call_target="tpu_custom_call" | custom-call | tf_op jit(solution)/shard_map/gram/pallas_call | solution.py:93
  47.9 2.2 %multiply_convert_fusion.2.first_ref = bf16[2,256,1024]{2,1,0:T(8,128)(2,1)S(1)} fusion(bf16[2,256,1024]{2,1,0:T(8,128)(2,1)} %collective-permute-done.3, f32[]{:T(128)} %bitcast.20, f32[2,256]{1,0:T(2,128)S(1)} %bitcast.77, f32[1024]{0:T(1024)S(1)} %convert_element_type.140), kind=kLoop, calls=%fused_computation.2 | loop fusion | flops 3670016 | bytes 2103300 | tf_op jit(solution)/shard_map/convert_element_type | solution.py:238
  50.2 4.6 %gram.7 = f32[4,256,512]{2,1,0:T(8,128)S(1)} custom-call(s32[4]{0:T(128)S(1)} %get-tuple-element.55.which_ref, s32[4]{0:T(128)S(1)} %get-tuple-element.56.group_ref, s32[4]{0:T(128)S(1)} %add_add_fusion.3.half_ref, bf16[2,256,1024]{2,1,0:T(8,128)(2,1)} %get-tuple-element.25.first_ref, bf16[2,256,1024]{2,1,0:T(8,128)(2,1)} %collective-permute-done.7.second_ref, ...), custom_call_target="tpu_custom_call" | custom-call | tf_op jit(solution)/shard_map/gram/pallas_call | solution.py:93
  57.9 2.5 %gram.8 = f32[4,256,512]{2,1,0:T(8,128)S(1)} custom-call(s32[4]{0:T(128)S(1)} %get-tuple-element.57.which_ref, s32[4]{0:T(128)S(1)} %get-tuple-element.58.group_ref, s32[4]{0:T(128)S(1)} %add_add_fusion.6.half_ref, bf16[2,256,1024]{2,1,0:T(8,128)(2,1)S(1)} %get-tuple-element.27.first_ref, bf16[2,256,1024]{2,1,0:T(8,128)(2,1)S(1)} %collective-permute-done.9.second_ref, ...), custom_call_target="tpu_custom_call" | custom-call | tf_op jit(solution)/shard_map/gram/pallas_call | solution.py:93
  62.6 6.7 %collective-permute-done.8 = f16[2,256,512]{2,1,0:T(8,128)(2,1)S(1)} collective-permute-done((f16[2,256,512]{2,1,0:T(8,128)(2,1)S(1)}, f16[2,256,512]{2,1,0:T(8,128)(2,1)S(1)}, u32[]{:S(2)}, u32[]{:S(2)}) %collective-permute-start.8) | collective-permute-done | bytes 524320 | tf_op jit(solution)/shard_map/ppermute | solution.py:221
  69.5 2.5 %gram.6 = f32[4,256,512]{2,1,0:T(8,128)S(1)} custom-call(s32[4]{0:T(128)S(1)} %get-tuple-element.55.which_ref, s32[4]{0:T(128)S(1)} %get-tuple-element.56.group_ref, s32[4]{0:T(128)S(1)} %add_add_fusion.2.half_ref, bf16[2,256,1024]{2,1,0:T(8,128)(2,1)S(1)} %multiply_convert_fusion.2.first_ref, bf16[2,256,1024]{2,1,0:T(8,128)(2,1)S(1)} %collective-permute-done.5.second_ref, ...), custom_call_target="tpu_custom_call" | custom-call | tf_op jit(solution)/shard_map/gram/pallas_call | solution.py:93
  77.7 4.7 %collective-permute-start.20 = (f16[1,512,512]{2,1,0:T(8,128)(2,1)S(1)}, f16[1,512,512]{2,1,0:T(8,128)(2,1)S(1)}, u32[]{:S(2)}, u32[]{:S(2)}) collective-permute-start(f16[1,512,512]{2,1,0:T(8,128)(2,1)S(1)} %fusion), channel_id=1, source_target_pairs={{2,18},{6,22},{11,27},{15,31},{16,0},{20,4},{25,9},{29,13}} | collective-permute-start | bytes 1572872 | tf_op jit(solution)/shard_map/ppermute | solution.py:337
  82.4 3.8 %collective-permute-done.10 = f16[2,256,512]{2,1,0:T(8,128)(2,1)S(1)} collective-permute-done((f16[2,256,512]{2,1,0:T(8,128)(2,1)S(1)}, f16[2,256,512]{2,1,0:T(8,128)(2,1)S(1)}, u32[]{:S(2)}, u32[]{:S(2)}) %collective-permute-start.10) | collective-permute-done | bytes 524320 | tf_op jit(solution)/shard_map/ppermute | solution.py:221
  87.2 2.5 %gram.9 = f32[4,256,512]{2,1,0:T(8,128)S(1)} custom-call(s32[4]{0:T(128)S(1)} %get-tuple-element.57.which_ref, s32[4]{0:T(128)S(1)} %get-tuple-element.58.group_ref, s32[4]{0:T(128)S(1)} %add_add_fusion.7.half_ref, bf16[2,256,1024]{2,1,0:T(8,128)(2,1)S(1)} %multiply_convert_fusion.first_ref, bf16[2,256,1024]{2,1,0:T(8,128)(2,1)S(1)} %collective-permute-done.18.second_ref, ...), custom_call_target="tpu_custom_call" | custom-call | tf_op jit(solution)/shard_map/gram/pallas_call | solution.py:93
  90.9 3.0 %collective-permute-done.15 = f16[1,256,512]{2,1,0:T(8,128)(2,1)S(1)} collective-permute-done((f16[1,256,512]{2,1,0:T(8,128)(2,1)S(1)}, f16[1,256,512]{2,1,0:T(8,128)(2,1)S(1)}, u32[]{:S(2)}, u32[]{:S(2)}) %collective-permute-start.15) | collective-permute-done | bytes 262176 | tf_op jit(solution)/shard_map/ppermute | solution.py:221
  95.1 4.8 %collective-permute-start.16 = (f16[256,512]{1,0:T(8,128)(2,1)S(1)}, f16[256,512]{1,0:T(8,128)(2,1)S(1)}, u32[]{:S(2)}, u32[]{:S(2)}) collective-permute-start(f16[256,512]{1,0:T(8,128)(2,1)S(1)} %fusion.2), channel_id=1, source_target_pairs={{0,16},{4,20},{8,24},{12,28},{16,0},{20,4},{24,8},{28,12},{1,17},{... | collective-permute-start | bytes 786440 | tf_op jit(solution)/shard_map/ppermute | solution.py:221
  99.9 2.5 %collective-permute-start.22 = (f16[1,256,512]{2,1,0:T(8,128)(2,1)S(1)}, f16[1,256,512]{2,1,0:T(8,128)(2,1)S(1)}, u32[]{:S(2)}, u32[]{:S(2)}) collective-permute-start(f16[1,256,512]{2,1,0:T(8,128)(2,1)S(1)} %slice_convert_fusion.5), channel_id=1, source_target_pairs={{0,8},{4,12},{8,0},{12,4},{16,24},{20,28},{24,16},{28,20},{1,9},{5... | collective-permute-start | bytes 786440 | tf_op jit(solution)/shard_map/ppermute | solution.py:221
  102.4 3.7 %collective-permute-done.21 = f16[2,256,512]{2,1,0:T(8,128)(2,1)S(1)} collective-permute-done((f16[2,256,512]{2,1,0:T(8,128)(2,1)S(1)}, f16[2,256,512]{2,1,0:T(8,128)(2,1)S(1)}, u32[]{:S(2)}, u32[]{:S(2)}) %collective-permute-start.21) | collective-permute-done | bytes 524320 | tf_op jit(solution)/shard_map/ppermute | solution.py:221
  106.4 3.6 %collective-permute-done.16 = f16[256,512]{1,0:T(8,128)(2,1)S(1)} collective-permute-done((f16[256,512]{1,0:T(8,128)(2,1)S(1)}, f16[256,512]{1,0:T(8,128)(2,1)S(1)}, u32[]{:S(2)}, u32[]{:S(2)}) %collective-permute-start.16) | collective-permute-done | bytes 262176 | tf_op jit(solution)/shard_map/ppermute | solution.py:221
  112.7 2.8 %collective-permute-start.24 = (f16[256,512]{1,0:T(8,128)(2,1)S(1)}, f16[256,512]{1,0:T(8,128)(2,1)S(1)}, u32[]{:S(2)}, u32[]{:S(2)}) collective-permute-start(f16[256,512]{1,0:T(8,128)(2,1)S(1)} %get-tuple-element.43), channel_id=1, source_target_pairs={{1,8},{2,16},{3,24},{5,12},{6,20},{7,28},{8,5},{10,17},{11,25},{12... | collective-permute-start | bytes 786440 | tf_op jit(solution)/shard_map/ppermute | solution.py:337
  117.4 12.4 %collective-permute-done.24 = f16[256,512]{1,0:T(8,128)(2,1)S(1)} collective-permute-done((f16[256,512]{1,0:T(8,128)(2,1)S(1)}, f16[256,512]{1,0:T(8,128)(2,1)S(1)}, u32[]{:S(2)}, u32[]{:S(2)}) %collective-permute-start.24) | collective-permute-done | bytes 262176 | tf_op jit(solution)/shard_map/ppermute | solution.py:337
  131.2 9.5 %collective-permute-done.25 = f16[256,512]{1,0:T(8,128)(2,1)} collective-permute-done((f16[256,512]{1,0:T(8,128)(2,1)}, f16[256,512]{1,0:T(8,128)(2,1)}, u32[]{:S(2)}, u32[]{:S(2)}) %collective-permute-start.25) | collective-permute-done | bytes 262176 | tf_op jit(solution)/shard_map/ppermute | solution.py:221
  142.1 2.1 %collective-permute-start.26 = (f16[256,512]{1,0:T(8,128)(2,1)S(1)}, f16[256,512]{1,0:T(8,128)(2,1)S(1)}, u32[]{:S(2)}, u32[]{:S(2)}) collective-permute-start(f16[256,512]{1,0:T(8,128)(2,1)S(1)} %get-tuple-element.41), channel_id=1, source_target_pairs={{1,8},{2,16},{3,24},{5,12},{6,20},{7,28},{8,5},{10,17},{11,25},{12... | collective-permute-start | bytes 786440 | tf_op jit(solution)/shard_map/ppermute | solution.py:337
  145.6 14.6 %collective-permute-done.26 = f16[256,512]{1,0:T(8,128)(2,1)S(1)} collective-permute-done((f16[256,512]{1,0:T(8,128)(2,1)S(1)}, f16[256,512]{1,0:T(8,128)(2,1)S(1)}, u32[]{:S(2)}, u32[]{:S(2)}) %collective-permute-start.26) | collective-permute-done | bytes 262176 | tf_op jit(solution)/shard_map/ppermute | solution.py:337
  160.3 2.4 %assemble.1 = f32[512,1024]{1,0:T(8,128)} custom-call(s32[3]{0:T(128)S(1)} %pad_add_fusion.flags_ref, f32[512,512]{1,0:T(8,128)S(1)} %pad_maximum_fusion.direct_ref, f32[1,512,512]{2,1,0:T(8,128)S(1)} %maximum_convert_fusion.mirror_ref, f32[512,512]{1,0:T(8,128)S(1)} %add_bitcast_fusion.diagonal_ref, f32[1,128]{1,0:T(1,128)S(1)} %multiply_divide_fusion.factor_ref), custom_call_target="tpu_custom_call" | custom-call | tf_op jit(solution)/shard_map/assemble/pallas_call | solution.py:144
  (127 shorter events, 47.4 us)
Async XLA Ops:
  19.9 28.0 %collective-permute-start.3 = (bf16[2,256,1024]{2,1,0:T(8,128)(2,1)}, bf16[2,256,1024]{2,1,0:T(8,128)(2,1)}, u32[]{:S(2)}, u32[]{:S(2)}) collective-permute-start(bf16[2,256,1024]{2,1,0:T(8,128)(2,1)} %get-tuple-element.45), channel_id=1, source_target_pairs={{0,2},{1,3},{2,0},{3,1},{4,6},{5,7},{6,4},{7,5},{8,10},{9,11},{10,... | collective-permute-start | bytes 3145736 | tf_op jit(solution)/shard_map/ppermute | solution.py:221
  24.8 4.8 %collective-permute-start.2 = (f32[8,1024]{1,0:T(8,128)S(1)}, f32[8,1024]{1,0:T(8,128)S(1)}, u32[]{:S(2)}, u32[]{:S(2)}) collective-permute-start(f32[8,1024]{1,0:T(8,128)S(1)} %add.67), channel_id=1, source_target_pairs={{0,16},{4,20},{8,24},{12,28},{16,0},{20,4},{24,8},{28,12},{1,17},{... | collective-permute-start | bytes 98312 | tf_op jit(solution)/shard_map/ppermute | solution.py:221
  39.8 6.3 %collective-permute-start.14 = (f32[8,1024]{1,0:T(8,128)S(1)}, f32[8,1024]{1,0:T(8,128)S(1)}, u32[]{:S(2)}, u32[]{:S(2)}) collective-permute-start(f32[8,1024]{1,0:T(8,128)S(1)} %copy-done.6), channel_id=1, source_target_pairs={{0,1},{1,0},{2,3},{3,2},{4,5},{5,4},{6,7},{7,6},{8,9},{9,8},{10,11... | collective-permute-start | bytes 98312 | tf_op jit(solution)/shard_map/ppermute | solution.py:221
  39.8 5.6 %collective-permute-start.4 = (f32[8,1024]{1,0:T(8,128)S(1)}, f32[8,1024]{1,0:T(8,128)S(1)}, u32[]{:S(2)}, u32[]{:S(2)}) collective-permute-start(f32[8,1024]{1,0:T(8,128)S(1)} %copy-done.6), channel_id=1, source_target_pairs={{0,2},{1,3},{2,0},{3,1},{4,6},{5,7},{6,4},{7,5},{8,10},{9,11},{10,... | collective-permute-start | bytes 98312 | tf_op jit(solution)/shard_map/ppermute | solution.py:221
  41.3 15.3 %collective-permute-start.6 = (f16[1,512,512]{2,1,0:T(8,128)(2,1)}, f16[1,512,512]{2,1,0:T(8,128)(2,1)}, u32[]{:S(2)}, u32[]{:S(2)}) collective-permute-start(f16[1,512,512]{2,1,0:T(8,128)(2,1)} %slice_convert_fusion.4), channel_id=1, source_target_pairs={{0,4},{4,0},{8,12},{12,8},{16,20},{20,16},{24,28},{28,24},{1,5},{5... | collective-permute-start | bytes 1572872 | tf_op jit(solution)/shard_map/ppermute | solution.py:221
  43.0 7.2 %collective-permute-start.7 = (bf16[2,256,1024]{2,1,0:T(8,128)(2,1)}, bf16[2,256,1024]{2,1,0:T(8,128)(2,1)}, u32[]{:S(2)}, u32[]{:S(2)}) collective-permute-start(bf16[2,256,1024]{2,1,0:T(8,128)(2,1)} %get-tuple-element.25.first_ref), channel_id=1, source_target_pairs={{0,1},{1,0},{2,3},{3,2},{4,5},{5,4},{6,7},{7,6},{8,9},{9,8},{10,11... | collective-permute-start | bytes 3145736 | tf_op jit(solution)/shard_map/ppermute | solution.py:221
  46.1 11.7 %collective-permute-start.9 = (bf16[2,256,1024]{2,1,0:T(8,128)(2,1)S(1)}, bf16[2,256,1024]{2,1,0:T(8,128)(2,1)S(1)}, u32[]{:S(2)}, u32[]{:S(2)}) collective-permute-start(bf16[2,256,1024]{2,1,0:T(8,128)(2,1)S(1)} %get-tuple-element.27.first_ref), channel_id=1, source_target_pairs={{0,1},{1,0},{2,3},{3,2},{4,5},{5,4},{6,7},{7,6},{8,9},{9,8},{10,11... | collective-permute-start | bytes 3145736 | tf_op jit(solution)/shard_map/ppermute | solution.py:221
  46.7 25.4 %collective-permute-start.17 = (bf16[2,256,1024]{2,1,0:T(8,128)(2,1)}, bf16[2,256,1024]{2,1,0:T(8,128)(2,1)S(1)}, u32[]{:S(2)}, u32[]{:S(2)}) collective-permute-start(bf16[2,256,1024]{2,1,0:T(8,128)(2,1)} %get-tuple-element.33), channel_id=1, source_target_pairs={{0,2},{1,3},{2,0},{3,1},{4,6},{5,7},{6,4},{7,5},{8,10},{9,11},{10,... | collective-permute-start | bytes 3145736 | tf_op jit(solution)/shard_map/ppermute | solution.py:221
  50.1 19.4 %collective-permute-start.5 = (bf16[2,256,1024]{2,1,0:T(8,128)(2,1)S(1)}, bf16[2,256,1024]{2,1,0:T(8,128)(2,1)S(1)}, u32[]{:S(2)}, u32[]{:S(2)}) collective-permute-start(bf16[2,256,1024]{2,1,0:T(8,128)(2,1)S(1)} %multiply_convert_fusion.2.first_ref), channel_id=1, source_target_pairs={{0,1},{1,0},{2,3},{3,2},{4,5},{5,4},{6,7},{7,6},{8,9},{9,8},{10,11... | collective-permute-start | bytes 3145736 | tf_op jit(solution)/shard_map/ppermute | solution.py:221
  55.0 14.4 %collective-permute-start.8 = (f16[2,256,512]{2,1,0:T(8,128)(2,1)S(1)}, f16[2,256,512]{2,1,0:T(8,128)(2,1)S(1)}, u32[]{:S(2)}, u32[]{:S(2)}) collective-permute-start(f16[2,256,512]{2,1,0:T(8,128)(2,1)S(1)} %slice_convert_fusion.2), channel_id=1, source_target_pairs={{0,8},{4,12},{8,0},{12,4},{16,24},{20,28},{24,16},{28,20},{1,9},{5... | collective-permute-start | bytes 1572872 | tf_op jit(solution)/shard_map/ppermute | solution.py:221
  60.5 25.9 %collective-permute-start.11 = (f16[2,256,512]{2,1,0:T(8,128)(2,1)S(1)}, f16[2,256,512]{2,1,0:T(8,128)(2,1)S(1)}, u32[]{:S(2)}, u32[]{:S(2)}) collective-permute-start(f16[2,256,512]{2,1,0:T(8,128)(2,1)S(1)} %slice_convert_fusion.1), channel_id=1, source_target_pairs={{0,4},{4,0},{8,12},{12,8},{16,20},{20,16},{24,28},{28,24},{1,5},{5... | collective-permute-start | bytes 1572872 | tf_op jit(solution)/shard_map/ppermute | solution.py:221
  61.3 14.0 %collective-permute-start.19 = (f16[1,512,512]{2,1,0:T(8,128)(2,1)S(1)}, f16[1,512,512]{2,1,0:T(8,128)(2,1)S(1)}, u32[]{:S(2)}, u32[]{:S(2)}) collective-permute-start(f16[1,512,512]{2,1,0:T(8,128)(2,1)S(1)} %fusion.1), channel_id=1, source_target_pairs={{1,9},{3,11},{5,13},{7,15},{8,0},{10,2},{12,4},{14,6},{17,25},{19,... | collective-permute-start | bytes 1572872 | tf_op jit(solution)/shard_map/ppermute | solution.py:337
  72.2 14.0 %collective-permute-start.10 = (f16[2,256,512]{2,1,0:T(8,128)(2,1)S(1)}, f16[2,256,512]{2,1,0:T(8,128)(2,1)S(1)}, u32[]{:S(2)}, u32[]{:S(2)}) collective-permute-start(f16[2,256,512]{2,1,0:T(8,128)(2,1)S(1)} %slice_convert_fusion.3), channel_id=1, source_target_pairs={{0,8},{4,12},{8,0},{12,4},{16,24},{20,28},{24,16},{28,20},{1,9},{5... | collective-permute-start | bytes 1572872 | tf_op jit(solution)/shard_map/ppermute | solution.py:221
  75.2 12.0 %collective-permute-start.18 = (bf16[2,256,1024]{2,1,0:T(8,128)(2,1)S(1)}, bf16[2,256,1024]{2,1,0:T(8,128)(2,1)S(1)}, u32[]{:S(2)}, u32[]{:S(2)}) collective-permute-start(bf16[2,256,1024]{2,1,0:T(8,128)(2,1)S(1)} %multiply_convert_fusion.first_ref), channel_id=1, source_target_pairs={{0,1},{1,0},{2,3},{3,2},{4,5},{5,4},{6,7},{7,6},{8,9},{9,8},{10,11... | collective-permute-start | bytes 3145736 | tf_op jit(solution)/shard_map/ppermute | solution.py:221
  76.9 9.6 %collective-permute-start.12 = (f16[1,256,512]{2,1,0:T(8,128)(2,1)S(1)}, f16[1,256,512]{2,1,0:T(8,128)(2,1)S(1)}, u32[]{:S(2)}, u32[]{:S(2)}) collective-permute-start(f16[1,256,512]{2,1,0:T(8,128)(2,1)S(1)} %slice_convert_fusion.7), channel_id=1, source_target_pairs={{0,4},{4,0},{8,12},{12,8},{16,20},{20,16},{24,28},{28,24},{1,5},{5... | collective-permute-start | bytes 786440 | tf_op jit(solution)/shard_map/ppermute | solution.py:221
  77.7 13.3 %collective-permute-start.20 = (f16[1,512,512]{2,1,0:T(8,128)(2,1)S(1)}, f16[1,512,512]{2,1,0:T(8,128)(2,1)S(1)}, u32[]{:S(2)}, u32[]{:S(2)}) collective-permute-start(f16[1,512,512]{2,1,0:T(8,128)(2,1)S(1)} %fusion), channel_id=1, source_target_pairs={{2,18},{6,22},{11,27},{15,31},{16,0},{20,4},{25,9},{29,13}} | collective-permute-start | bytes 1572872 | tf_op jit(solution)/shard_map/ppermute | solution.py:337
  86.5 7.5 %collective-permute-start.15 = (f16[1,256,512]{2,1,0:T(8,128)(2,1)S(1)}, f16[1,256,512]{2,1,0:T(8,128)(2,1)S(1)}, u32[]{:S(2)}, u32[]{:S(2)}) collective-permute-start(f16[1,256,512]{2,1,0:T(8,128)(2,1)S(1)} %slice_convert_fusion.8), channel_id=1, source_target_pairs={{0,4},{4,0},{8,12},{12,8},{16,20},{20,16},{24,28},{28,24},{1,5},{5... | collective-permute-start | bytes 786440 | tf_op jit(solution)/shard_map/ppermute | solution.py:221
  94.0 12.1 %collective-permute-start.21 = (f16[2,256,512]{2,1,0:T(8,128)(2,1)S(1)}, f16[2,256,512]{2,1,0:T(8,128)(2,1)S(1)}, u32[]{:S(2)}, u32[]{:S(2)}) collective-permute-start(f16[2,256,512]{2,1,0:T(8,128)(2,1)S(1)} %slice_convert_fusion), channel_id=1, source_target_pairs={{0,4},{4,0},{8,12},{12,8},{16,20},{20,16},{24,28},{28,24},{1,5},{5... | collective-permute-start | bytes 1572872 | tf_op jit(solution)/shard_map/ppermute | solution.py:221
  95.1 14.9 %collective-permute-start.16 = (f16[256,512]{1,0:T(8,128)(2,1)S(1)}, f16[256,512]{1,0:T(8,128)(2,1)S(1)}, u32[]{:S(2)}, u32[]{:S(2)}) collective-permute-start(f16[256,512]{1,0:T(8,128)(2,1)S(1)} %fusion.2), channel_id=1, source_target_pairs={{0,16},{4,20},{8,24},{12,28},{16,0},{20,4},{24,8},{28,12},{1,17},{... | collective-permute-start | bytes 786440 | tf_op jit(solution)/shard_map/ppermute | solution.py:221
  99.9 10.2 %collective-permute-start.22 = (f16[1,256,512]{2,1,0:T(8,128)(2,1)S(1)}, f16[1,256,512]{2,1,0:T(8,128)(2,1)S(1)}, u32[]{:S(2)}, u32[]{:S(2)}) collective-permute-start(f16[1,256,512]{2,1,0:T(8,128)(2,1)S(1)} %slice_convert_fusion.5), channel_id=1, source_target_pairs={{0,8},{4,12},{8,0},{12,4},{16,24},{20,28},{24,16},{28,20},{1,9},{5... | collective-permute-start | bytes 786440 | tf_op jit(solution)/shard_map/ppermute | solution.py:221
  110.1 6.4 %collective-permute-start.23 = (f16[1,256,512]{2,1,0:T(8,128)(2,1)S(1)}, f16[1,256,512]{2,1,0:T(8,128)(2,1)S(1)}, u32[]{:S(2)}, u32[]{:S(2)}) collective-permute-start(f16[1,256,512]{2,1,0:T(8,128)(2,1)S(1)} %slice_convert_fusion.6), channel_id=1, source_target_pairs={{0,8},{4,12},{8,0},{12,4},{16,24},{20,28},{24,16},{28,20},{1,9},{5... | collective-permute-start | bytes 786440 | tf_op jit(solution)/shard_map/ppermute | solution.py:221
  112.7 17.1 %collective-permute-start.24 = (f16[256,512]{1,0:T(8,128)(2,1)S(1)}, f16[256,512]{1,0:T(8,128)(2,1)S(1)}, u32[]{:S(2)}, u32[]{:S(2)}) collective-permute-start(f16[256,512]{1,0:T(8,128)(2,1)S(1)} %get-tuple-element.43), channel_id=1, source_target_pairs={{1,8},{2,16},{3,24},{5,12},{6,20},{7,28},{8,5},{10,17},{11,25},{12... | collective-permute-start | bytes 786440 | tf_op jit(solution)/shard_map/ppermute | solution.py:337
  130.5 10.1 %collective-permute-start.25 = (f16[256,512]{1,0:T(8,128)(2,1)}, f16[256,512]{1,0:T(8,128)(2,1)}, u32[]{:S(2)}, u32[]{:S(2)}) collective-permute-start(f16[256,512]{1,0:T(8,128)(2,1)} %fusion.3), channel_id=1, source_target_pairs={{0,16},{4,20},{8,24},{12,28},{16,0},{20,4},{24,8},{28,12},{1,17},{... | collective-permute-start | bytes 786440 | tf_op jit(solution)/shard_map/ppermute | solution.py:221
  142.1 18.1 %collective-permute-start.26 = (f16[256,512]{1,0:T(8,128)(2,1)S(1)}, f16[256,512]{1,0:T(8,128)(2,1)S(1)}, u32[]{:S(2)}, u32[]{:S(2)}) collective-permute-start(f16[256,512]{1,0:T(8,128)(2,1)S(1)} %get-tuple-element.41), channel_id=1, source_target_pairs={{1,8},{2,16},{3,24},{5,12},{6,20},{7,28},{8,5},{10,17},{11,25},{12... | collective-permute-start | bytes 786440 | tf_op jit(solution)/shard_map/ppermute | solution.py:337
  (22 other events, 160.0 us)

commit v6 on v5

--- a/solution.py
+++ b/solution.py
@@ -434,7 +434,7 @@
         b3 = y11 + [t0] + z10
         z11 = d_step(held[1, 1], *b3)
         m0 = mirror(0)
-        top_steps(1, *(z11 + m0))
+        top_steps(1, *z11)
         mirror(1)
 
         direct = jnp.concatenate([done[k] for k in range(CHUNKS)])

time: 163 us -> 160 us (0.982)
  waiting for transfers between devices: 66 us -> 47.5 us
  starting transfers between devices: 36 us -> 48.6 us
    ppermute x4, waiting for transfers between devices: 28.1 us -> 13.3 us  [directed(): return lax.ppermute(after(x, *gates), ('frame', 'coord'), pairs)]
    ppermute x4, starting transfers between devices: 10.8 us -> 20.5 us  [directed(): return lax.ppermute(after(x, *gates), ('frame', 'coord'), pairs)]
    ppermute x23, waiting for transfers between devices: 37.9 us -> 34.3 us  [swap(): lax.ppermute(x, axis, [(i, i ^ bit) for i in range(mesh.shape[axis])])]
    ppermute x23, starting transfers between devices: 25.2 us -> 28.1 us  [swap(): lax.ppermute(x, axis, [(i, i ^ bit) for i in range(mesh.shape[axis])])]
    unnamed x41 -> x43, local copies, waits for them, and re-layouts: 5.77 us -> 6.54 us
  transfers between devices with their start and end apart: 27 -> 27, of which waited for: 15 -> 15; matrix products, arithmetic and copies ran while one was open for 11% -> 13% of each run, Pallas kernels for 11% -> 11%
where the time goes in v6:
time: 160 us; the launch traced here: 159 us
  starting transfers between devices  48.6 us (30%)
  waiting for transfers between devices  47.5 us (30%)
  Pallas kernels  32.9 us (21%)
  other arithmetic  16.5 us (10%)
  local copies, waits for them, and re-layouts  11.7 us (7%)
  between operations  1.81 us (1%)
    ppermute x23, waiting for transfers between devices, swap(): lax.ppermute(x, axis, [(i, i ^ bit) for i in range(mesh.shape[axis])])  34.3 us
    ppermute x23, starting transfers between devices, swap(): lax.ppermute(x, axis, [(i, i ^ bit) for i in range(mesh.shape[axis])])  28.1 us
    ppermute x4, starting transfers between devices, directed(): return lax.ppermute(after(x, *gates), ('frame', 'coord'), pairs)  20.5 us
    pallas_call x5, Pallas kernels, gram(): pl.pallas_call(gram_kernel, grid_spec=pltpu.PrefetchScalarGridSpec(num_sc...  14.3 us
    pallas_call x1, Pallas kernels, project(): pl.pallas_call(project_kernel, grid=(rows // tile,), in_specs=[pl.BlockSp...  13.5 us
    ppermute x4, waiting for transfers between devices, directed(): return lax.ppermute(after(x, *gates), ('frame', 'coord'), pairs)  13.3 us
    unnamed x43, local copies, waits for them, and re-layouts  6.54 us
    convert_element_type x2, other arithmetic, center_far(): return (centered.astype(F32) * scale).astype(BF16)  3.32 us
  transfers between devices with their start and end apart: 27, of which 15 were waited for; matrix products, arithmetic and copies ran while one was open for 13% of the time, Pallas kernels for 11%

profile of v6, /device:TPU:2, one launch (start us, length us, event | category | flops | bytes accessed | tf_op | source)
XLA Modules:
  0.0 159.1 jit_solution(4665446193178454246)
XLA Ops:
  3.3 13.5 %project.1 = (bf16[1024,1024]{1,0:T(8,128)(2,1)S(1)}, f32[8,1024]{1,0:T(8,128)S(1)}) custom-call(s32[16,8]{1,0:T(8,128)S(1)} %copy.8.cols_ref, bf16[1024,4224]{1,0:T(8,128)(2,1)} %frames_ref.1, bf16[1024,512]{1,0:T(8,128)(2,1)S(1)} %copy-done.9, s32[1,1024]{1,0:T(1,128)S(1)} %bitcast.72), custom_call_target="tpu_custom_call" | custom-call | flops 8858370048 | bytes 10747904 | tf_op jit(solution)/shard_map/project/pallas_call | solution.py:46
  22.5 2.3 %collective-permute-done.1 = f32[8,1024]{1,0:T(8,128)S(1)} collective-permute-done((f32[8,1024]{1,0:T(8,128)S(1)}, f32[8,1024]{1,0:T(8,128)S(1)}, u32[]{:S(2)}, u32[]{:S(2)}) %collective-permute-start.1) | collective-permute-done | bytes 32800 | tf_op jit(solution)/shard_map/ppermute | solution.py:221
  24.8 2.6 %collective-permute-start.2 = (f32[8,1024]{1,0:T(8,128)S(1)}, f32[8,1024]{1,0:T(8,128)S(1)}, u32[]{:S(2)}, u32[]{:S(2)}) collective-permute-start(f32[8,1024]{1,0:T(8,128)S(1)} %add.67), channel_id=1, source_target_pairs={{0,16},{4,20},{8,24},{12,28},{16,0},{20,4},{24,8},{28,12},{1,17},{... | collective-permute-start | bytes 98312 | tf_op jit(solution)/shard_map/ppermute | solution.py:221
  27.5 2.1 %collective-permute-done.2 = f32[8,1024]{1,0:T(8,128)S(1)} collective-permute-done((f32[8,1024]{1,0:T(8,128)S(1)}, f32[8,1024]{1,0:T(8,128)S(1)}, u32[]{:S(2)}, u32[]{:S(2)}) %collective-permute-start.2) | collective-permute-done | bytes 32800 | tf_op jit(solution)/shard_map/ppermute | solution.py:221
  47.9 2.3 %multiply_convert_fusion.2.first_ref = bf16[2,256,1024]{2,1,0:T(8,128)(2,1)S(1)} fusion(bf16[2,256,1024]{2,1,0:T(8,128)(2,1)} %collective-permute-done.3, f32[]{:T(128)} %bitcast.20, f32[2,256]{1,0:T(2,128)S(1)} %bitcast.77, f32[1024]{0:T(1024)S(1)} %convert_element_type.140), kind=kLoop, calls=%fused_computation.2 | loop fusion | flops 3670016 | bytes 2103300 | tf_op jit(solution)/shard_map/convert_element_type | solution.py:238
  50.3 4.6 %gram.7 = f32[4,256,512]{2,1,0:T(8,128)S(1)} custom-call(s32[4]{0:T(128)S(1)} %get-tuple-element.55.which_ref, s32[4]{0:T(128)S(1)} %get-tuple-element.56.group_ref, s32[4]{0:T(128)S(1)} %add_add_fusion.3.half_ref, bf16[2,256,1024]{2,1,0:T(8,128)(2,1)} %get-tuple-element.25.first_ref, bf16[2,256,1024]{2,1,0:T(8,128)(2,1)} %collective-permute-done.7.second_ref, ...), custom_call_target="tpu_custom_call" | custom-call | tf_op jit(solution)/shard_map/gram/pallas_call | solution.py:93
  57.9 2.5 %gram.8 = f32[4,256,512]{2,1,0:T(8,128)S(1)} custom-call(s32[4]{0:T(128)S(1)} %get-tuple-element.57.which_ref, s32[4]{0:T(128)S(1)} %get-tuple-element.58.group_ref, s32[4]{0:T(128)S(1)} %add_add_fusion.6.half_ref, bf16[2,256,1024]{2,1,0:T(8,128)(2,1)S(1)} %get-tuple-element.27.first_ref, bf16[2,256,1024]{2,1,0:T(8,128)(2,1)S(1)} %collective-permute-done.9.second_ref, ...), custom_call_target="tpu_custom_call" | custom-call | tf_op jit(solution)/shard_map/gram/pallas_call | solution.py:93
  62.6 6.8 %collective-permute-done.8 = f16[2,256,512]{2,1,0:T(8,128)(2,1)S(1)} collective-permute-done((f16[2,256,512]{2,1,0:T(8,128)(2,1)S(1)}, f16[2,256,512]{2,1,0:T(8,128)(2,1)S(1)}, u32[]{:S(2)}, u32[]{:S(2)}) %collective-permute-start.8) | collective-permute-done | bytes 524320 | tf_op jit(solution)/shard_map/ppermute | solution.py:221
  69.6 2.5 %gram.6 = f32[4,256,512]{2,1,0:T(8,128)S(1)} custom-call(s32[4]{0:T(128)S(1)} %get-tuple-element.55.which_ref, s32[4]{0:T(128)S(1)} %get-tuple-element.56.group_ref, s32[4]{0:T(128)S(1)} %add_add_fusion.2.half_ref, bf16[2,256,1024]{2,1,0:T(8,128)(2,1)S(1)} %multiply_convert_fusion.2.first_ref, bf16[2,256,1024]{2,1,0:T(8,128)(2,1)S(1)} %collective-permute-done.5.second_ref, ...), custom_call_target="tpu_custom_call" | custom-call | tf_op jit(solution)/shard_map/gram/pallas_call | solution.py:93
  77.8 4.7 %collective-permute-start.20 = (f16[1,512,512]{2,1,0:T(8,128)(2,1)S(1)}, f16[1,512,512]{2,1,0:T(8,128)(2,1)S(1)}, u32[]{:S(2)}, u32[]{:S(2)}) collective-permute-start(f16[1,512,512]{2,1,0:T(8,128)(2,1)S(1)} %fusion), channel_id=1, source_target_pairs={{2,18},{6,22},{11,27},{15,31},{16,0},{20,4},{25,9},{29,13}} | collective-permute-start | bytes 1572872 | tf_op jit(solution)/shard_map/ppermute | solution.py:337
  82.5 3.7 %collective-permute-done.10 = f16[2,256,512]{2,1,0:T(8,128)(2,1)S(1)} collective-permute-done((f16[2,256,512]{2,1,0:T(8,128)(2,1)S(1)}, f16[2,256,512]{2,1,0:T(8,128)(2,1)S(1)}, u32[]{:S(2)}, u32[]{:S(2)}) %collective-permute-start.10) | collective-permute-done | bytes 524320 | tf_op jit(solution)/shard_map/ppermute | solution.py:221
  87.3 2.5 %gram.9 = f32[4,256,512]{2,1,0:T(8,128)S(1)} custom-call(s32[4]{0:T(128)S(1)} %get-tuple-element.57.which_ref, s32[4]{0:T(128)S(1)} %get-tuple-element.58.group_ref, s32[4]{0:T(128)S(1)} %add_add_fusion.7.half_ref, bf16[2,256,1024]{2,1,0:T(8,128)(2,1)S(1)} %multiply_convert_fusion.first_ref, bf16[2,256,1024]{2,1,0:T(8,128)(2,1)S(1)} %collective-permute-done.18.second_ref, ...), custom_call_target="tpu_custom_call" | custom-call | tf_op jit(solution)/shard_map/gram/pallas_call | solution.py:93
  91.0 3.0 %collective-permute-done.15 = f16[1,256,512]{2,1,0:T(8,128)(2,1)S(1)} collective-permute-done((f16[1,256,512]{2,1,0:T(8,128)(2,1)S(1)}, f16[1,256,512]{2,1,0:T(8,128)(2,1)S(1)}, u32[]{:S(2)}, u32[]{:S(2)}) %collective-permute-start.15) | collective-permute-done | bytes 262176 | tf_op jit(solution)/shard_map/ppermute | solution.py:221
  95.2 4.8 %collective-permute-start.16 = (f16[256,512]{1,0:T(8,128)(2,1)S(1)}, f16[256,512]{1,0:T(8,128)(2,1)S(1)}, u32[]{:S(2)}, u32[]{:S(2)}) collective-permute-start(f16[256,512]{1,0:T(8,128)(2,1)S(1)} %fusion.2), channel_id=1, source_target_pairs={{0,16},{4,20},{8,24},{12,28},{16,0},{20,4},{24,8},{28,12},{1,17},{... | collective-permute-start | bytes 786440 | tf_op jit(solution)/shard_map/ppermute | solution.py:221
  100.0 2.5 %collective-permute-start.22 = (f16[1,256,512]{2,1,0:T(8,128)(2,1)S(1)}, f16[1,256,512]{2,1,0:T(8,128)(2,1)}, u32[]{:S(2)}, u32[]{:S(2)}) collective-permute-start(f16[1,256,512]{2,1,0:T(8,128)(2,1)S(1)} %slice_convert_fusion.5), channel_id=1, source_target_pairs={{0,8},{4,12},{8,0},{12,4},{16,24},{20,28},{24,16},{28,20},{1,9},{5... | collective-permute-start | bytes 786440 | tf_op jit(solution)/shard_map/ppermute | solution.py:221
  102.5 3.7 %collective-permute-done.21 = f16[2,256,512]{2,1,0:T(8,128)(2,1)S(1)} collective-permute-done((f16[2,256,512]{2,1,0:T(8,128)(2,1)S(1)}, f16[2,256,512]{2,1,0:T(8,128)(2,1)S(1)}, u32[]{:S(2)}, u32[]{:S(2)}) %collective-permute-start.21) | collective-permute-done | bytes 524320 | tf_op jit(solution)/shard_map/ppermute | solution.py:221
  112.6 5.0 %collective-permute-done.23 = f16[1,256,512]{2,1,0:T(8,128)(2,1)} collective-permute-done((f16[1,256,512]{2,1,0:T(8,128)(2,1)}, f16[1,256,512]{2,1,0:T(8,128)(2,1)}, u32[]{:S(2)}, u32[]{:S(2)}) %collective-permute-start.23) | collective-permute-done | bytes 262176 | tf_op jit(solution)/shard_map/ppermute | solution.py:221
  118.9 3.4 %collective-permute-start.24 = (f16[256,512]{1,0:T(8,128)(2,1)S(1)}, f16[256,512]{1,0:T(8,128)(2,1)S(1)}, u32[]{:S(2)}, u32[]{:S(2)}) collective-permute-start(f16[256,512]{1,0:T(8,128)(2,1)S(1)} %fusion.3), channel_id=1, source_target_pairs={{0,16},{4,20},{8,24},{12,28},{16,0},{20,4},{24,8},{28,12},{1,17},{... | collective-permute-start | bytes 786440 | tf_op jit(solution)/shard_map/ppermute | solution.py:221
  123.6 4.6 %collective-permute-start.25 = (f16[256,512]{1,0:T(8,128)(2,1)S(1)}, f16[256,512]{1,0:T(8,128)(2,1)S(1)}, u32[]{:S(2)}, u32[]{:S(2)}) collective-permute-start(f16[256,512]{1,0:T(8,128)(2,1)S(1)} %get-tuple-element.41), channel_id=1, source_target_pairs={{1,8},{2,16},{3,24},{5,12},{6,20},{7,28},{8,5},{10,17},{11,25},{12... | collective-permute-start | bytes 786440 | tf_op jit(solution)/shard_map/ppermute | solution.py:337
  128.2 3.5 %collective-permute-done.24 = f16[256,512]{1,0:T(8,128)(2,1)S(1)} collective-permute-done((f16[256,512]{1,0:T(8,128)(2,1)S(1)}, f16[256,512]{1,0:T(8,128)(2,1)S(1)}, u32[]{:S(2)}, u32[]{:S(2)}) %collective-permute-start.24) | collective-permute-done | bytes 262176 | tf_op jit(solution)/shard_map/ppermute | solution.py:221
  133.0 9.9 %collective-permute-start.26 = (f16[256,512]{1,0:T(8,128)(2,1)S(1)}, f16[256,512]{1,0:T(8,128)(2,1)S(1)}, u32[]{:S(2)}, u32[]{:S(2)}) collective-permute-start(f16[256,512]{1,0:T(8,128)(2,1)S(1)} %get-tuple-element.43), channel_id=1, source_target_pairs={{1,8},{2,16},{3,24},{5,12},{6,20},{7,28},{8,5},{10,17},{11,25},{12... | collective-permute-start | bytes 786440 | tf_op jit(solution)/shard_map/ppermute | solution.py:337
  144.4 7.2 %collective-permute-done.25 = f16[256,512]{1,0:T(8,128)(2,1)S(1)} collective-permute-done((f16[256,512]{1,0:T(8,128)(2,1)S(1)}, f16[256,512]{1,0:T(8,128)(2,1)S(1)}, u32[]{:S(2)}, u32[]{:S(2)}) %collective-permute-start.25) | collective-permute-done | bytes 262176 | tf_op jit(solution)/shard_map/ppermute | solution.py:337
  151.5 5.0 %collective-permute-done.26 = f16[256,512]{1,0:T(8,128)(2,1)S(1)} collective-permute-done((f16[256,512]{1,0:T(8,128)(2,1)S(1)}, f16[256,512]{1,0:T(8,128)(2,1)S(1)}, u32[]{:S(2)}, u32[]{:S(2)}) %collective-permute-start.26) | collective-permute-done | bytes 262176 | tf_op jit(solution)/shard_map/ppermute | solution.py:337
  156.7 2.4 %assemble.1 = f32[512,1024]{1,0:T(8,128)} custom-call(s32[3]{0:T(128)S(1)} %pad_add_fusion.flags_ref, f32[512,512]{1,0:T(8,128)S(1)} %pad_maximum_fusion.direct_ref, f32[1,512,512]{2,1,0:T(8,128)S(1)} %maximum_convert_fusion.mirror_ref, f32[512,512]{1,0:T(8,128)S(1)} %add_bitcast_fusion.diagonal_ref, f32[1,128]{1,0:T(1,128)S(1)} %multiply_divide_fusion.factor_ref), custom_call_target="tpu_custom_call" | custom-call | tf_op jit(solution)/shard_map/assemble/pallas_call | solution.py:144
  (129 shorter events, 52.1 us)
Async XLA Ops:
  19.9 28.0 %collective-permute-start.3 = (bf16[2,256,1024]{2,1,0:T(8,128)(2,1)}, bf16[2,256,1024]{2,1,0:T(8,128)(2,1)}, u32[]{:S(2)}, u32[]{:S(2)}) collective-permute-start(bf16[2,256,1024]{2,1,0:T(8,128)(2,1)} %get-tuple-element.45), channel_id=1, source_target_pairs={{0,2},{1,3},{2,0},{3,1},{4,6},{5,7},{6,4},{7,5},{8,10},{9,11},{10,... | collective-permute-start | bytes 3145736 | tf_op jit(solution)/shard_map/ppermute | solution.py:221
  24.8 4.8 %collective-permute-start.2 = (f32[8,1024]{1,0:T(8,128)S(1)}, f32[8,1024]{1,0:T(8,128)S(1)}, u32[]{:S(2)}, u32[]{:S(2)}) collective-permute-start(f32[8,1024]{1,0:T(8,128)S(1)} %add.67), channel_id=1, source_target_pairs={{0,16},{4,20},{8,24},{12,28},{16,0},{20,4},{24,8},{28,12},{1,17},{... | collective-permute-start | bytes 98312 | tf_op jit(solution)/shard_map/ppermute | solution.py:221
  39.9 6.3 %collective-permute-start.14 = (f32[8,1024]{1,0:T(8,128)S(1)}, f32[8,1024]{1,0:T(8,128)S(1)}, u32[]{:S(2)}, u32[]{:S(2)}) collective-permute-start(f32[8,1024]{1,0:T(8,128)S(1)} %copy-done.6), channel_id=1, source_target_pairs={{0,1},{1,0},{2,3},{3,2},{4,5},{5,4},{6,7},{7,6},{8,9},{9,8},{10,11... | collective-permute-start | bytes 98312 | tf_op jit(solution)/shard_map/ppermute | solution.py:221
  39.9 5.6 %collective-permute-start.4 = (f32[8,1024]{1,0:T(8,128)S(1)}, f32[8,1024]{1,0:T(8,128)S(1)}, u32[]{:S(2)}, u32[]{:S(2)}) collective-permute-start(f32[8,1024]{1,0:T(8,128)S(1)} %copy-done.6), channel_id=1, source_target_pairs={{0,2},{1,3},{2,0},{3,1},{4,6},{5,7},{6,4},{7,5},{8,10},{9,11},{10,... | collective-permute-start | bytes 98312 | tf_op jit(solution)/shard_map/ppermute | solution.py:221
  41.3 15.3 %collective-permute-start.6 = (f16[1,512,512]{2,1,0:T(8,128)(2,1)}, f16[1,512,512]{2,1,0:T(8,128)(2,1)}, u32[]{:S(2)}, u32[]{:S(2)}) collective-permute-start(f16[1,512,512]{2,1,0:T(8,128)(2,1)} %slice_convert_fusion.4), channel_id=1, source_target_pairs={{0,4},{4,0},{8,12},{12,8},{16,20},{20,16},{24,28},{28,24},{1,5},{5... | collective-permute-start | bytes 1572872 | tf_op jit(solution)/shard_map/ppermute | solution.py:221
  43.0 7.3 %collective-permute-start.7 = (bf16[2,256,1024]{2,1,0:T(8,128)(2,1)}, bf16[2,256,1024]{2,1,0:T(8,128)(2,1)}, u32[]{:S(2)}, u32[]{:S(2)}) collective-permute-start(bf16[2,256,1024]{2,1,0:T(8,128)(2,1)} %get-tuple-element.25.first_ref), channel_id=1, source_target_pairs={{0,1},{1,0},{2,3},{3,2},{4,5},{5,4},{6,7},{7,6},{8,9},{9,8},{10,11... | collective-permute-start | bytes 3145736 | tf_op jit(solution)/shard_map/ppermute | solution.py:221
  46.1 11.8 %collective-permute-start.9 = (bf16[2,256,1024]{2,1,0:T(8,128)(2,1)S(1)}, bf16[2,256,1024]{2,1,0:T(8,128)(2,1)S(1)}, u32[]{:S(2)}, u32[]{:S(2)}) collective-permute-start(bf16[2,256,1024]{2,1,0:T(8,128)(2,1)S(1)} %get-tuple-element.27.first_ref), channel_id=1, source_target_pairs={{0,1},{1,0},{2,3},{3,2},{4,5},{5,4},{6,7},{7,6},{8,9},{9,8},{10,11... | collective-permute-start | bytes 3145736 | tf_op jit(solution)/shard_map/ppermute | solution.py:221
  46.7 25.5 %collective-permute-start.17 = (bf16[2,256,1024]{2,1,0:T(8,128)(2,1)}, bf16[2,256,1024]{2,1,0:T(8,128)(2,1)S(1)}, u32[]{:S(2)}, u32[]{:S(2)}) collective-permute-start(bf16[2,256,1024]{2,1,0:T(8,128)(2,1)} %get-tuple-element.33), channel_id=1, source_target_pairs={{0,2},{1,3},{2,0},{3,1},{4,6},{5,7},{6,4},{7,5},{8,10},{9,11},{10,... | collective-permute-start | bytes 3145736 | tf_op jit(solution)/shard_map/ppermute | solution.py:221
  50.2 19.4 %collective-permute-start.5 = (bf16[2,256,1024]{2,1,0:T(8,128)(2,1)S(1)}, bf16[2,256,1024]{2,1,0:T(8,128)(2,1)S(1)}, u32[]{:S(2)}, u32[]{:S(2)}) collective-permute-start(bf16[2,256,1024]{2,1,0:T(8,128)(2,1)S(1)} %multiply_convert_fusion.2.first_ref), channel_id=1, source_target_pairs={{0,1},{1,0},{2,3},{3,2},{4,5},{5,4},{6,7},{7,6},{8,9},{9,8},{10,11... | collective-permute-start | bytes 3145736 | tf_op jit(solution)/shard_map/ppermute | solution.py:221
  55.0 14.4 %collective-permute-start.8 = (f16[2,256,512]{2,1,0:T(8,128)(2,1)S(1)}, f16[2,256,512]{2,1,0:T(8,128)(2,1)S(1)}, u32[]{:S(2)}, u32[]{:S(2)}) collective-permute-start(f16[2,256,512]{2,1,0:T(8,128)(2,1)S(1)} %slice_convert_fusion.2), channel_id=1, source_target_pairs={{0,8},{4,12},{8,0},{12,4},{16,24},{20,28},{24,16},{28,20},{1,9},{5... | collective-permute-start | bytes 1572872 | tf_op jit(solution)/shard_map/ppermute | solution.py:221
  60.6 26.0 %collective-permute-start.11 = (f16[2,256,512]{2,1,0:T(8,128)(2,1)S(1)}, f16[2,256,512]{2,1,0:T(8,128)(2,1)S(1)}, u32[]{:S(2)}, u32[]{:S(2)}) collective-permute-start(f16[2,256,512]{2,1,0:T(8,128)(2,1)S(1)} %slice_convert_fusion.1), channel_id=1, source_target_pairs={{0,4},{4,0},{8,12},{12,8},{16,20},{20,16},{24,28},{28,24},{1,5},{5... | collective-permute-start | bytes 1572872 | tf_op jit(solution)/shard_map/ppermute | solution.py:221
  61.4 14.1 %collective-permute-start.19 = (f16[1,512,512]{2,1,0:T(8,128)(2,1)S(1)}, f16[1,512,512]{2,1,0:T(8,128)(2,1)S(1)}, u32[]{:S(2)}, u32[]{:S(2)}) collective-permute-start(f16[1,512,512]{2,1,0:T(8,128)(2,1)S(1)} %fusion.1), channel_id=1, source_target_pairs={{1,9},{3,11},{5,13},{7,15},{8,0},{10,2},{12,4},{14,6},{17,25},{19,... | collective-permute-start | bytes 1572872 | tf_op jit(solution)/shard_map/ppermute | solution.py:337
  72.2 14.0 %collective-permute-start.10 = (f16[2,256,512]{2,1,0:T(8,128)(2,1)S(1)}, f16[2,256,512]{2,1,0:T(8,128)(2,1)S(1)}, u32[]{:S(2)}, u32[]{:S(2)}) collective-permute-start(f16[2,256,512]{2,1,0:T(8,128)(2,1)S(1)} %slice_convert_fusion.3), channel_id=1, source_target_pairs={{0,8},{4,12},{8,0},{12,4},{16,24},{20,28},{24,16},{28,20},{1,9},{5... | collective-permute-start | bytes 1572872 | tf_op jit(solution)/shard_map/ppermute | solution.py:221
  75.3 12.0 %collective-permute-start.18 = (bf16[2,256,1024]{2,1,0:T(8,128)(2,1)S(1)}, bf16[2,256,1024]{2,1,0:T(8,128)(2,1)S(1)}, u32[]{:S(2)}, u32[]{:S(2)}) collective-permute-start(bf16[2,256,1024]{2,1,0:T(8,128)(2,1)S(1)} %multiply_convert_fusion.first_ref), channel_id=1, source_target_pairs={{0,1},{1,0},{2,3},{3,2},{4,5},{5,4},{6,7},{7,6},{8,9},{9,8},{10,11... | collective-permute-start | bytes 3145736 | tf_op jit(solution)/shard_map/ppermute | solution.py:221
  77.0 9.5 %collective-permute-start.12 = (f16[1,256,512]{2,1,0:T(8,128)(2,1)S(1)}, f16[1,256,512]{2,1,0:T(8,128)(2,1)S(1)}, u32[]{:S(2)}, u32[]{:S(2)}) collective-permute-start(f16[1,256,512]{2,1,0:T(8,128)(2,1)S(1)} %slice_convert_fusion.7), channel_id=1, source_target_pairs={{0,4},{4,0},{8,12},{12,8},{16,20},{20,16},{24,28},{28,24},{1,5},{5... | collective-permute-start | bytes 786440 | tf_op jit(solution)/shard_map/ppermute | solution.py:221
  77.8 13.2 %collective-permute-start.20 = (f16[1,512,512]{2,1,0:T(8,128)(2,1)S(1)}, f16[1,512,512]{2,1,0:T(8,128)(2,1)S(1)}, u32[]{:S(2)}, u32[]{:S(2)}) collective-permute-start(f16[1,512,512]{2,1,0:T(8,128)(2,1)S(1)} %fusion), channel_id=1, source_target_pairs={{2,18},{6,22},{11,27},{15,31},{16,0},{20,4},{25,9},{29,13}} | collective-permute-start | bytes 1572872 | tf_op jit(solution)/shard_map/ppermute | solution.py:337
  86.5 7.5 %collective-permute-start.15 = (f16[1,256,512]{2,1,0:T(8,128)(2,1)S(1)}, f16[1,256,512]{2,1,0:T(8,128)(2,1)S(1)}, u32[]{:S(2)}, u32[]{:S(2)}) collective-permute-start(f16[1,256,512]{2,1,0:T(8,128)(2,1)S(1)} %slice_convert_fusion.8), channel_id=1, source_target_pairs={{0,4},{4,0},{8,12},{12,8},{16,20},{20,16},{24,28},{28,24},{1,5},{5... | collective-permute-start | bytes 786440 | tf_op jit(solution)/shard_map/ppermute | solution.py:221
  94.1 12.2 %collective-permute-start.21 = (f16[2,256,512]{2,1,0:T(8,128)(2,1)S(1)}, f16[2,256,512]{2,1,0:T(8,128)(2,1)S(1)}, u32[]{:S(2)}, u32[]{:S(2)}) collective-permute-start(f16[2,256,512]{2,1,0:T(8,128)(2,1)S(1)} %slice_convert_fusion), channel_id=1, source_target_pairs={{0,4},{4,0},{8,12},{12,8},{16,20},{20,16},{24,28},{28,24},{1,5},{5... | collective-permute-start | bytes 1572872 | tf_op jit(solution)/shard_map/ppermute | solution.py:221
  95.2 14.9 %collective-permute-start.16 = (f16[256,512]{1,0:T(8,128)(2,1)S(1)}, f16[256,512]{1,0:T(8,128)(2,1)S(1)}, u32[]{:S(2)}, u32[]{:S(2)}) collective-permute-start(f16[256,512]{1,0:T(8,128)(2,1)S(1)} %fusion.2), channel_id=1, source_target_pairs={{0,16},{4,20},{8,24},{12,28},{16,0},{20,4},{24,8},{28,12},{1,17},{... | collective-permute-start | bytes 786440 | tf_op jit(solution)/shard_map/ppermute | solution.py:221
  100.0 10.3 %collective-permute-start.22 = (f16[1,256,512]{2,1,0:T(8,128)(2,1)S(1)}, f16[1,256,512]{2,1,0:T(8,128)(2,1)}, u32[]{:S(2)}, u32[]{:S(2)}) collective-permute-start(f16[1,256,512]{2,1,0:T(8,128)(2,1)S(1)} %slice_convert_fusion.5), channel_id=1, source_target_pairs={{0,8},{4,12},{8,0},{12,4},{16,24},{20,28},{24,16},{28,20},{1,9},{5... | collective-permute-start | bytes 786440 | tf_op jit(solution)/shard_map/ppermute | solution.py:221
  110.9 6.7 %collective-permute-start.23 = (f16[1,256,512]{2,1,0:T(8,128)(2,1)}, f16[1,256,512]{2,1,0:T(8,128)(2,1)}, u32[]{:S(2)}, u32[]{:S(2)}) collective-permute-start(f16[1,256,512]{2,1,0:T(8,128)(2,1)} %slice_convert_fusion.6), channel_id=1, source_target_pairs={{0,8},{4,12},{8,0},{12,4},{16,24},{20,28},{24,16},{28,20},{1,9},{5... | collective-permute-start | bytes 786440 | tf_op jit(solution)/shard_map/ppermute | solution.py:221
  118.9 12.8 %collective-permute-start.24 = (f16[256,512]{1,0:T(8,128)(2,1)S(1)}, f16[256,512]{1,0:T(8,128)(2,1)S(1)}, u32[]{:S(2)}, u32[]{:S(2)}) collective-permute-start(f16[256,512]{1,0:T(8,128)(2,1)S(1)} %fusion.3), channel_id=1, source_target_pairs={{0,16},{4,20},{8,24},{12,28},{16,0},{20,4},{24,8},{28,12},{1,17},{... | collective-permute-start | bytes 786440 | tf_op jit(solution)/shard_map/ppermute | solution.py:221
  123.6 28.0 %collective-permute-start.25 = (f16[256,512]{1,0:T(8,128)(2,1)S(1)}, f16[256,512]{1,0:T(8,128)(2,1)S(1)}, u32[]{:S(2)}, u32[]{:S(2)}) collective-permute-start(f16[256,512]{1,0:T(8,128)(2,1)S(1)} %get-tuple-element.41), channel_id=1, source_target_pairs={{1,8},{2,16},{3,24},{5,12},{6,20},{7,28},{8,5},{10,17},{11,25},{12... | collective-permute-start | bytes 786440 | tf_op jit(solution)/shard_map/ppermute | solution.py:337
  133.0 23.6 %collective-permute-start.26 = (f16[256,512]{1,0:T(8,128)(2,1)S(1)}, f16[256,512]{1,0:T(8,128)(2,1)S(1)}, u32[]{:S(2)}, u32[]{:S(2)}) collective-permute-start(f16[256,512]{1,0:T(8,128)(2,1)S(1)} %get-tuple-element.43), channel_id=1, source_target_pairs={{1,8},{2,16},{3,24},{5,12},{6,20},{7,28},{8,5},{10,17},{11,25},{12... | collective-permute-start | bytes 786440 | tf_op jit(solution)/shard_map/ppermute | solution.py:337
  (23 other events, 184.3 us)
